TPU v7x, 32 devices: a whole 2x2x4 slice. The times are simulated.
32 devices in a mesh: gx: 4 (over y, x), gy: 4 (over z), gz: 2 (over core).
Axes of the slice: x: 2, y: 2, z: 4, core: 2. Of those that a mesh axis runs over, the one named last changes fastest.
Arguments:
- orbitals: float32 [4, 256, 256, 256], P(None, 'gx', 'gy', 'gz'), may hold values from -6 to 6
- potential: float32 [256, 256, 256], P('gx', 'gy', 'gz'), may hold values from -2 to 0
Outputs:
- basis: float32 [4, 256, 256, 256], P(None, 'gx', 'gy', 'gz')
- factor: float32 [4, 4], replicated
All inputs are finite; a program needn't handle non-finite values.
Results may differ from a plain program's by a relative error of at most 0.00011.
Values sent between devices are 32-bit elements; how exact they have to be, the bound alone decides.
No kernel may reach another device: no remote copies, remote signals or barrier semaphores. Data moves between devices by JAX's collectives and lax.ppermute only.
A program may use at most 256 MiB of HBM per device.

v0:
```python
import jax
import jax.numpy as jnp
from jax import lax
from jax.sharding import PartitionSpec as P


def padded_2(block, sides, width):
    for axis, dim in sides:
        count = lax.axis_size(axis)
        forward = [(i, i + 1) for i in range(count - 1)]
        backward = [(target, source) for source, target in forward]
        low = lax.ppermute(
            lax.slice_in_dim(block, block.shape[dim] - width, None, axis=dim), axis, forward
        )
        high = lax.ppermute(lax.slice_in_dim(block, 0, width, axis=dim), axis, backward)
        block = jnp.concatenate([low, block, high], axis=dim)
    return block


def shifted(padded, axis, offset):
    pieces = []
    for which in range(3):
        length = padded.shape[which - 3]
        if which - 3 == axis:
            pieces.append(slice(2 + offset, length - 2 + offset))
        else:
            pieces.append(slice(2, length - 2))
    return padded[..., pieces[0], pieces[1], pieces[2]]


def kinetic(padded):
    total = -7.5 * shifted(padded, -1, 0)
    for axis in (-3, -2, -1):
        for offset, weight in ((1, 4.0 / 3.0), (2, -1.0 / 12.0)):
            total = total + weight * (
                shifted(padded, axis, offset) + shifted(padded, axis, -offset)
            )
    return -0.5 * total


def apply_hamiltonian(field, potential):
    padded = padded_2(field, (("gx", 1), ("gy", 2), ("gz", 3)), 2)
    return kinetic(padded) + potential[None] * field


def upper_factor(gram):
    order = gram.shape[0]
    zero = jnp.zeros((), jnp.float32)
    entries = [[zero for column in range(order)] for line in range(order)]
    for line in range(order):
        for column in range(line, order):
            value = gram[line, column]
            for inner in range(line):
                value = value - entries[inner][line] * entries[inner][column]
            if column == line:
                entries[line][line] = jnp.sqrt(value)
            else:
                entries[line][column] = value / entries[line][line]
    return jnp.stack([jnp.stack(entries[line]) for line in range(order)])


def invert_upper(factor):
    order = factor.shape[0]
    zero = jnp.zeros((), jnp.float32)
    entries = [[zero for column in range(order)] for line in range(order)]
    for column in range(order):
        entries[column][column] = 1.0 / factor[column, column]
        for line in range(column - 1, -1, -1):
            value = zero
            for inner in range(line + 1, column + 1):
                value = value + factor[line, inner] * entries[inner][column]
            entries[line][column] = -value / factor[line, line]
    return jnp.stack([jnp.stack(entries[line]) for line in range(order)])


def body(orbitals, potential):
    centre = 4.5
    half_width = 3.5
    level_one = (apply_hamiltonian(orbitals, potential) - centre * orbitals) / half_width
    level_two = (
        2.0 * (apply_hamiltonian(level_one, potential) - centre * level_one) / half_width - orbitals
    )
    filtered = (
        2.0 * (apply_hamiltonian(level_two, potential) - centre * level_two) / half_width
        - level_one
    )
    total_cells = (
        orbitals.shape[1]
        * lax.axis_size("gx")
        * (orbitals.shape[2] * lax.axis_size("gy"))
        * (orbitals.shape[3] * lax.axis_size("gz"))
    )
    local_gram = (
        jnp.einsum("iabc,jabc->ij", filtered, filtered, precision=lax.Precision.HIGHEST)
        / total_cells
    )
    gram = lax.psum(local_gram, ("gx", "gy", "gz"))
    factor = upper_factor(gram)
    inverse = invert_upper(factor)
    basis = jnp.einsum("ij,iabc->jabc", inverse, filtered, precision=lax.Precision.HIGHEST)
    return (basis, factor)


def solution(mesh):
    return jax.shard_map(
        body,
        mesh=mesh,
        in_specs=(P(None, "gx", "gy", "gz"), P("gx", "gy", "gz")),
        out_specs=(P(None, "gx", "gy", "gz"), P()),
        check_vma=False,
    )
```

profile of v0, /device:TPU:0, one launch (start us, length us, event | category | flops | bytes accessed | tf_op | source)
XLA Modules:
  0.0 557.0 jit_solution(14031895794163608625)
XLA Ops:
  3.0 5.5 collective-permute-start.1
  8.5 14.4 %constant_dynamic-update-slice_fusion.1 = (f32[4,66,64,128]{3,1,2,0:T(8,128)}, f32[4,64,64,128]{3,1,2,0:T(8,128)}) fusion(f32[4,64,64,128]{3,2,1,0:T(8,128)} %param.2), kind=kLoop, calls=%fused_computation.144 | loop fusion | bytes 25165824
  27.4 4.6 collective-permute-start.3
  40.5 7.9 %fusion.93 = (f32[4,68,68,2]{3,1,2,0:T(8,128)}, f32[4,68,68,2]{3,1,2,0:T(8,128)}) fusion(f32[4,68,68,128]{3,1,2,0:T(8,128)S(1)} %pad_maximum_fusion), kind=kLoop, calls=%fused_computation.175 | loop fusion | bytes 591872 | tf_op jit(solution)/shard_map/slice | solution.py:15
  48.4 6.3 %copy.51 = f32[4,68,68,2]{2,1,3,0:T(8,128)S(1)} copy(f32[4,68,68,2]{3,1,2,0:T(8,128)} %get-tuple-element.14) | data formatting | bytes 295936 | tf_op jit(solution)/shard_map/slice | solution.py:15
  56.0 6.3 %copy.53 = f32[4,68,68,2]{2,1,3,0:T(8,128)S(1)} copy(f32[4,68,68,2]{3,1,2,0:T(8,128)} %get-tuple-element.15) | data formatting | bytes 295936 | tf_op jit(solution)/shard_map/slice | solution.py:13
  65.6 14.6 %pad_maximum_fusion.3 = (f32[4,68,66,128]{3,1,2,0:T(8,128)}, f32[4,68,66,128]{3,1,2,0:T(8,128)}) fusion(f32[4,68,2,128]{3,1,2,0:T(8,128)S(1)} %collective-permute-done.2, f32[4,2,64,128]{3,1,2,0:T(2,128)S(1)} %get-tuple-element.37, f32[4,64,64,128]{3,1,2,0:T(8,128)} %get-tuple-element.33, f32[4,2,64,128]{3,1,2,0:T(2,128)S(1)} %copy.46, ...), kind=kLoop, calls=%fused_computation.3 | loop fusion | flops 13787136 | bytes 27852800 | tf_op jit(solution)/shard_map/concatenate | solution.py:16
  80.2 5.7 %copy.52 = f32[4,68,68,2]{3,1,2,0:T(8,128)} copy(f32[4,68,68,2]{2,1,3,0:T(8,128)S(1)} %collective-permute-done.4) | data formatting | bytes 295936 | tf_op jit(solution)/shard_map/ppermute | solution.py:15
  85.9 5.8 %copy.54 = f32[4,68,68,2]{3,1,2,0:T(8,128)} copy(f32[4,68,68,2]{2,1,3,0:T(8,128)S(1)} %collective-permute-done.5) | data formatting | bytes 295936 | tf_op jit(solution)/shard_map/ppermute | solution.py:12
  91.7 54.9 %broadcast_multiply_fusion = (f32[4,64,64,128]{3,1,2,0:T(8,128)S(1)}, f32[4,64,64,128]{3,1,2,0:T(8,128)}) fusion(f32[4,64,64,128]{3,1,2,0:T(8,128)} %get-tuple-element.33, f32[64,64,128]{2,0,1:T(8,128)} %copy.55, f32[4,68,2,128]{3,1,2,0:T(8,128)S(1)} %collective-permute-done.2, f32[4,2,64,128]{3,1,2,0:T(2,128)S(1)} %get-tuple-element.37, ...), kind=kLoop, calls=%fused_computation.130 | loop fusion | flops 98566144 | bytes 78971904 | tf_op jit(solution)/shard_map/div | solution.py:79
  148.4 5.2 collective-permute-start.7
  153.7 5.2 collective-permute-done.6
  160.7 5.0 collective-permute-start.9
  173.0 7.9 %fusion.92 = (f32[4,68,68,2]{3,1,2,0:T(8,128)}, f32[4,68,68,2]{3,1,2,0:T(8,128)}) fusion(f32[4,68,68,128]{3,1,2,0:T(8,128)S(1)} %pad_maximum_fusion.1), kind=kLoop, calls=%fused_computation.174 | loop fusion | bytes 591872 | tf_op jit(solution)/shard_map/slice | solution.py:15
  180.9 6.3 %copy.64 = f32[4,68,68,2]{2,1,3,0:T(8,128)S(1)} copy(f32[4,68,68,2]{3,1,2,0:T(8,128)} %get-tuple-element.12) | data formatting | bytes 295936 | tf_op jit(solution)/shard_map/slice | solution.py:15
  188.9 6.3 %copy.66 = f32[4,68,68,2]{2,1,3,0:T(8,128)S(1)} copy(f32[4,68,68,2]{3,1,2,0:T(8,128)} %get-tuple-element.13) | data formatting | bytes 295936 | tf_op jit(solution)/shard_map/slice | solution.py:13
  198.3 14.6 %pad_maximum_fusion.4 = (f32[4,68,66,128]{3,1,2,0:T(8,128)}, f32[4,68,66,128]{3,1,2,0:T(8,128)}) fusion(f32[4,68,2,128]{3,1,2,0:T(8,128)S(1)} %collective-permute-done.8, f32[4,2,64,128]{3,1,2,0:T(2,128)S(1)} %copy.59, f32[4,64,64,128]{3,1,2,0:T(8,128)} %copy-done.1, f32[4,2,64,128]{3,1,2,0:T(2,128)S(1)} %copy.61, f32[4,68,2,128]{3,1,2,0:T(8,128)S(1)} %collective-permute-done.9), kind=kLoop, calls=%fused_computation.5 | loop fusion | flops 13787136 | bytes 27852800 | tf_op jit(solution)/shard_map/concatenate | solution.py:16
  212.9 5.7 %copy.65 = f32[4,68,68,2]{3,1,2,0:T(8,128)} copy(f32[4,68,68,2]{2,1,3,0:T(8,128)S(1)} %collective-permute-done.10) | data formatting | bytes 295936 | tf_op jit(solution)/shard_map/ppermute | solution.py:15
  218.6 5.8 %copy.67 = f32[4,68,68,2]{3,1,2,0:T(8,128)} copy(f32[4,68,68,2]{2,1,3,0:T(8,128)S(1)} %collective-permute-done.11) | data formatting | bytes 295936 | tf_op jit(solution)/shard_map/ppermute | solution.py:12
  224.5 56.2 %fusion.28 = f32[4,64,64,128]{3,1,2,0:T(8,128)S(1)} fusion(f32[4,2,64,128]{3,1,2,0:T(2,128)S(1)} %copy.61, f32[4,64,64,128]{3,1,2,0:T(8,128)} %copy-done.1, f32[4,2,64,128]{3,1,2,0:T(2,128)S(1)} %copy.59, f32[4,68,68,2]{3,1,2,0:T(8,128)} %copy.67, f32[4,68,2,128]{3,1,2,0:T(8,128)S(1)} %collective-permute-done.8, ...), kind=kLoop, calls=%fused_computation.47 | loop fusion | flops 104857600 | bytes 70583296 | tf_op jit(solution)/shard_map/sub | solution.py:81
  282.2 6.8 %collective-permute-start.13 = (f32[4,2,64,128]{3,2,1,0:T(8,128)S(1)}, f32[4,2,64,128]{3,2,1,0:T(8,128)S(1)}, u32[]{:S(2)}, u32[]{:S(2)}) collective-permute-start(f32[4,2,64,128]{3,2,1,0:T(8,128)S(1)} %copy.72), channel_id=1, source_target_pairs={{0,8},{8,16},{16,24},{1,9},{9,17},{17,25},{2,10},{10,18},{18,26},{... | collective-permute-start | bytes 786440 | tf_op jit(solution)/shard_map/ppermute | solution.py:12
  295.6 5.0 collective-permute-start.15
  308.3 7.9 %fusion.91 = (f32[4,68,68,2]{3,1,2,0:T(8,128)}, f32[4,68,68,2]{3,1,2,0:T(8,128)}) fusion(f32[4,68,68,128]{3,1,2,0:T(8,128)S(1)} %pad_maximum_fusion.2), kind=kLoop, calls=%fused_computation.173 | loop fusion | bytes 591872 | tf_op jit(solution)/shard_map/slice | solution.py:15
  316.2 6.3 %copy.76 = f32[4,68,68,2]{2,1,3,0:T(8,128)S(1)} copy(f32[4,68,68,2]{3,1,2,0:T(8,128)} %get-tuple-element.10) | data formatting | bytes 295936 | tf_op jit(solution)/shard_map/slice | solution.py:15
  323.9 6.3 %copy.78 = f32[4,68,68,2]{2,1,3,0:T(8,128)S(1)} copy(f32[4,68,68,2]{3,1,2,0:T(8,128)} %get-tuple-element.11) | data formatting | bytes 295936 | tf_op jit(solution)/shard_map/slice | solution.py:13
  333.4 14.6 %pad_maximum_fusion.5 = (f32[4,68,66,128]{3,1,2,0:T(8,128)}, f32[4,68,66,128]{3,1,2,0:T(8,128)}) fusion(f32[4,68,2,128]{3,1,2,0:T(8,128)S(1)} %collective-permute-done.14, f32[4,2,64,128]{3,1,2,0:T(2,128)S(1)} %copy.71, f32[4,64,64,128]{3,1,2,0:T(8,128)} %copy-done, f32[4,2,64,128]{3,1,2,0:T(2,128)S(1)} %copy.73, f32[4,68,2,128]{3,1,2,0:T(8,128)S(1)} %collective-permute-done.15), kind=kLoop, calls=%fused_computation.7 | loop fusion | flops 13787136 | bytes 27852800 | tf_op jit(solution)/shard_map/concatenate | solution.py:16
  348.0 5.7 %copy.77 = f32[4,68,68,2]{3,1,2,0:T(8,128)} copy(f32[4,68,68,2]{2,1,3,0:T(8,128)S(1)} %collective-permute-done.16) | data formatting | bytes 295936 | tf_op jit(solution)/shard_map/ppermute | solution.py:15
  353.7 5.8 %copy.79 = f32[4,68,68,2]{3,1,2,0:T(8,128)} copy(f32[4,68,68,2]{2,1,3,0:T(8,128)S(1)} %collective-permute-done.17) | data formatting | bytes 295936 | tf_op jit(solution)/shard_map/ppermute | solution.py:12
  359.6 56.6 %fusion.13 = f32[4,64,64,128]{3,1,2,0:T(8,128)S(1)} fusion(f32[4,2,64,128]{3,1,2,0:T(2,128)S(1)} %copy.73, f32[4,64,64,128]{3,1,2,0:T(8,128)} %copy-done, f32[4,2,64,128]{3,1,2,0:T(2,128)S(1)} %copy.71, f32[4,68,68,2]{3,1,2,0:T(8,128)} %copy.79, f32[4,68,2,128]{3,1,2,0:T(8,128)S(1)} %collective-permute-done.14, ...), kind=kLoop, calls=%fused_computation.32 | loop fusion | flops 106954752 | bytes 62194688 | tf_op jit(solution)/shard_map/sub | solution.py:84
  419.5 36.9 %fusion.70 = f32[4,4]{1,0:T(4,128)S(1)} fusion(f32[4,64,64,128]{3,1,2,0:T(8,128)S(1)} %fusion.13), kind=kOutput, calls=%fused_computation.132 | convolution fusion | flops 100663312 | bytes 8388672 | tf_op jit(solution)/shard_map/iabc,jabc->ij/dot_general | solution.py:94
  456.4 47.4 %psum.7 = f32[4,4]{1,0:T(4,128)S(1)} all-reduce(f32[4,4]{1,0:T(4,128)S(1)} %fusion.70), channel_id=1, replica_groups=mesh['gx'=4,'gy'=4,'gz'=2] {'gx','gy','gz'}, use_global_device_ids=true, to_apply=%region_0.0 | all-reduce | flops 16 | bytes 128 | tf_op jit(solution)/shard_map/psum | solution.py:97
  527.6 24.6 %fusion.63 = f32[4,64,64,128]{3,0,2,1:T(4,128)S(1)} fusion(f32[4,64,64,128]{3,1,2,0:T(8,128)} %copy-done.3, f32[1,4]{0,1:T(4,128)S(1)} %copy.85, f32[1,4]{0,1:T(4,128)S(1)} %copy.84, f32[1,4]{0,1:T(4,128)S(1)} %copy.83, f32[1,4]{0,1:T(4,128)S(1)} %copy.82), kind=kOutput, calls=%fused_computation.126 | convolution fusion | flops 100663344 | bytes 16777280 | tf_op jit(solution)/shard_map/ij,iabc->jabc/dot_general | solution.py:100
  (80 shorter events, 68.1 us)
Async XLA Ops:
  1.7 21.5 %collective-permute-start = (f32[4,2,64,128]{3,2,1,0:T(8,128)S(1)}, f32[4,2,64,128]{3,2,1,0:T(8,128)S(1)}, u32[]{:S(2)}, u32[]{:S(2)}) collective-permute-start(f32[4,2,64,128]{3,2,1,0:T(8,128)S(1)} %get-tuple-element.35), channel_id=1, source_target_pairs={{8,0},{16,8},{24,16},{9,1},{17,9},{25,17},{10,2},{18,10},{26,18},{... | collective-permute-start | bytes 786440 | tf_op jit(solution)/shard_map/ppermute | solution.py:15
  3.0 19.9 %collective-permute-start.1 = (f32[4,2,64,128]{3,2,1,0:T(8,128)S(1)}, f32[4,2,64,128]{3,2,1,0:T(8,128)S(1)}, u32[]{:S(2)}, u32[]{:S(2)}) collective-permute-start(f32[4,2,64,128]{3,2,1,0:T(8,128)S(1)} %get-tuple-element.34), channel_id=1, source_target_pairs={{0,8},{8,16},{16,24},{1,9},{9,17},{17,25},{2,10},{10,18},{18,26},{... | collective-permute-start | bytes 786440 | tf_op jit(solution)/shard_map/ppermute | solution.py:12
  22.9 9.1 %copy-start.4 = (f32[64,64,128]{2,1,0:T(8,128)S(1)}, f32[64,64,128]{2,1,0:T(8,128)}, u32[]{:S(2)}) copy-start(f32[64,64,128]{2,1,0:T(8,128)} %param.3) | copy-start | bytes 6291460
  23.0 14.7 %copy-start.2 = (f32[4,64,64,128]{3,1,2,0:T(8,128)S(1)}, f32[4,64,64,128]{3,1,2,0:T(8,128)}, u32[]{:S(2)}) copy-start(f32[4,64,64,128]{3,1,2,0:T(8,128)} %get-tuple-element.33) | copy-start | bytes 25165828
  25.9 10.6 %collective-permute-start.2 = (f32[4,68,2,128]{3,1,2,0:T(8,128)S(1)}, f32[4,68,2,128]{3,1,2,0:T(8,128)S(1)}, u32[]{:S(2)}, u32[]{:S(2)}) collective-permute-start(f32[4,68,2,128]{3,1,2,0:T(8,128)S(1)} %get-tuple-element.27), channel_id=1, source_target_pairs={{2,0},{4,2},{6,4},{3,1},{5,3},{7,5},{10,8},{12,10},{14,12},{11,9},... | collective-permute-start | bytes 835592 | tf_op jit(solution)/shard_map/ppermute | solution.py:15
  27.4 10.3 %collective-permute-start.3 = (f32[4,68,2,128]{3,1,2,0:T(8,128)S(1)}, f32[4,68,2,128]{3,1,2,0:T(8,128)S(1)}, u32[]{:S(2)}, u32[]{:S(2)}) collective-permute-start(f32[4,68,2,128]{3,1,2,0:T(8,128)S(1)} %get-tuple-element.26), channel_id=1, source_target_pairs={{0,2},{2,4},{4,6},{1,3},{3,5},{5,7},{8,10},{10,12},{12,14},{9,11},... | collective-permute-start | bytes 835592 | tf_op jit(solution)/shard_map/ppermute | solution.py:12
  54.7 25.5 %collective-permute-start.4 = (f32[4,68,68,2]{2,1,3,0:T(8,128)S(1)}, f32[4,68,68,2]{2,1,3,0:T(8,128)S(1)}, u32[]{:S(2)}, u32[]{:S(2)}) collective-permute-start(f32[4,68,68,2]{2,1,3,0:T(8,128)S(1)} %copy.51), channel_id=1, source_target_pairs={{1,0},{3,2},{5,4},{7,6},{9,8},{11,10},{13,12},{15,14},{17,16},{19,... | collective-permute-start | bytes 443912 | tf_op jit(solution)/shard_map/ppermute | solution.py:15
  62.3 23.6 %collective-permute-start.5 = (f32[4,68,68,2]{2,1,3,0:T(8,128)S(1)}, f32[4,68,68,2]{2,1,3,0:T(8,128)S(1)}, u32[]{:S(2)}, u32[]{:S(2)}) collective-permute-start(f32[4,68,68,2]{2,1,3,0:T(8,128)S(1)} %copy.53), channel_id=1, source_target_pairs={{0,1},{2,3},{4,5},{6,7},{8,9},{10,11},{12,13},{14,15},{16,17},{18,... | collective-permute-start | bytes 443912 | tf_op jit(solution)/shard_map/ppermute | solution.py:12
  146.6 23.6 %copy-start.1 = (f32[4,64,64,128]{3,1,2,0:T(8,128)}, f32[4,64,64,128]{3,1,2,0:T(8,128)S(1)}, u32[]{:S(2)}) copy-start(f32[4,64,64,128]{3,1,2,0:T(8,128)S(1)} %get-tuple-element.8) | copy-start | bytes 25165828
  146.6 19.1 %copy-start.5 = (f32[64,64,128]{2,1,0:T(8,128)S(1)}, f32[64,64,128]{2,1,0:T(8,128)}, u32[]{:S(2)}) copy-start(f32[64,64,128]{2,1,0:T(8,128)} %param.3) | copy-start | bytes 6291460
  146.8 12.0 %collective-permute-start.6 = (f32[4,2,64,128]{3,2,1,0:T(8,128)S(1)}, f32[4,2,64,128]{3,2,1,0:T(8,128)S(1)}, u32[]{:S(2)}, u32[]{:S(2)}) collective-permute-start(f32[4,2,64,128]{3,2,1,0:T(8,128)S(1)} %copy.58), channel_id=1, source_target_pairs={{8,0},{16,8},{24,16},{9,1},{17,9},{25,17},{10,2},{18,10},{26,18},{... | collective-permute-start | bytes 786440 | tf_op jit(solution)/shard_map/ppermute | solution.py:15
  148.4 10.7 %collective-permute-start.7 = (f32[4,2,64,128]{3,2,1,0:T(8,128)S(1)}, f32[4,2,64,128]{3,2,1,0:T(8,128)S(1)}, u32[]{:S(2)}, u32[]{:S(2)}) collective-permute-start(f32[4,2,64,128]{3,2,1,0:T(8,128)S(1)} %copy.60), channel_id=1, source_target_pairs={{0,8},{8,16},{16,24},{1,9},{9,17},{17,25},{2,10},{10,18},{18,26},{... | collective-permute-start | bytes 786440 | tf_op jit(solution)/shard_map/ppermute | solution.py:12
  159.4 9.6 %collective-permute-start.8 = (f32[4,68,2,128]{3,1,2,0:T(8,128)S(1)}, f32[4,68,2,128]{3,1,2,0:T(8,128)S(1)}, u32[]{:S(2)}, u32[]{:S(2)}) collective-permute-start(f32[4,68,2,128]{3,1,2,0:T(8,128)S(1)} %get-tuple-element.23), channel_id=1, source_target_pairs={{2,0},{4,2},{6,4},{3,1},{5,3},{7,5},{10,8},{12,10},{14,12},{11,9},... | collective-permute-start | bytes 835592 | tf_op jit(solution)/shard_map/ppermute | solution.py:15
  160.7 9.5 %collective-permute-start.9 = (f32[4,68,2,128]{3,1,2,0:T(8,128)S(1)}, f32[4,68,2,128]{3,1,2,0:T(8,128)S(1)}, u32[]{:S(2)}, u32[]{:S(2)}) collective-permute-start(f32[4,68,2,128]{3,1,2,0:T(8,128)S(1)} %get-tuple-element.22), channel_id=1, source_target_pairs={{0,2},{2,4},{4,6},{1,3},{3,5},{5,7},{8,10},{10,12},{12,14},{9,11},... | collective-permute-start | bytes 835592 | tf_op jit(solution)/shard_map/ppermute | solution.py:12
  187.2 25.7 %collective-permute-start.10 = (f32[4,68,68,2]{2,1,3,0:T(8,128)S(1)}, f32[4,68,68,2]{2,1,3,0:T(8,128)S(1)}, u32[]{:S(2)}, u32[]{:S(2)}) collective-permute-start(f32[4,68,68,2]{2,1,3,0:T(8,128)S(1)} %copy.64), channel_id=1, source_target_pairs={{1,0},{3,2},{5,4},{7,6},{9,8},{11,10},{13,12},{15,14},{17,16},{19,... | collective-permute-start | bytes 443912 | tf_op jit(solution)/shard_map/ppermute | solution.py:15
  195.3 23.4 %collective-permute-start.11 = (f32[4,68,68,2]{2,1,3,0:T(8,128)S(1)}, f32[4,68,68,2]{2,1,3,0:T(8,128)S(1)}, u32[]{:S(2)}, u32[]{:S(2)}) collective-permute-start(f32[4,68,68,2]{2,1,3,0:T(8,128)S(1)} %copy.66), channel_id=1, source_target_pairs={{0,1},{2,3},{4,5},{6,7},{8,9},{10,11},{12,13},{14,15},{16,17},{18,... | collective-permute-start | bytes 443912 | tf_op jit(solution)/shard_map/ppermute | solution.py:12
  280.6 27.7 %copy-start = (f32[4,64,64,128]{3,1,2,0:T(8,128)}, f32[4,64,64,128]{3,1,2,0:T(8,128)S(1)}, u32[]{:S(2)}) copy-start(f32[4,64,64,128]{3,1,2,0:T(8,128)S(1)} %fusion.28) | copy-start | bytes 25165828
  280.9 12.5 %collective-permute-start.12 = (f32[4,2,64,128]{3,2,1,0:T(8,128)S(1)}, f32[4,2,64,128]{3,2,1,0:T(8,128)S(1)}, u32[]{:S(2)}, u32[]{:S(2)}) collective-permute-start(f32[4,2,64,128]{3,2,1,0:T(8,128)S(1)} %copy.70), channel_id=1, source_target_pairs={{8,0},{16,8},{24,16},{9,1},{17,9},{25,17},{10,2},{18,10},{26,18},{... | collective-permute-start | bytes 786440 | tf_op jit(solution)/shard_map/ppermute | solution.py:15
  282.2 11.9 %collective-permute-start.13 = (f32[4,2,64,128]{3,2,1,0:T(8,128)S(1)}, f32[4,2,64,128]{3,2,1,0:T(8,128)S(1)}, u32[]{:S(2)}, u32[]{:S(2)}) collective-permute-start(f32[4,2,64,128]{3,2,1,0:T(8,128)S(1)} %copy.72), channel_id=1, source_target_pairs={{0,8},{8,16},{16,24},{1,9},{9,17},{17,25},{2,10},{10,18},{18,26},{... | collective-permute-start | bytes 786440 | tf_op jit(solution)/shard_map/ppermute | solution.py:12
  294.3 10.0 %collective-permute-start.14 = (f32[4,68,2,128]{3,1,2,0:T(8,128)S(1)}, f32[4,68,2,128]{3,1,2,0:T(8,128)S(1)}, u32[]{:S(2)}, u32[]{:S(2)}) collective-permute-start(f32[4,68,2,128]{3,1,2,0:T(8,128)S(1)} %get-tuple-element.19), channel_id=1, source_target_pairs={{2,0},{4,2},{6,4},{3,1},{5,3},{7,5},{10,8},{12,10},{14,12},{11,9},... | collective-permute-start | bytes 835592 | tf_op jit(solution)/shard_map/ppermute | solution.py:15
  295.6 9.9 %collective-permute-start.15 = (f32[4,68,2,128]{3,1,2,0:T(8,128)S(1)}, f32[4,68,2,128]{3,1,2,0:T(8,128)S(1)}, u32[]{:S(2)}, u32[]{:S(2)}) collective-permute-start(f32[4,68,2,128]{3,1,2,0:T(8,128)S(1)} %get-tuple-element.18), channel_id=1, source_target_pairs={{0,2},{2,4},{4,6},{1,3},{3,5},{5,7},{8,10},{10,12},{12,14},{9,11},... | collective-permute-start | bytes 835592 | tf_op jit(solution)/shard_map/ppermute | solution.py:12
  322.6 25.4 %collective-permute-start.16 = (f32[4,68,68,2]{2,1,3,0:T(8,128)S(1)}, f32[4,68,68,2]{2,1,3,0:T(8,128)S(1)}, u32[]{:S(2)}, u32[]{:S(2)}) collective-permute-start(f32[4,68,68,2]{2,1,3,0:T(8,128)S(1)} %copy.76), channel_id=1, source_target_pairs={{1,0},{3,2},{5,4},{7,6},{9,8},{11,10},{13,12},{15,14},{17,16},{19,... | collective-permute-start | bytes 443912 | tf_op jit(solution)/shard_map/ppermute | solution.py:15
  330.2 23.6 %collective-permute-start.17 = (f32[4,68,68,2]{2,1,3,0:T(8,128)S(1)}, f32[4,68,68,2]{2,1,3,0:T(8,128)S(1)}, u32[]{:S(2)}, u32[]{:S(2)}) collective-permute-start(f32[4,68,68,2]{2,1,3,0:T(8,128)S(1)} %copy.78), channel_id=1, source_target_pairs={{0,1},{2,3},{4,5},{6,7},{8,9},{10,11},{12,13},{14,15},{16,17},{18,... | collective-permute-start | bytes 443912 | tf_op jit(solution)/shard_map/ppermute | solution.py:12
  416.1 3.4 copy-start.3
where the time goes:
time: 566 us; the launch traced here: 557 us
  other arithmetic  223 us (39%)
  local copies, waits for them, and re-layouts  131 us (23%)
  matrix products  61.5 us (11%)
  starting transfers between devices  54.2 us (10%)
  blocking collectives  47.4 us (8%)
  between operations  20.4 us (4%)
  waiting for transfers between devices  19.5 us (3%)
    sub x1, other arithmetic, body(): 2.0 * (apply_hamiltonian(level_two, potential) - centre * level_two)  56.6 us
    sub x1, other arithmetic, body(): 2.0 * (apply_hamiltonian(level_one, potential) - centre * level_one)  56.2 us
    div x1, other arithmetic, body(): (apply_hamiltonian(orbitals, potential) - centre * orbitals) / half_width  54.9 us
    concatenate x9, other arithmetic, padded_2(): block = jnp.concatenate([low, block, high], axis=dim)  53.9 us
    psum x1, blocking collectives, body(): gram = lax.psum(local_gram, ('gx', 'gy', 'gz'))  47.4 us
    slice x10, local copies, waits for them, and re-layouts, padded_2(): lax.slice_in_dim(block, 0, width, axis=dim)  43.2 us
    ppermute x9, starting transfers between devices, padded_2(): lax.ppermute(lax.slice_in_dim(block, block.shape[dim] - width, None, axis...  41.8 us
    dot_general x1, matrix products, body(): jnp.einsum('iabc,jabc->ij', filtered, filtered, precision=lax.Precision.H...  36.9 us
  transfers between devices with their start and end apart: 18, of which 9 were waited for; matrix products, arithmetic and copies ran while one was open for 18% of the time, Pallas kernels for 0%

commit v1 on v0

v1 whole, which is shorter than its diff:
```python
import functools

import jax
import jax.numpy as jnp
from jax import lax
from jax.experimental import pallas as pl
from jax.experimental.pallas import tpu as pltpu
from jax.sharding import PartitionSpec as P

CENTRE = 4.5
HALF_WIDTH = 3.5
SCALE = 2.0 / HALF_WIDTH
EDGE = SCALE / 24.0
LANES = 128
TILE = 8
PAD = 8
VMEM_LIMIT = 8 * 1024 * 1024


def vmem_out(shape):
    return pltpu.VMEM(shape, jnp.float32)


def in_vmem(array):
    return pltpu.with_memory_space_constraint(array, pltpu.VMEM)


WHOLE = pl.BlockSpec(memory_space=pltpu.VMEM)
ANYWHERE = pl.BlockSpec(memory_space=pl.ANY)


def params():
    return pltpu.CompilerParams(vmem_limit_bytes=VMEM_LIMIT)


def cost(flops, moved):
    return pl.CostEstimate(flops=flops, bytes_accessed=moved, transcendentals=0)


def pairing(axis, parity):
    pairs = []
    for low in range(parity, lax.axis_size(axis) - 1, 2):
        pairs += [(low, low + 1), (low + 1, low)]
    return pairs


def swap(array, axis, parity):
    pairs = pairing(axis, parity)
    if not pairs:
        return jnp.zeros_like(array)
    return lax.ppermute(array, axis, pairs)


def is_odd(axis):
    return lax.rem(lax.axis_index(axis), 2) == 1


def faces_x_kernel(field, even, odd, sems):
    count = field.shape[1]
    low = field.at[:, pl.ds(0, 2)]
    high = field.at[:, pl.ds(count - 2, 2)]
    flip = is_odd("gx")

    def move(first, second):
        one = pltpu.make_async_copy(first, even, sems.at[0])
        two = pltpu.make_async_copy(second, odd, sems.at[1])
        one.start()
        two.start()
        one.wait()
        two.wait()

    @pl.when(flip)
    def _():
        move(low, high)

    @pl.when(jnp.logical_not(flip))
    def _():
        move(high, low)


def faces_x(orbitals):
    orbs, _, ny, nz = orbitals.shape
    shape = vmem_out((orbs, 2, ny, nz))
    return pl.pallas_call(
        faces_x_kernel,
        out_shape=(shape, shape),
        in_specs=[ANYWHERE],
        out_specs=(WHOLE, WHOLE),
        scratch_shapes=[pltpu.SemaphoreType.DMA((2,))],
        compiler_params=params(),
        name="faces_x",
    )(orbitals)


def pack_y_group(rows, even, odd, orb, group, flip):
    place = pl.ds(group * TILE, TILE)
    for layer in range(2):
        low, high = rows[layer], rows[2 + layer]
        even[orb, layer, place, :] = jnp.where(flip, low, high)
        odd[orb, layer, place, :] = jnp.where(flip, high, low)


def load_kernel(nx, ny, field, potential, out, weight, even, odd, sems):
    orbs = field.shape[0]
    pitch = ny + PAD
    flat = out.reshape(orbs, (nx + 4) * pitch, LANES)
    copies = []
    for orb in range(orbs):
        copy = pltpu.make_async_copy(
            field.at[orb], out.at[orb, pl.ds(2, nx), pl.ds(0, ny)], sems.at[orb]
        )
        copy.start()
        copies.append(copy)
    flip = is_odd("gy")
    zero_planes = jnp.zeros((2 * pitch, LANES), jnp.float32)
    zero_rows = jnp.zeros((PAD, LANES), jnp.float32)
    for orb in range(orbs):
        flat[orb, pl.ds(0, 2 * pitch), :] = zero_planes
        flat[orb, pl.ds((nx + 2) * pitch, 2 * pitch), :] = zero_planes

        @pl.loop(0, nx, unroll=8)
        def _(x):
            flat[orb, pl.ds(pl.multiple_of((x + 2) * pitch + ny, TILE), PAD), :] = zero_rows

    @pl.loop(0, nx, unroll=2)
    def _(x):
        weight[x] = SCALE * potential[x] + SCALE * (0.5 * 7.5 - CENTRE)

    for orb in range(orbs):
        copies[orb].wait()

        @pl.loop(0, nx // TILE, unroll=2)
        def _(group):
            start = (group * TILE + 2) * pitch
            rows = [
                flat[orb, pl.ds(start + y, TILE, stride=pitch), :] for y in (0, 1, ny - 2, ny - 1)
            ]
            pack_y_group(rows, even, odd, orb, group, flip)


def load(orbitals, potential):
    orbs, nx, ny, nz = orbitals.shape
    face = vmem_out((orbs, 2, nx, nz))
    return pl.pallas_call(
        functools.partial(load_kernel, nx, ny),
        out_shape=(
            vmem_out((orbs, nx + 4, ny + PAD, nz)),
            vmem_out((nx, ny, nz)),
            face,
            face,
        ),
        in_specs=[ANYWHERE, WHOLE],
        out_specs=(WHOLE,) * 4,
        scratch_shapes=[pltpu.SemaphoreType.DMA((orbs,))],
        compiler_params=params(),
        cost_estimate=cost(0, orbitals.size * 8),
        name="load",
    )(orbitals, potential)


def pack_z_kernel(nx, ny, field, packed):
    orbs = field.shape[0]
    pitch = ny + PAD
    per = LANES // 4
    lane = lax.broadcasted_iota(jnp.int32, (TILE, LANES), 1)
    flat = field.reshape(orbs, (nx + 4) * pitch, LANES)
    unroll = 8

    @pl.loop(0, orbs * (nx // per))
    def _(index):
        orb = index // (nx // per)
        group = index % (nx // per)

        @pl.loop(0, ny // TILE)
        def _(tile):
            def step(part, total):
                for which in range(unroll):
                    plane = part * unroll + which
                    start = pl.multiple_of(
                        (group * per + plane + 2) * pitch + tile * TILE, TILE
                    )
                    rows = flat[orb, pl.ds(start, TILE), :]
                    moved = pltpu.roll(rows, 4 * which + 2, 1)
                    total = jnp.where(lane // 4 == which, moved, total)
                return pltpu.roll(total, LANES - 4 * unroll, 1)

            total = jnp.zeros((TILE, LANES), jnp.float32)
            for part in range(per // unroll):
                total = step(part, total)
            packed[orb, group, pl.ds(pl.multiple_of(tile * TILE, TILE), TILE), :] = total


def pack_z(field, nx, ny):
    orbs = field.shape[0]
    return pl.pallas_call(
        functools.partial(pack_z_kernel, nx, ny),
        out_shape=vmem_out((orbs, nx * 4 // LANES, ny, LANES)),
        in_specs=[WHOLE],
        out_specs=WHOLE,
        compiler_params=params(),
        cost_estimate=cost(0, field.size * 4),
        name="pack_z",
    )(in_vmem(field))


def step_kernel(nx, ny, first, field, weight, own, z_even, z_odd, *rest):
    if first:
        out, correction = rest
    else:
        before, out, correction = rest
    orbs = field.shape[0]
    pitch = ny + PAD
    per = LANES // 4
    flat = field.reshape(orbs, (nx + 4) * pitch, LANES)
    flat_out = out.reshape(orbs, (nx + 4) * pitch, LANES)
    edge = EDGE * (0.5 if first else 1.0)
    chunk = 8
    flip = is_odd("gz")
    wide = lax.broadcasted_iota(jnp.int32, (ny, LANES), 1) % 4
    lane = lax.broadcasted_iota(jnp.int32, (TILE, LANES), 1)
    ends = (lane < 2) | (lane >= LANES - 2)

    if first:
        zero_planes = jnp.zeros((2 * pitch, LANES), jnp.float32)
        zero_rows = jnp.zeros((PAD, LANES), jnp.float32)
        for orb in range(orbs):
            flat_out[orb, pl.ds(0, 2 * pitch), :] = zero_planes
            flat_out[orb, pl.ds((nx + 2) * pitch, 2 * pitch), :] = zero_planes

            @pl.loop(0, nx, unroll=8)
            def _(x):
                place = pl.ds(pl.multiple_of((x + 2) * pitch + ny, TILE), PAD)
                flat_out[orb, place, :] = zero_rows

    for orb in range(orbs):
        for group in range(nx // per):
            mine = own[orb, group]
            even, odd = z_even[orb, group], z_odd[orb, group]
            below = jnp.where(flip, even, odd)
            above = jnp.where(flip, odd, even)
            gap = jnp.where(wide < 2, below, above) - mine
            left = pltpu.roll(gap, LANES - 2, 1) - 16.0 * jnp.where(
                wide == 1, pltpu.roll(gap, LANES - 1, 1), 0.0
            )
            right = pltpu.roll(gap, 2, 1) - 16.0 * jnp.where(
                wide == 2, pltpu.roll(gap, 1, 1), 0.0
            )
            correction[orb, group] = edge * jnp.where(wide < 2, left, right)

    @pl.loop(0, orbs)
    def _(orb):
        @pl.loop(0, nx // chunk)
        def _(part):
            x0 = part * chunk
            group = x0 // per
            turn = lax.rem(LANES - 4 * lax.rem(x0, per), LANES)

            for tile in range(ny // TILE):
                base = (x0 + 2) * pitch + tile * TILE

                def rows(plane, shift=0):
                    start = base + plane * pitch + shift
                    if shift == 0:
                        start = pl.multiple_of(start, TILE)
                    return flat[orb, pl.ds(start, TILE), :]

                mine = [rows(plane) for plane in range(-2, chunk + 2)]
                place = pl.ds(tile * TILE, TILE)
                fix = pltpu.roll(correction[orb, group, place, :], turn, 1)
                for plane in range(chunk):
                    centre = mine[plane + 2]
                    near = (
                        (mine[plane + 1] + mine[plane + 3])
                        + (rows(plane, -1) + rows(plane, 1))
                        + (pltpu.roll(centre, 1, 1) + pltpu.roll(centre, LANES - 1, 1))
                    )
                    far = (
                        (mine[plane] + mine[plane + 4])
                        + (rows(plane, -2) + rows(plane, 2))
                        + (pltpu.roll(centre, 2, 1) + pltpu.roll(centre, LANES - 2, 1))
                    )
                    ours = weight[x0 + plane, place, :]
                    if first:
                        ours = 0.5 * ours
                    value = ours * centre + edge * (far - 16.0 * near)
                    value = value + jnp.where(
                        ends, pltpu.roll(fix, LANES - 4 * plane - 2, 1), 0.0
                    )
                    there = pl.ds(pl.multiple_of(base + plane * pitch, TILE), TILE)
                    if not first:
                        value = value - flat_before(before, orbs, nx, pitch)[orb, there, :]
                    flat_out[orb, there, :] = value


def flat_before(before, orbs, nx, pitch):
    return before.reshape(orbs, (nx + 4) * pitch, LANES)


def step(field, weight, packed, z_even, z_odd, before):
    orbs = field.shape[0]
    nx, ny, nz = weight.shape
    first = before is None
    args = [field, weight, packed, z_even, z_odd] + ([] if first else [before])
    return pl.pallas_call(
        functools.partial(step_kernel, nx, ny, first),
        out_shape=vmem_out(field.shape),
        in_specs=[WHOLE] * len(args),
        out_specs=WHOLE,
        scratch_shapes=[pltpu.VMEM(packed.shape, jnp.float32)],
        input_output_aliases={} if first else {5: 0},
        compiler_params=params(),
        cost_estimate=cost(field.size * 20, field.size * 12),
        name="step",
    )(*[in_vmem(arg) for arg in args])


def edges_kernel(nx, ny, edge, last, field, x_even, x_odd, y_even, y_odd, out, *faces):
    orbs = field.shape[0]
    pitch = ny + PAD
    flat = out.reshape(orbs, (nx + 4) * pitch, LANES)
    flip_x, flip_y = is_odd("gx"), is_odd("gy")
    if not last:
        next_x_even, next_x_odd, next_y_even, next_y_odd = faces

    def plane_rows(x):
        return pl.ds((x + 2) * pitch, ny)

    @pl.loop(0, orbs)
    def _(orb):
        def halves(layer):
            even, odd = x_even[orb, layer], x_odd[orb, layer]
            return jnp.where(flip_x, even, odd), jnp.where(flip_x, odd, even)

        low_far, high_near = halves(0)
        low_near, high_far = halves(1)
        flat[orb, plane_rows(0), :] += edge * (low_far - 16.0 * low_near)
        flat[orb, plane_rows(1), :] += edge * low_near
        flat[orb, plane_rows(nx - 2), :] += edge * high_near
        flat[orb, plane_rows(nx - 1), :] += edge * (high_far - 16.0 * high_near)

        @pl.loop(0, nx // TILE, unroll=2)
        def _(group):
            place = pl.ds(group * TILE, TILE)

            def pick(layer):
                even, odd = y_even[orb, layer, place, :], y_odd[orb, layer, place, :]
                return jnp.where(flip_y, even, odd), jnp.where(flip_y, odd, even)

            low_far, high_near = pick(0)
            low_near, high_far = pick(1)
            adds = (
                edge * (low_far - 16.0 * low_near),
                edge * low_near,
                edge * high_near,
                edge * (high_far - 16.0 * high_near),
            )
            start = (group * TILE + 2) * pitch
            rows = []
            for y, add in zip((0, 1, ny - 2, ny - 1), adds):
                there = pl.ds(start + y, TILE, stride=pitch)
                value = flat[orb, there, :] + add
                flat[orb, there, :] = value
                rows.append(value)
            if not last:
                pack_y_group(rows, next_y_even, next_y_odd, orb, group, flip_y)

        if not last:
            for layer in range(2):
                low = flat[orb, plane_rows(layer), :]
                high = flat[orb, plane_rows(nx - 2 + layer), :]
                next_x_even[orb, layer] = jnp.where(flip_x, low, high)
                next_x_odd[orb, layer] = jnp.where(flip_x, high, low)


def edges(field, nx, ny, halos, edge, last):
    orbs, nz = field.shape[0], field.shape[-1]
    shapes = [vmem_out(field.shape)]
    if not last:
        shapes += [vmem_out((orbs, 2, ny, nz))] * 2 + [vmem_out((orbs, 2, nx, nz))] * 2
    return pl.pallas_call(
        functools.partial(edges_kernel, nx, ny, edge, last),
        out_shape=tuple(shapes),
        in_specs=[WHOLE] * 5,
        out_specs=(WHOLE,) * len(shapes),
        input_output_aliases={0: 0},
        compiler_params=params(),
        cost_estimate=cost(0, field.size),
        name="edges",
    )(*[in_vmem(arg) for arg in (field, *halos)])


PAIRS = [(line, column) for line in range(4) for column in range(line, 4)]


def pair_list(orbs):
    return [(line, column) for line in range(orbs) for column in range(line, orbs)]


def gram_kernel(nx, ny, field, out):
    orbs = field.shape[0]
    pitch = ny + PAD
    flat = field.reshape(orbs, (nx + 4) * pitch, LANES)
    pairs = pair_list(orbs)

    def plane(x, totals):
        totals = list(totals)
        for tile in range(ny // TILE):
            start = pl.multiple_of((x + 2) * pitch + tile * TILE, TILE)
            rows = [flat[orb, pl.ds(start, TILE), :] for orb in range(orbs)]
            for index, (line, column) in enumerate(pairs):
                totals[index] = totals[index] + rows[line] * rows[column]
        return tuple(totals)

    zero = jnp.zeros((TILE, LANES), jnp.float32)
    totals = lax.fori_loop(0, nx, plane, (zero,) * len(pairs))
    out[...] = jnp.zeros_like(out)
    for index, total in enumerate(totals):
        out[pl.ds(index, 1), :] = jnp.sum(total, axis=0, keepdims=True)


def gram(field, nx, ny):
    orbs = field.shape[0]
    rows = -(-len(pair_list(orbs)) // TILE) * TILE
    return pl.pallas_call(
        functools.partial(gram_kernel, nx, ny),
        out_shape=jax.ShapeDtypeStruct((rows, LANES), jnp.float32),
        in_specs=[WHOLE],
        out_specs=WHOLE,
        compiler_params=params(),
        name="gram",
    )(in_vmem(field))


def basis_kernel(nx, ny, chunk, cells, parts, field, *rest):
    sums, (out, factor, inverse) = rest[:parts], rest[parts:]
    orbs = field.shape[0]
    pitch = ny + PAD
    flat = field.reshape(orbs, (nx + 4) * pitch, LANES)
    pairs = pair_list(orbs)

    @pl.when(pl.program_id(0) == 0)
    def _():
        total = sums[0][...]
        for part in sums[1:]:
            total = total + part[...]
        total = jnp.broadcast_to(jnp.sum(total, axis=1, keepdims=True), total.shape) / cells
        entry = {}
        for index, pair in enumerate(pairs):
            entry[pair] = total[index : index + 1, :]
        upper, inv = {}, {}
        for line in range(orbs):
            for column in range(line, orbs):
                value = entry[line, column]
                for inner in range(line):
                    value = value - upper[inner, line] * upper[inner, column]
                if column == line:
                    upper[line, line] = jnp.sqrt(value)
                    inv[line, line] = 1.0 / upper[line, line]
                else:
                    upper[line, column] = value * inv[line, line]
        for column in range(orbs):
            for line in range(column - 1, -1, -1):
                value = upper[line, line + 1] * inv[line + 1, column]
                for inner in range(line + 2, column + 1):
                    value = value + upper[line, inner] * inv[inner, column]
                inv[line, column] = -value * inv[line, line]
        row = lax.broadcasted_iota(jnp.int32, (TILE, LANES), 0)
        col = lax.broadcasted_iota(jnp.int32, (TILE, LANES), 1)
        whole = jnp.zeros((TILE, LANES), jnp.float32)
        for (line, column), value in upper.items():
            there = (row == line) & (col == column)
            whole = jnp.where(there, jnp.broadcast_to(value, whole.shape), whole)
        factor[...] = whole[:orbs, :orbs]
        for index, pair in enumerate(pairs):
            inverse[index] = jnp.broadcast_to(inv[pair], (TILE, LANES))

    first = pl.program_id(0) * chunk
    gains = {pair: inverse[index] for index, pair in enumerate(pairs)}

    @pl.loop(0, chunk)
    def _(plane):
        for tile in range(ny // TILE):
            start = pl.multiple_of((first + plane + 2) * pitch + tile * TILE, TILE)
            rows = [flat[orb, pl.ds(start, TILE), :] for orb in range(orbs)]
            for column in range(orbs):
                value = rows[0] * gains[0, column]
                for line in range(1, column + 1):
                    value = value + rows[line] * gains[line, column]
                out[column, plane, pl.ds(tile * TILE, TILE), :] = value


def basis(field, nx, ny, sums, cells):
    orbs, nz = field.shape[0], field.shape[-1]
    chunk = 4
    return pl.pallas_call(
        functools.partial(basis_kernel, nx, ny, chunk, cells, len(sums)),
        out_shape=(
            jax.ShapeDtypeStruct((orbs, nx, ny, nz), jnp.float32),
            jax.ShapeDtypeStruct((orbs, orbs), jnp.float32),
        ),
        grid=(nx // chunk,),
        in_specs=[WHOLE] * (1 + len(sums)),
        out_specs=(
            pl.BlockSpec((orbs, chunk, ny, nz), lambda i: (0, i, 0, 0)),
            pl.BlockSpec((orbs, orbs), lambda i: (0, 0)),
        ),
        scratch_shapes=[pltpu.VMEM((len(pair_list(orbs)), TILE, LANES), jnp.float32)],
        compiler_params=params(),
        name="basis",
    )(in_vmem(field), *sums)


def rotations(array, axis):
    count = lax.axis_size(axis)
    return [
        lax.ppermute(array, axis, [(i, (i + by) % count) for i in range(count)])
        for by in range(1, count)
    ]


def body(orbitals, potential):
    _, nx, ny, _ = orbitals.shape
    cells = (
        nx
        * lax.axis_size("gx")
        * (ny * lax.axis_size("gy"))
        * (orbitals.shape[3] * lax.axis_size("gz"))
    )
    x_faces = faces_x(orbitals)
    halo_x = [swap(face, "gx", parity) for parity, face in enumerate(x_faces)]
    field, weight, *y_faces = load(orbitals, potential)
    before = None
    for level in range(3):
        last = level == 2
        halo_y = [swap(face, "gy", parity) for parity, face in enumerate(y_faces)]
        packed = pack_z(field, nx, ny)
        z_even, z_odd = swap(packed, "gz", 0), swap(packed, "gz", 1)
        after = step(field, weight, packed, z_even, z_odd, before)
        edge = EDGE * (0.5 if level == 0 else 1.0)
        after, *faces = edges(after, nx, ny, (*halo_x, *halo_y), edge, last)
        if not last:
            halo_x = [swap(face, "gx", parity) for parity, face in enumerate(faces[:2])]
            y_faces = faces[2:]
        before, field = field, after
    local = gram(field, nx, ny)
    for axis in ("gz", "gy"):
        for part in rotations(local, axis):
            local = local + part
    return basis(field, nx, ny, [local, *rotations(local, "gx")], cells)


def solution(mesh):
    return jax.shard_map(
        body,
        mesh=mesh,
        in_specs=(P(None, "gx", "gy", "gz"), P("gx", "gy", "gz")),
        out_specs=(P(None, "gx", "gy", "gz"), P()),
        check_vma=False,
    )
```

time: 566 us -> 198 us (0.35); the launches traced: 557 us -> 197 us
  other arithmetic: 223 us -> 0.01 us
  Pallas kernels: 0 us -> 150 us
  local copies, waits for them, and re-layouts: 131 us -> 4.98 us
  matrix products: 61.5 us -> 0 us
  blocking collectives: 47.4 us -> 0 us
  starting transfers between devices: 54.2 us -> 31.2 us
  between operations: 20.4 us -> 0.9 us
  waiting for transfers between devices: 19.5 us -> 10.4 us
    pallas_call x0 -> x13, Pallas kernels: none -> 150 us  [the longest x3 69.5 us: pack_z(): pl.pallas_call(functools.partial(pack_z_kernel, nx, ny), out_shape=vmem_o...]
    sub x2 -> x0, other arithmetic: 113 us -> none  [the longest x1 56.6 us: body(): 2.0 * (apply_hamiltonian(level_two, potential) - centre * level_two)]
    slice x21 -> x0, local copies, waits for them, and re-layouts: 66.5 us -> none  [the longest x10 43.2 us: padded_2(): lax.slice_in_dim(block, 0, width, axis=dim)]
    dot_general x2 -> x0, matrix products: 61.5 us -> none  [the longest x1 36.9 us: body(): jnp.einsum('iabc,jabc->ij', filtered, filtered, precision=lax.Precision.H...]
    div x1 -> x0, other arithmetic: 54.9 us -> none  [body(): (apply_hamiltonian(orbitals, potential) - centre * orbitals) / half_width]
    concatenate x9 -> x0, other arithmetic: 53.9 us -> none  [padded_2(): block = jnp.concatenate([low, block, high], axis=dim)]
    psum x1 -> x0, blocking collectives: 47.4 us -> none  [body(): gram = lax.psum(local_gram, ('gx', 'gy', 'gz'))]
    ppermute x11 -> x0, local copies, waits for them, and re-layouts: 35.7 us -> none  [the longest x6 18.1 us: padded_2(): lax.ppermute(lax.slice_in_dim(block, block.shape[dim] - width, None, axis...]
  transfers between devices with their start and end apart: 18 -> 22, of which waited for: 9 -> 6; matrix products, arithmetic and copies ran while one was open for 18% -> 0% of each run, Pallas kernels for 0% -> 34%
where the time goes in v1:
time: 198 us; the launch traced here: 197 us
  Pallas kernels  150 us (76%)
  starting transfers between devices  31.2 us (16%)
  waiting for transfers between devices  10.4 us (5%)
  local copies, waits for them, and re-layouts  4.98 us (3%)
    pallas_call x3, Pallas kernels, pack_z(): pl.pallas_call(functools.partial(pack_z_kernel, nx, ny), out_shape=vmem_o...  69.5 us
    pallas_call x3, Pallas kernels, step(): pl.pallas_call(functools.partial(step_kernel, nx, ny, first), out_shape=v...  67.9 us
    ppermute x15, starting transfers between devices, swap(): return lax.ppermute(array, axis, pairs)  20.6 us
    ppermute x7, starting transfers between devices, rotations(): lax.ppermute(array, axis, [(i, (i + by) % count) for i in range(count)])  10.6 us
    ppermute x7, waiting for transfers between devices, rotations(): lax.ppermute(array, axis, [(i, (i + by) % count) for i in range(count)])  10.4 us
    pallas_call x1, Pallas kernels, basis(): pl.pallas_call(functools.partial(basis_kernel, nx, ny, chunk, cells, len(...  7.44 us
    unnamed x4, local copies, waits for them, and re-layouts  4.97 us
  transfers between devices with their start and end apart: 22, of which 6 were waited for; matrix products, arithmetic and copies ran while one was open for 0% of the time, Pallas kernels for 34%

profile of v1, /device:TPU:0, one launch (start us, length us, event | category | flops | bytes accessed | tf_op | source)
XLA Modules:
  0.0 197.3 jit_solution(17385002749664211271)
XLA Ops:
  0.6 3.4 %copy-done = f32[4,64,64,128]{3,2,1,0:T(8,128)S(1)} copy-done((f32[4,64,64,128]{3,2,1,0:T(8,128)S(1)}, f32[4,64,64,128]{3,2,1,0:T(8,128)}, u32[]{:S(2)}) %copy-start) | copy-done | bytes 8388632
  4.0 1.6 copy-done.1
  5.6 2.0 load.1
  7.6 23.2 %pack_z.3.own = f32[4,2,64,128]{3,2,1,0:T(8,128)S(1)} custom-call(f32[4,68,72,128]{3,2,1,0:T(8,128)S(1)} %get-tuple-element.18.field.rest_0_), custom_call_target="tpu_custom_call" | custom-call | bytes 10027008 | tf_op jit(solution)/shard_map/pack_z/pallas_call | solution.py:195
  31.3 2.6 %collective-permute-start.1 = (f32[4,2,64,128]{3,2,1,0:T(8,128)S(1)}, f32[4,2,64,128]{3,2,1,0:T(8,128)S(1)}, u32[]{:S(2)}, u32[]{:S(2)}) collective-permute-start(f32[4,2,64,128]{3,2,1,0:T(8,128)S(1)} %get-tuple-element.20), channel_id=1, source_target_pairs={{0,8},{8,0},{16,24},{24,16},{1,9},{9,1},{17,25},{25,17},{2,10},{10... | collective-permute-start | bytes 786440 | tf_op jit(solution)/shard_map/ppermute | solution.py:51
  33.8 0.7 collective-permute-start.2
  34.5 1.6 collective-permute-start.3
  36.1 0.7 collective-permute-start.4
  36.9 24.7 %step.3.field = f32[4,68,72,128]{3,2,1,0:T(8,128)S(1)} custom-call(f32[4,68,72,128]{3,2,1,0:T(8,128)S(1)} %get-tuple-element.18.field.rest_0_, f32[64,64,128]{2,1,0:T(8,128)S(1)} %get-tuple-element.19.weight, f32[4,2,64,128]{3,2,1,0:T(8,128)S(1)} %pack_z.3.own, f32[4,2,64,128]{3,2,1,0:T(8,128)S(1)} %collective-permute-done.z_even, ...), custom_call_target="tpu_custom_call" | custom-call | flops 50135040 | bytes 30081024 | tf_op jit(solution)/shard_map/step/pallas_call | solution.py:304
  62.0 23.2 %pack_z.4.own = f32[4,2,64,128]{3,2,1,0:T(8,128)S(1)} custom-call(f32[4,68,72,128]{3,2,1,0:T(8,128)S(1)} %get-tuple-element.24.field.rest_0_), custom_call_target="tpu_custom_call" | custom-call | bytes 10027008 | tf_op jit(solution)/shard_map/pack_z/pallas_call | solution.py:195
  85.2 4.2 %collective-permute-start.6 = (f32[4,2,64,128]{3,2,1,0:T(8,128)S(1)}, f32[4,2,64,128]{3,2,1,0:T(8,128)S(1)}, u32[]{:S(2)}, u32[]{:S(2)}) collective-permute-start(f32[4,2,64,128]{3,2,1,0:T(8,128)S(1)} %get-tuple-element.25), channel_id=1, source_target_pairs={{0,8},{8,0},{16,24},{24,16},{1,9},{9,1},{17,25},{25,17},{2,10},{10... | collective-permute-start | bytes 786440 | tf_op jit(solution)/shard_map/ppermute | solution.py:51
  89.5 0.7 collective-permute-start.7
  90.1 4.4 %collective-permute-start.8 = (f32[4,2,64,128]{3,2,1,0:T(8,128)S(1)}, f32[4,2,64,128]{3,2,1,0:T(8,128)S(1)}, u32[]{:S(2)}, u32[]{:S(2)}) collective-permute-start(f32[4,2,64,128]{3,2,1,0:T(8,128)S(1)} %get-tuple-element.27), channel_id=1, source_target_pairs={{0,2},{2,0},{4,6},{6,4},{1,3},{3,1},{5,7},{7,5},{8,10},{10,8},{12,... | collective-permute-start | bytes 786440 | tf_op jit(solution)/shard_map/ppermute | solution.py:51
  94.6 0.7 collective-permute-start.9
  95.3 21.6 %step.4.field = f32[4,68,72,128]{3,2,1,0:T(8,128)S(1)} custom-call(f32[4,68,72,128]{3,2,1,0:T(8,128)S(1)} %get-tuple-element.24.field.rest_0_, f32[64,64,128]{2,1,0:T(8,128)S(1)} %get-tuple-element.19.weight, f32[4,2,64,128]{3,2,1,0:T(8,128)S(1)} %pack_z.4.own, f32[4,2,64,128]{3,2,1,0:T(8,128)S(1)} %collective-permute-done.5.z_even, ...), custom_call_target="tpu_custom_call", output_to_operand_aliasing={{}: (5, {})} | custom-call | flops 50135040 | bytes 30081024 | tf_op jit(solution)/shard_map/step/pallas_call | solution.py:304
  117.4 23.2 %pack_z.5.own = f32[4,2,64,128]{3,2,1,0:T(8,128)S(1)} custom-call(f32[4,68,72,128]{3,2,1,0:T(8,128)S(1)} %get-tuple-element.29.field), custom_call_target="tpu_custom_call" | custom-call | bytes 10027008 | tf_op jit(solution)/shard_map/pack_z/pallas_call | solution.py:195
  140.5 1.8 collective-permute-start.11
  142.3 0.7 collective-permute-start.12
  143.0 1.5 collective-permute-start.13
  145.2 21.6 %step.5.field = f32[4,68,72,128]{3,2,1,0:T(8,128)S(1)} custom-call(f32[4,68,72,128]{3,2,1,0:T(8,128)S(1)} %get-tuple-element.29.field, f32[64,64,128]{2,1,0:T(8,128)S(1)} %get-tuple-element.19.weight, f32[4,2,64,128]{3,2,1,0:T(8,128)S(1)} %pack_z.5.own, f32[4,2,64,128]{3,2,1,0:T(8,128)S(1)} %collective-permute-done.10.z_even, ...), custom_call_target="tpu_custom_call", output_to_operand_aliasing={{}: (5, {})} | custom-call | flops 50135040 | bytes 30081024 | tf_op jit(solution)/shard_map/step/pallas_call | solution.py:304
  167.2 1.6 gram.1
  169.0 1.2 collective-permute-done.15
  170.1 2.8 %collective-permute-start.18 = (f32[16,128]{1,0:T(8,128)S(1)}, f32[16,128]{1,0:T(8,128)S(1)}, u32[]{:S(2)}, u32[]{:S(2)}) collective-permute-start(f32[16,128]{1,0:T(8,128)S(1)} %add.12), channel_id=1, source_target_pairs={{0,6},{2,0},{4,2},{6,4},{1,7},{3,1},{5,3},{7,5},{8,14},{10,8},{12,... | collective-permute-start | bytes 24584 | tf_op jit(solution)/shard_map/ppermute | solution.py:516
  172.9 1.8 collective-permute-start.17
  174.7 0.7 collective-permute-start.16
  175.4 2.0 %collective-permute-done.17 = f32[16,128]{1,0:T(8,128)S(1)} collective-permute-done((f32[16,128]{1,0:T(8,128)S(1)}, f32[16,128]{1,0:T(8,128)S(1)}, u32[]{:S(2)}, u32[]{:S(2)}) %collective-permute-start.17) | collective-permute-done | bytes 8224 | tf_op jit(solution)/shard_map/ppermute | solution.py:516
  177.4 2.7 %collective-permute-done.16 = f32[16,128]{1,0:T(8,128)S(1)} collective-permute-done((f32[16,128]{1,0:T(8,128)S(1)}, f32[16,128]{1,0:T(8,128)S(1)}, u32[]{:S(2)}, u32[]{:S(2)}) %collective-permute-start.16) | collective-permute-done | bytes 8224 | tf_op jit(solution)/shard_map/ppermute | solution.py:516
  180.1 2.4 %collective-permute-start.21 = (f32[16,128]{1,0:T(8,128)S(1)}, f32[16,128]{1,0:T(8,128)S(1)}, u32[]{:S(2)}, u32[]{:S(2)}) collective-permute-start(f32[16,128]{1,0:T(8,128)S(1)} %add_add_fusion.rest_0_), channel_id=1, source_target_pairs={{0,24},{8,0},{16,8},{24,16},{1,25},{9,1},{17,9},{25,17},{2,26},{10... | collective-permute-start | bytes 24584 | tf_op jit(solution)/shard_map/ppermute | solution.py:516
  182.6 2.7 %collective-permute-start.20 = (f32[16,128]{1,0:T(8,128)S(1)}, f32[16,128]{1,0:T(8,128)S(1)}, u32[]{:S(2)}, u32[]{:S(2)}) collective-permute-start(f32[16,128]{1,0:T(8,128)S(1)} %add_add_fusion.rest_0_), channel_id=1, source_target_pairs={{0,16},{8,24},{16,0},{24,8},{1,17},{9,25},{17,1},{25,9},{2,18},{10... | collective-permute-start | bytes 24584 | tf_op jit(solution)/shard_map/ppermute | solution.py:516
  185.5 1.5 collective-permute-done.20.rest_2_
  186.9 2.9 %collective-permute-done.19.rest_1_ = f32[16,128]{1,0:T(8,128)S(1)} collective-permute-done((f32[16,128]{1,0:T(8,128)S(1)}, f32[16,128]{1,0:T(8,128)S(1)}, u32[]{:S(2)}, u32[]{:S(2)}) %collective-permute-start.19) | collective-permute-done | bytes 8224 | tf_op jit(solution)/shard_map/ppermute | solution.py:516
  189.9 7.4 %basis.1 = (f32[4,64,64,128]{3,2,1,0:T(8,128)}, f32[4,4]{1,0:T(4,128)}) custom-call(f32[4,68,72,128]{3,2,1,0:T(8,128)S(1)} %edges.5.field, f32[16,128]{1,0:T(8,128)S(1)} %add_add_fusion.rest_0_, f32[16,128]{1,0:T(8,128)S(1)} %collective-permute-done.19.rest_1_, f32[16,128]{1,0:T(8,128)S(1)} %collective-permute-done.20.rest_2_, ...), custom_call_target="tpu_custom_call" | custom-call | tf_op jit(solution)/shard_map/basis/pallas_call | solution.py:495
  (32 shorter events, 2.8 us)
Async XLA Ops:
  0.6 3.4 %copy-start = (f32[4,64,64,128]{3,2,1,0:T(8,128)S(1)}, f32[4,64,64,128]{3,2,1,0:T(8,128)}, u32[]{:S(2)}) copy-start(f32[4,64,64,128]{3,2,1,0:T(8,128)} %field.3) | copy-start | bytes 25165828
  4.0 1.6 copy-start.1
  30.7 6.1 %collective-permute-start = (f32[4,2,64,128]{3,2,1,0:T(8,128)S(1)}, f32[4,2,64,128]{3,2,1,0:T(8,128)S(1)}, u32[]{:S(2)}, u32[]{:S(2)}) collective-permute-start(f32[4,2,64,128]{3,2,1,0:T(8,128)S(1)} %pack_z.3.own), channel_id=1, source_target_pairs={{0,1},{1,0},{2,3},{3,2},{4,5},{5,4},{6,7},{7,6},{8,9},{9,8},{10,11... | collective-permute-start | bytes 786440 | tf_op jit(solution)/shard_map/ppermute | solution.py:51
  31.3 30.3 %collective-permute-start.1 = (f32[4,2,64,128]{3,2,1,0:T(8,128)S(1)}, f32[4,2,64,128]{3,2,1,0:T(8,128)S(1)}, u32[]{:S(2)}, u32[]{:S(2)}) collective-permute-start(f32[4,2,64,128]{3,2,1,0:T(8,128)S(1)} %get-tuple-element.20), channel_id=1, source_target_pairs={{0,8},{8,0},{16,24},{24,16},{1,9},{9,1},{17,25},{25,17},{2,10},{10... | collective-permute-start | bytes 786440 | tf_op jit(solution)/shard_map/ppermute | solution.py:51
  33.8 27.7 %collective-permute-start.2 = (f32[4,2,64,128]{3,2,1,0:T(8,128)S(1)}, f32[4,2,64,128]{3,2,1,0:T(8,128)S(1)}, u32[]{:S(2)}, u32[]{:S(2)}) collective-permute-start(f32[4,2,64,128]{3,2,1,0:T(8,128)S(1)} %get-tuple-element.21), channel_id=1, source_target_pairs={{8,16},{16,8},{9,17},{17,9},{10,18},{18,10},{11,19},{19,11},{12,20... | collective-permute-start | bytes 786440 | tf_op jit(solution)/shard_map/ppermute | solution.py:51
  34.5 27.1 %collective-permute-start.3 = (f32[4,2,64,128]{3,2,1,0:T(8,128)S(1)}, f32[4,2,64,128]{3,2,1,0:T(8,128)S(1)}, u32[]{:S(2)}, u32[]{:S(2)}) collective-permute-start(f32[4,2,64,128]{3,2,1,0:T(8,128)S(1)} %get-tuple-element.22), channel_id=1, source_target_pairs={{0,2},{2,0},{4,6},{6,4},{1,3},{3,1},{5,7},{7,5},{8,10},{10,8},{12,... | collective-permute-start | bytes 786440 | tf_op jit(solution)/shard_map/ppermute | solution.py:51
  36.1 25.5 %collective-permute-start.4 = (f32[4,2,64,128]{3,2,1,0:T(8,128)S(1)}, f32[4,2,64,128]{3,2,1,0:T(8,128)S(1)}, u32[]{:S(2)}, u32[]{:S(2)}) collective-permute-start(f32[4,2,64,128]{3,2,1,0:T(8,128)S(1)} %get-tuple-element.23), channel_id=1, source_target_pairs={{2,4},{4,2},{3,5},{5,3},{10,12},{12,10},{11,13},{13,11},{18,20},{2... | collective-permute-start | bytes 786440 | tf_op jit(solution)/shard_map/ppermute | solution.py:51
  85.2 10.1 %collective-permute-start.5 = (f32[4,2,64,128]{3,2,1,0:T(8,128)S(1)}, f32[4,2,64,128]{3,2,1,0:T(8,128)S(1)}, u32[]{:S(2)}, u32[]{:S(2)}) collective-permute-start(f32[4,2,64,128]{3,2,1,0:T(8,128)S(1)} %pack_z.4.own), channel_id=1, source_target_pairs={{0,1},{1,0},{2,3},{3,2},{4,5},{5,4},{6,7},{7,6},{8,9},{9,8},{10,11... | collective-permute-start | bytes 786440 | tf_op jit(solution)/shard_map/ppermute | solution.py:51
  85.2 31.7 %collective-permute-start.6 = (f32[4,2,64,128]{3,2,1,0:T(8,128)S(1)}, f32[4,2,64,128]{3,2,1,0:T(8,128)S(1)}, u32[]{:S(2)}, u32[]{:S(2)}) collective-permute-start(f32[4,2,64,128]{3,2,1,0:T(8,128)S(1)} %get-tuple-element.25), channel_id=1, source_target_pairs={{0,8},{8,0},{16,24},{24,16},{1,9},{9,1},{17,25},{25,17},{2,10},{10... | collective-permute-start | bytes 786440 | tf_op jit(solution)/shard_map/ppermute | solution.py:51
  89.5 27.4 %collective-permute-start.7 = (f32[4,2,64,128]{3,2,1,0:T(8,128)S(1)}, f32[4,2,64,128]{3,2,1,0:T(8,128)S(1)}, u32[]{:S(2)}, u32[]{:S(2)}) collective-permute-start(f32[4,2,64,128]{3,2,1,0:T(8,128)S(1)} %get-tuple-element.26), channel_id=1, source_target_pairs={{8,16},{16,8},{9,17},{17,9},{10,18},{18,10},{11,19},{19,11},{12,20... | collective-permute-start | bytes 786440 | tf_op jit(solution)/shard_map/ppermute | solution.py:51
  90.1 26.8 %collective-permute-start.8 = (f32[4,2,64,128]{3,2,1,0:T(8,128)S(1)}, f32[4,2,64,128]{3,2,1,0:T(8,128)S(1)}, u32[]{:S(2)}, u32[]{:S(2)}) collective-permute-start(f32[4,2,64,128]{3,2,1,0:T(8,128)S(1)} %get-tuple-element.27), channel_id=1, source_target_pairs={{0,2},{2,0},{4,6},{6,4},{1,3},{3,1},{5,7},{7,5},{8,10},{10,8},{12,... | collective-permute-start | bytes 786440 | tf_op jit(solution)/shard_map/ppermute | solution.py:51
  94.6 22.3 %collective-permute-start.9 = (f32[4,2,64,128]{3,2,1,0:T(8,128)S(1)}, f32[4,2,64,128]{3,2,1,0:T(8,128)S(1)}, u32[]{:S(2)}, u32[]{:S(2)}) collective-permute-start(f32[4,2,64,128]{3,2,1,0:T(8,128)S(1)} %get-tuple-element.28), channel_id=1, source_target_pairs={{2,4},{4,2},{3,5},{5,3},{10,12},{12,10},{11,13},{13,11},{18,20},{2... | collective-permute-start | bytes 786440 | tf_op jit(solution)/shard_map/ppermute | solution.py:51
  140.5 4.6 %collective-permute-start.10 = (f32[4,2,64,128]{3,2,1,0:T(8,128)S(1)}, f32[4,2,64,128]{3,2,1,0:T(8,128)S(1)}, u32[]{:S(2)}, u32[]{:S(2)}) collective-permute-start(f32[4,2,64,128]{3,2,1,0:T(8,128)S(1)} %pack_z.5.own), channel_id=1, source_target_pairs={{0,1},{1,0},{2,3},{3,2},{4,5},{5,4},{6,7},{7,6},{8,9},{9,8},{10,11... | collective-permute-start | bytes 786440 | tf_op jit(solution)/shard_map/ppermute | solution.py:51
  140.5 26.2 %collective-permute-start.11 = (f32[4,2,64,128]{3,2,1,0:T(8,128)S(1)}, f32[4,2,64,128]{3,2,1,0:T(8,128)S(1)}, u32[]{:S(2)}, u32[]{:S(2)}) collective-permute-start(f32[4,2,64,128]{3,2,1,0:T(8,128)S(1)} %get-tuple-element.30), channel_id=1, source_target_pairs={{0,8},{8,0},{16,24},{24,16},{1,9},{9,1},{17,25},{25,17},{2,10},{10... | collective-permute-start | bytes 786440 | tf_op jit(solution)/shard_map/ppermute | solution.py:51
  142.3 24.5 %collective-permute-start.12 = (f32[4,2,64,128]{3,2,1,0:T(8,128)S(1)}, f32[4,2,64,128]{3,2,1,0:T(8,128)S(1)}, u32[]{:S(2)}, u32[]{:S(2)}) collective-permute-start(f32[4,2,64,128]{3,2,1,0:T(8,128)S(1)} %get-tuple-element.31), channel_id=1, source_target_pairs={{8,16},{16,8},{9,17},{17,9},{10,18},{18,10},{11,19},{19,11},{12,20... | collective-permute-start | bytes 786440 | tf_op jit(solution)/shard_map/ppermute | solution.py:51
  143.0 23.8 %collective-permute-start.13 = (f32[4,2,64,128]{3,2,1,0:T(8,128)S(1)}, f32[4,2,64,128]{3,2,1,0:T(8,128)S(1)}, u32[]{:S(2)}, u32[]{:S(2)}) collective-permute-start(f32[4,2,64,128]{3,2,1,0:T(8,128)S(1)} %get-tuple-element.32), channel_id=1, source_target_pairs={{0,2},{2,0},{4,6},{6,4},{1,3},{3,1},{5,7},{7,5},{8,10},{10,8},{12,... | collective-permute-start | bytes 786440 | tf_op jit(solution)/shard_map/ppermute | solution.py:51
  144.5 22.3 %collective-permute-start.14 = (f32[4,2,64,128]{3,2,1,0:T(8,128)S(1)}, f32[4,2,64,128]{3,2,1,0:T(8,128)S(1)}, u32[]{:S(2)}, u32[]{:S(2)}) collective-permute-start(f32[4,2,64,128]{3,2,1,0:T(8,128)S(1)} %get-tuple-element.33), channel_id=1, source_target_pairs={{2,4},{4,2},{3,5},{5,3},{10,12},{12,10},{11,13},{13,11},{18,20},{2... | collective-permute-start | bytes 786440 | tf_op jit(solution)/shard_map/ppermute | solution.py:51
  168.9 1.2 collective-permute-start.15
  170.1 5.3 %collective-permute-start.18 = (f32[16,128]{1,0:T(8,128)S(1)}, f32[16,128]{1,0:T(8,128)S(1)}, u32[]{:S(2)}, u32[]{:S(2)}) collective-permute-start(f32[16,128]{1,0:T(8,128)S(1)} %add.12), channel_id=1, source_target_pairs={{0,6},{2,0},{4,2},{6,4},{1,7},{3,1},{5,3},{7,5},{8,14},{10,8},{12,... | collective-permute-start | bytes 24584 | tf_op jit(solution)/shard_map/ppermute | solution.py:516
  172.9 4.5 %collective-permute-start.17 = (f32[16,128]{1,0:T(8,128)S(1)}, f32[16,128]{1,0:T(8,128)S(1)}, u32[]{:S(2)}, u32[]{:S(2)}) collective-permute-start(f32[16,128]{1,0:T(8,128)S(1)} %add.12), channel_id=1, source_target_pairs={{0,4},{2,6},{4,0},{6,2},{1,5},{3,7},{5,1},{7,3},{8,12},{10,14},{12... | collective-permute-start | bytes 24584 | tf_op jit(solution)/shard_map/ppermute | solution.py:516
  174.7 5.4 %collective-permute-start.16 = (f32[16,128]{1,0:T(8,128)S(1)}, f32[16,128]{1,0:T(8,128)S(1)}, u32[]{:S(2)}, u32[]{:S(2)}) collective-permute-start(f32[16,128]{1,0:T(8,128)S(1)} %add.12), channel_id=1, source_target_pairs={{0,2},{2,4},{4,6},{6,0},{1,3},{3,5},{5,7},{7,1},{8,10},{10,12},{12... | collective-permute-start | bytes 24584 | tf_op jit(solution)/shard_map/ppermute | solution.py:516
  180.1 5.3 %collective-permute-start.21 = (f32[16,128]{1,0:T(8,128)S(1)}, f32[16,128]{1,0:T(8,128)S(1)}, u32[]{:S(2)}, u32[]{:S(2)}) collective-permute-start(f32[16,128]{1,0:T(8,128)S(1)} %add_add_fusion.rest_0_), channel_id=1, source_target_pairs={{0,24},{8,0},{16,8},{24,16},{1,25},{9,1},{17,9},{25,17},{2,26},{10... | collective-permute-start | bytes 24584 | tf_op jit(solution)/shard_map/ppermute | solution.py:516
  182.6 4.3 %collective-permute-start.20 = (f32[16,128]{1,0:T(8,128)S(1)}, f32[16,128]{1,0:T(8,128)S(1)}, u32[]{:S(2)}, u32[]{:S(2)}) collective-permute-start(f32[16,128]{1,0:T(8,128)S(1)} %add_add_fusion.rest_0_), channel_id=1, source_target_pairs={{0,16},{8,24},{16,0},{24,8},{1,17},{9,25},{17,1},{25,9},{2,18},{10... | collective-permute-start | bytes 24584 | tf_op jit(solution)/shard_map/ppermute | solution.py:516
  185.3 4.5 %collective-permute-start.19 = (f32[16,128]{1,0:T(8,128)S(1)}, f32[16,128]{1,0:T(8,128)S(1)}, u32[]{:S(2)}, u32[]{:S(2)}) collective-permute-start(f32[16,128]{1,0:T(8,128)S(1)} %add_add_fusion.rest_0_), channel_id=1, source_target_pairs={{0,8},{8,16},{16,24},{24,0},{1,9},{9,17},{17,25},{25,1},{2,10},{10... | collective-permute-start | bytes 24584 | tf_op jit(solution)/shard_map/ppermute | solution.py:516

commit v2 on v1

v2 whole, which is shorter than its diff:
```python
import functools

import jax
import jax.numpy as jnp
from jax import lax
from jax.experimental import pallas as pl
from jax.experimental.pallas import tpu as pltpu
from jax.sharding import PartitionSpec as P

CENTRE = 4.5
HALF_WIDTH = 3.5
SCALE = 2.0 / HALF_WIDTH
EDGE = SCALE / 24.0
LANES = 128
TILE = 8
PAD = 8
PER = LANES // 4
VMEM_LIMIT = 8 * 1024 * 1024


def vmem_out(shape):
    return pltpu.VMEM(shape, jnp.float32)


def in_vmem(array):
    return pltpu.with_memory_space_constraint(array, pltpu.VMEM)


WHOLE = pl.BlockSpec(memory_space=pltpu.VMEM)
ANYWHERE = pl.BlockSpec(memory_space=pl.ANY)


def params():
    return pltpu.CompilerParams(vmem_limit_bytes=VMEM_LIMIT)


LITTLE = pl.CostEstimate(flops=1, bytes_accessed=1, transcendentals=0)


def pairing(axis, parity):
    pairs = []
    for low in range(parity, lax.axis_size(axis) - 1, 2):
        pairs += [(low, low + 1), (low + 1, low)]
    return pairs


def swap(array, axis, parity):
    pairs = pairing(axis, parity)
    if not pairs:
        return jnp.zeros_like(array)
    return lax.ppermute(array, axis, pairs)


def is_odd(axis):
    return lax.rem(lax.axis_index(axis), 2) == 1


def faces_x_kernel(field, even, odd, sems):
    count = field.shape[1]
    low = field.at[:, pl.ds(0, 2)]
    high = field.at[:, pl.ds(count - 2, 2)]
    flip = is_odd("gx")

    def move(first, second):
        one = pltpu.make_async_copy(first, even, sems.at[0])
        two = pltpu.make_async_copy(second, odd, sems.at[1])
        one.start()
        two.start()
        one.wait()
        two.wait()

    @pl.when(flip)
    def _():
        move(low, high)

    @pl.when(jnp.logical_not(flip))
    def _():
        move(high, low)


def faces_x(orbitals):
    orbs, _, ny, nz = orbitals.shape
    shape = vmem_out((orbs, 2, ny, nz))
    return pl.pallas_call(
        faces_x_kernel,
        out_shape=(shape, shape),
        in_specs=[ANYWHERE],
        out_specs=(WHOLE, WHOLE),
        scratch_shapes=[pltpu.SemaphoreType.DMA((2,))],
        compiler_params=params(),
        cost_estimate=LITTLE,
        name="faces_x",
    )(orbitals)


def pack_y_group(rows, even, odd, orb, group, flip):
    place = pl.ds(group * TILE, TILE)
    for layer in range(2):
        low, high = rows[layer], rows[2 + layer]
        even[orb, layer, place, :] = jnp.where(flip, low, high)
        odd[orb, layer, place, :] = jnp.where(flip, high, low)


def pack_z_lanes(rows, plane, total):
    lane = lax.broadcasted_iota(jnp.int32, rows.shape, 1)
    moved = pltpu.roll(rows, (4 * plane + 2) % LANES, 1)
    return moved if total is None else jnp.where(lane // 4 == plane, moved, total)


def pack_z_tiles(flat, packed, pitch, orb, group, tiles):
    totals = [None] * len(tiles)
    for plane in range(PER):
        for number, tile in enumerate(tiles):
            start = pl.multiple_of((group * PER + plane + 2) * pitch + tile * TILE, TILE)
            rows = flat[orb, pl.ds(start, TILE), :]
            totals[number] = pack_z_lanes(rows, plane, totals[number])
    for number, tile in enumerate(tiles):
        packed[orb, group, pl.ds(tile * TILE, TILE), :] = totals[number]


def load_kernel(nx, ny, field, potential, out, weight, even, odd, packed, sems):
    orbs = field.shape[0]
    pitch = ny + PAD
    flat = out.reshape(orbs, (nx + 4) * pitch, LANES)
    copies = []
    for orb in range(orbs):
        copy = pltpu.make_async_copy(
            field.at[orb], out.at[orb, pl.ds(2, nx), pl.ds(0, ny)], sems.at[orb]
        )
        copy.start()
        copies.append(copy)
    last = pltpu.make_async_copy(potential, weight, sems.at[orbs])
    last.start()
    flip = is_odd("gy")
    zero_planes = jnp.zeros((2 * pitch, LANES), jnp.float32)
    zero_rows = jnp.zeros((PAD, LANES), jnp.float32)
    for orb in range(orbs):
        flat[orb, pl.ds(0, 2 * pitch), :] = zero_planes
        flat[orb, pl.ds((nx + 2) * pitch, 2 * pitch), :] = zero_planes

        @pl.loop(0, nx, unroll=8)
        def _(x):
            flat[orb, pl.ds(pl.multiple_of((x + 2) * pitch + ny, TILE), PAD), :] = zero_rows

    for orb in range(orbs):
        copies[orb].wait()

        @pl.loop(0, nx // TILE, unroll=2)
        def _(group):
            start = (group * TILE + 2) * pitch
            rows = [
                flat[orb, pl.ds(start + y, TILE, stride=pitch), :] for y in (0, 1, ny - 2, ny - 1)
            ]
            pack_y_group(rows, even, odd, orb, group, flip)

        @pl.loop(0, nx // PER)
        def _(group):
            pack_z_tiles(flat, packed, pitch, orb, group, range(ny // TILE))

    last.wait()

    @pl.loop(0, nx, unroll=2)
    def _(x):
        weight[x] = SCALE * weight[x] + SCALE * (0.5 * 7.5 - CENTRE)


def load(orbitals, potential):
    orbs, nx, ny, nz = orbitals.shape
    face = vmem_out((orbs, 2, nx, nz))
    return pl.pallas_call(
        functools.partial(load_kernel, nx, ny),
        out_shape=(
            vmem_out((orbs, nx + 4, ny + PAD, nz)),
            vmem_out((nx, ny, nz)),
            face,
            face,
            vmem_out((orbs, nx // PER, ny, nz)),
        ),
        in_specs=[ANYWHERE, ANYWHERE],
        out_specs=(WHOLE,) * 5,
        scratch_shapes=[pltpu.SemaphoreType.DMA((orbs + 1,))],
        compiler_params=params(),
        cost_estimate=LITTLE,
        name="load",
    )(orbitals, potential)


def step_kernel(nx, ny, first, last, field, weight, z_even, z_odd, *rest):
    rest = rest if first else rest[1:]
    out, packed = rest[0], None if last else rest[1]
    correction, mix = rest[-2:]
    orbs = field.shape[0]
    pitch = ny + PAD
    flat = field.reshape(orbs, (nx + 4) * pitch, LANES)
    flat_out = out.reshape(orbs, (nx + 4) * pitch, LANES)
    edge = EDGE * (0.5 if first else 1.0)
    groups = nx // PER
    tiles = ny // TILE
    flip = is_odd("gz")
    place = lax.broadcasted_iota(jnp.int32, (ny, LANES), 1) % 4
    lane = lax.broadcasted_iota(jnp.int32, (TILE, LANES), 1)
    ends = (lane < 2) | (lane >= LANES - 2)

    if first:
        zero_planes = jnp.zeros((2 * pitch, LANES), jnp.float32)
        zero_rows = jnp.zeros((PAD, LANES), jnp.float32)
        for orb in range(orbs):
            flat_out[orb, pl.ds(0, 2 * pitch), :] = zero_planes
            flat_out[orb, pl.ds((nx + 2) * pitch, 2 * pitch), :] = zero_planes

            @pl.loop(0, nx, unroll=8)
            def _(x):
                there = pl.ds(pl.multiple_of((x + 2) * pitch + ny, TILE), PAD)
                flat_out[orb, there, :] = zero_rows

    line = lax.broadcasted_iota(jnp.int32, (LANES, LANES), 0)
    column = lax.broadcasted_iota(jnp.int32, (LANES, LANES), 1)
    apart = jnp.abs(line - column)
    weights = jnp.where(apart == 1, -16.0, jnp.where(apart == 2, 1.0, 0.0)).astype(jnp.bfloat16)
    mix[pl.ds(0, LANES), :] = weights
    mix[pl.ds(LANES, LANES), :] = weights

    for orb in range(orbs):
        for group in range(groups):
            even, odd = z_even[orb, group], z_odd[orb, group]
            below = jnp.where(flip, even, odd)
            above = jnp.where(flip, odd, even)
            beyond = jnp.where(place < 2, below, above)
            left = pltpu.roll(beyond, LANES - 2, 1) - 16.0 * jnp.where(
                place == 1, pltpu.roll(beyond, LANES - 1, 1), 0.0
            )
            right = pltpu.roll(beyond, 2, 1) - 16.0 * jnp.where(
                place == 2, pltpu.roll(beyond, 1, 1), 0.0
            )
            correction[orb, group] = jnp.where(place < 2, left, right)

    def locate(index, tile):
        orb, group = index // groups, lax.rem(index, groups)
        return orb, group, (group * PER + 2) * pitch + tile * TILE

    def along_z(index, tile):
        orb, group, base = locate(index, tile)
        rows = [
            flat[orb, pl.ds(pl.multiple_of(base + plane * pitch, TILE), TILE), :]
            for plane in range(PER)
        ]
        stacked = jnp.concatenate(rows, axis=0)
        high = stacked.astype(jnp.bfloat16)
        low = (stacked - high.astype(jnp.float32)).astype(jnp.bfloat16)
        product = jnp.dot(
            jnp.concatenate([high, low], axis=1), mix[...], preferred_element_type=jnp.float32
        )
        fix = correction[orb, group, pl.ds(tile * TILE, TILE), :]
        sums = []
        for plane in range(PER):
            moved = pltpu.roll(fix, LANES - 4 * plane - 2, 1)
            sums.append(
                product[plane * TILE : (plane + 1) * TILE] + jnp.where(ends, moved, 0.0)
            )
        return tuple(sums)

    def block(index, sums):
        for tile in range(tiles):
            if tile + 1 < tiles:
                later = along_z(index, tile + 1)
            else:
                later = along_z(jnp.minimum(index + 1, orbs * groups - 1), 0)
            finish(index, tile, sums)
            sums = later
        return sums

    def finish(index, tile, sums):
        orb, group, base = locate(index, tile)

        def rows(plane, shift=0):
            start = base + plane * pitch + shift
            if shift == 0:
                start = pl.multiple_of(start, TILE)
            return flat[orb, pl.ds(start, TILE), :]

        mine = [rows(plane) for plane in range(-2, PER + 2)]
        values = []
        total = None
        for plane in range(PER):
            near = (mine[plane + 1] + mine[plane + 3]) + (rows(plane, -1) + rows(plane, 1))
            far = (mine[plane] + mine[plane + 4]) + (rows(plane, -2) + rows(plane, 2))
            ours = weight[group * PER + plane, pl.ds(tile * TILE, TILE), :]
            if first:
                ours = 0.5 * ours
            value = ours * mine[plane + 2] + edge * ((far - 16.0 * near) + sums[plane])
            if not first:
                start = pl.multiple_of(base + plane * pitch, TILE)
                value = value - flat_out[orb, pl.ds(start, TILE), :]
            if not last:
                total = pack_z_lanes(value, plane, total)
            values.append(value)
        for plane in range(PER):
            start = pl.multiple_of(base + plane * pitch, TILE)
            flat_out[orb, pl.ds(start, TILE), :] = values[plane]
        if not last:
            packed[orb, group, pl.ds(tile * TILE, TILE), :] = total

    lax.fori_loop(0, orbs * groups, block, along_z(0, 0))


def step(field, weight, z_even, z_odd, before, last):
    orbs = field.shape[0]
    nx, ny, nz = weight.shape
    first = before is None
    args = [field, weight, z_even, z_odd] + ([] if first else [before])
    shapes = [vmem_out(field.shape)] + ([] if last else [vmem_out(z_even.shape)])
    return pl.pallas_call(
        functools.partial(step_kernel, nx, ny, first, last),
        out_shape=tuple(shapes),
        in_specs=[WHOLE] * len(args),
        out_specs=(WHOLE,) * len(shapes),
        scratch_shapes=[
            pltpu.VMEM((orbs, nx // PER, ny, nz), jnp.float32),
            pltpu.VMEM((2 * nz, nz), jnp.bfloat16),
        ],
        input_output_aliases={} if first else {4: 0},
        compiler_params=params(),
        cost_estimate=LITTLE,
        name="step",
    )(*[in_vmem(arg) for arg in args])


def edges_kernel(nx, ny, edge, last, field, x_even, x_odd, y_even, y_odd, *rest):
    orbs = field.shape[0]
    pitch = ny + PAD
    if last:
        (out,) = rest
    else:
        _, out, next_x_even, next_x_odd, next_y_even, next_y_odd, packed = rest
    flat = out.reshape(orbs, (nx + 4) * pitch, LANES)
    flip_x, flip_y = is_odd("gx"), is_odd("gy")

    def plane_rows(x):
        return pl.ds((x + 2) * pitch, ny)

    @pl.loop(0, orbs)
    def _(orb):
        def halves(layer):
            even, odd = x_even[orb, layer], x_odd[orb, layer]
            return jnp.where(flip_x, even, odd), jnp.where(flip_x, odd, even)

        low_far, high_near = halves(0)
        low_near, high_far = halves(1)
        flat[orb, plane_rows(0), :] += edge * (low_far - 16.0 * low_near)
        flat[orb, plane_rows(1), :] += edge * low_near
        flat[orb, plane_rows(nx - 2), :] += edge * high_near
        flat[orb, plane_rows(nx - 1), :] += edge * (high_far - 16.0 * high_near)

        @pl.loop(0, nx // TILE, unroll=2)
        def _(group):
            place = pl.ds(group * TILE, TILE)

            def pick(layer):
                even, odd = y_even[orb, layer, place, :], y_odd[orb, layer, place, :]
                return jnp.where(flip_y, even, odd), jnp.where(flip_y, odd, even)

            low_far, high_near = pick(0)
            low_near, high_far = pick(1)
            adds = (
                edge * (low_far - 16.0 * low_near),
                edge * low_near,
                edge * high_near,
                edge * (high_far - 16.0 * high_near),
            )
            start = (group * TILE + 2) * pitch
            rows = []
            for y, add in zip((0, 1, ny - 2, ny - 1), adds):
                there = pl.ds(start + y, TILE, stride=pitch)
                value = flat[orb, there, :] + add
                flat[orb, there, :] = value
                rows.append(value)
            if not last:
                pack_y_group(rows, next_y_even, next_y_odd, orb, group, flip_y)

        if not last:
            for layer in range(2):
                low = flat[orb, plane_rows(layer), :]
                high = flat[orb, plane_rows(nx - 2 + layer), :]
                next_x_even[orb, layer] = jnp.where(flip_x, low, high)
                next_x_odd[orb, layer] = jnp.where(flip_x, high, low)

            tiles = ny // TILE
            for group in range(nx // PER):
                pack_z_tiles(flat, packed, pitch, orb, group, (0, tiles - 1))
            for x in (0, 1, nx - 2, nx - 1):
                group, plane = x // PER, x % PER
                there = pl.ds(TILE, ny - 2 * TILE)
                rows = flat[orb, pl.ds((x + 2) * pitch + TILE, ny - 2 * TILE), :]
                packed[orb, group, there, :] = pack_z_lanes(
                    rows, plane, packed[orb, group, there, :]
                )


def edges(field, packed, nx, ny, halos, edge, last):
    orbs, nz = field.shape[0], field.shape[-1]
    args = [field, *halos] + ([] if last else [packed])
    shapes = [vmem_out(field.shape)]
    if not last:
        shapes += [vmem_out((orbs, 2, ny, nz))] * 2 + [vmem_out((orbs, 2, nx, nz))] * 2
        shapes += [vmem_out(packed.shape)]
    return pl.pallas_call(
        functools.partial(edges_kernel, nx, ny, edge, last),
        out_shape=tuple(shapes),
        in_specs=[WHOLE] * len(args),
        out_specs=(WHOLE,) * len(shapes),
        input_output_aliases={0: 0} if last else {0: 0, 5: 5},
        compiler_params=params(),
        cost_estimate=LITTLE,
        name="edges",
    )(*[in_vmem(arg) for arg in args])


def pair_list(orbs):
    return [(line, column) for line in range(orbs) for column in range(line, orbs)]


def gram_kernel(nx, ny, field, out):
    orbs = field.shape[0]
    pitch = ny + PAD
    flat = field.reshape(orbs, (nx + 4) * pitch, LANES)
    pairs = pair_list(orbs)

    def plane(x, totals):
        totals = list(totals)
        for tile in range(ny // TILE):
            start = pl.multiple_of((x + 2) * pitch + tile * TILE, TILE)
            rows = [flat[orb, pl.ds(start, TILE), :] for orb in range(orbs)]
            for index, (line, column) in enumerate(pairs):
                totals[index] = totals[index] + rows[line] * rows[column]
        return tuple(totals)

    zero = jnp.zeros((TILE, LANES), jnp.float32)
    totals = lax.fori_loop(0, nx, plane, (zero,) * len(pairs))
    out[...] = jnp.zeros_like(out)
    for index, total in enumerate(totals):
        out[pl.ds(index, 1), :] = jnp.sum(total, axis=0, keepdims=True)


def gram(field, nx, ny):
    orbs = field.shape[0]
    rows = -(-len(pair_list(orbs)) // TILE) * TILE
    return pl.pallas_call(
        functools.partial(gram_kernel, nx, ny),
        out_shape=jax.ShapeDtypeStruct((rows, LANES), jnp.float32),
        in_specs=[WHOLE],
        out_specs=WHOLE,
        compiler_params=params(),
        cost_estimate=LITTLE,
        name="gram",
    )(in_vmem(field))


def basis_kernel(nx, ny, chunk, cells, parts, field, *rest):
    sums, (out, factor, held, sems) = rest[:parts], rest[parts:]
    orbs = field.shape[0]
    pitch = ny + PAD
    flat = field.reshape(orbs, (nx + 4) * pitch, LANES)
    pairs = pair_list(orbs)

    total = sums[0][...]
    for part in sums[1:]:
        total = total + part[...]
    total = jnp.broadcast_to(jnp.sum(total, axis=1, keepdims=True), total.shape) / cells
    entry = {}
    for index, pair in enumerate(pairs):
        entry[pair] = total[index : index + 1, :]
    upper, inv = {}, {}
    for line in range(orbs):
        for column in range(line, orbs):
            value = entry[line, column]
            for inner in range(line):
                value = value - upper[inner, line] * upper[inner, column]
            if column == line:
                upper[line, line] = jnp.sqrt(value)
                inv[line, line] = 1.0 / upper[line, line]
            else:
                upper[line, column] = value * inv[line, line]
    for column in range(orbs):
        for line in range(column - 1, -1, -1):
            value = upper[line, line + 1] * inv[line + 1, column]
            for inner in range(line + 2, column + 1):
                value = value + upper[line, inner] * inv[inner, column]
            inv[line, column] = -value * inv[line, line]
    row = lax.broadcasted_iota(jnp.int32, (TILE, LANES), 0)
    col = lax.broadcasted_iota(jnp.int32, (TILE, LANES), 1)
    whole = jnp.zeros((TILE, LANES), jnp.float32)
    for (line, column), value in upper.items():
        there = (row == line) & (col == column)
        whole = jnp.where(there, jnp.broadcast_to(value, whole.shape), whole)
    factor[...] = whole[:orbs, :orbs]
    gains = {pair: jnp.broadcast_to(inv[pair], (TILE, LANES)) for pair in pairs}

    half = ny // TILE // 2
    pieces = [(plane, part) for plane in range(chunk) for part in (0, half)]

    def copy(index):
        place = pl.ds(index * chunk, chunk)
        return pltpu.make_async_copy(held.at[:, place], out.at[:, place], sems.at[index])

    @pl.loop(0, nx // chunk)
    def _(index):
        first = index * chunk

        def fetch(plane, part):
            rows = []
            for tile in range(part, part + half):
                start = pl.multiple_of((first + plane + 2) * pitch + tile * TILE, TILE)
                rows.append([flat[orb, pl.ds(start, TILE), :] for orb in range(orbs)])
            return rows

        rows = fetch(*pieces[0])
        for number, (plane, part) in enumerate(pieces):
            later = fetch(*pieces[number + 1]) if number + 1 < len(pieces) else None
            values = []
            for tile in range(half):
                for column in range(orbs):
                    value = rows[tile][0] * gains[0, column]
                    for line in range(1, column + 1):
                        value = value + rows[tile][line] * gains[line, column]
                    values.append(value)
            for tile in range(half):
                for column in range(orbs):
                    there = pl.ds((part + tile) * TILE, TILE)
                    held[column, first + plane, there, :] = values[tile * orbs + column]
            rows = later
        copy(index).start()

    @pl.loop(0, nx // chunk)
    def _(index):
        copy(index).wait()


def basis(field, nx, ny, sums, cells):
    orbs, nz = field.shape[0], field.shape[-1]
    chunk = 4
    return pl.pallas_call(
        functools.partial(basis_kernel, nx, ny, chunk, cells, len(sums)),
        out_shape=(
            jax.ShapeDtypeStruct((orbs, nx, ny, nz), jnp.float32),
            jax.ShapeDtypeStruct((orbs, orbs), jnp.float32),
        ),
        in_specs=[WHOLE] * (1 + len(sums)),
        out_specs=(pl.BlockSpec(memory_space=pltpu.HBM), WHOLE),
        scratch_shapes=[
            pltpu.VMEM((orbs, nx, ny, nz), jnp.float32),
            pltpu.SemaphoreType.DMA((nx // chunk,)),
        ],
        compiler_params=pltpu.CompilerParams(vmem_limit_bytes=VMEM_LIMIT + 4 * orbs * nx * ny * nz),
        cost_estimate=LITTLE,
        name="basis",
    )(in_vmem(field), *sums)


def exchanges(array, axis):
    count = lax.axis_size(axis)
    if count & (count - 1):
        moves = [[(i, (i + by) % count) for i in range(count)] for by in range(1, count)]
    else:
        moves = [[(i, i ^ by) for i in range(count)] for by in range(1, count)]
    return [lax.ppermute(array, axis, move) for move in moves]


def body(orbitals, potential):
    _, nx, ny, _ = orbitals.shape
    cells = (
        nx
        * lax.axis_size("gx")
        * (ny * lax.axis_size("gy"))
        * (orbitals.shape[3] * lax.axis_size("gz"))
    )
    orbitals = pltpu.with_memory_space_constraint(orbitals, pltpu.HBM)
    potential = pltpu.with_memory_space_constraint(potential, pltpu.HBM)
    x_faces = faces_x(orbitals)
    x_faces, orbitals = lax.optimization_barrier((x_faces, orbitals))
    field, weight, *y_faces, packed = load(orbitals, potential)
    before = None
    for level in range(3):
        last = level == 2
        halo_x = [swap(face, "gx", parity) for parity, face in enumerate(x_faces)]
        halo_y = [swap(face, "gy", parity) for parity, face in enumerate(y_faces)]
        z_even, z_odd = swap(packed, "gz", 0), swap(packed, "gz", 1)
        after, *packed = step(field, weight, z_even, z_odd, before, last)
        packed = None if last else packed[0]
        edge = EDGE * (0.5 if level == 0 else 1.0)
        after, *faces = edges(after, packed, nx, ny, (*halo_x, *halo_y), edge, last)
        if not last:
            x_faces, y_faces, packed = faces[:2], faces[2:4], faces[4]
        before, field = field, after
    local = gram(field, nx, ny)
    for axis in ("gz", "gy"):
        for part in exchanges(local, axis):
            local = local + part
    return basis(field, nx, ny, [local, *exchanges(local, "gx")], cells)


def solution(mesh):
    return jax.shard_map(
        body,
        mesh=mesh,
        in_specs=(P(None, "gx", "gy", "gz"), P("gx", "gy", "gz")),
        out_specs=(P(None, "gx", "gy", "gz"), P()),
        check_vma=False,
    )
```

time: 198 us -> 78 us (0.39)
  Pallas kernels: 150 us -> 37.3 us
  local copies, waits for them, and re-layouts: 4.98 us -> 0.02 us
  waiting for transfers between devices: 10.4 us -> 8.23 us
    pallas_call x6 -> x3, Pallas kernels: 137 us -> 22.5 us  [step(): pl.pallas_call(functools.partial(step_kernel, nx, ny, first, last), out_s...]
    unnamed x4 -> x0, local copies, waits for them, and re-layouts: 4.97 us -> none
    pallas_call x1, Pallas kernels: 7.44 us -> 4.23 us  [basis(): pl.pallas_call(functools.partial(basis_kernel, nx, ny, chunk, cells, len(...]
    pallas_call x1, Pallas kernels: 1.96 us -> 4.96 us  [load(): pl.pallas_call(functools.partial(load_kernel, nx, ny), out_shape=(vmem_ou...]
    ppermute x7, waiting for transfers between devices: 10.4 us -> 8.19 us  [exchanges(): return [lax.ppermute(array, axis, move) for move in moves]]
  transfers between devices with their start and end apart: 22 -> 22, of which waited for: 6 -> 6; matrix products, arithmetic and copies ran while one was open for 0% -> 0% of each run, Pallas kernels for 34% -> 29%
where the time goes in v2:
time: 78 us; the launch traced here: 77.7 us
  Pallas kernels  37.3 us (48%)
  starting transfers between devices  31.3 us (40%)
  waiting for transfers between devices  8.23 us (11%)
  between operations  0.91 us (1%)
    pallas_call x3, Pallas kernels, step(): pl.pallas_call(functools.partial(step_kernel, nx, ny, first, last), out_s...  22.5 us
    ppermute x15, starting transfers between devices, swap(): return lax.ppermute(array, axis, pairs)  21.4 us
    ppermute x7, starting transfers between devices, exchanges(): return [lax.ppermute(array, axis, move) for move in moves]  9.87 us
    ppermute x7, waiting for transfers between devices, exchanges(): return [lax.ppermute(array, axis, move) for move in moves]  8.19 us
    pallas_call x1, Pallas kernels, load(): pl.pallas_call(functools.partial(load_kernel, nx, ny), out_shape=(vmem_ou...  4.96 us
    pallas_call x1, Pallas kernels, basis(): pl.pallas_call(functools.partial(basis_kernel, nx, ny, chunk, cells, len(...  4.23 us
    pallas_call x3, Pallas kernels, edges(): pl.pallas_call(functools.partial(edges_kernel, nx, ny, edge, last), out_s...  2.94 us
    pallas_call x1, Pallas kernels, gram(): pl.pallas_call(functools.partial(gram_kernel, nx, ny), out_shape=jax.Shap...  1.63 us
  transfers between devices with their start and end apart: 22, of which 6 were waited for; matrix products, arithmetic and copies ran while one was open for 0% of the time, Pallas kernels for 29%

profile of v2, /device:TPU:0, one launch (start us, length us, event | category | flops | bytes accessed | tf_op | source)
XLA Modules:
  0.0 77.7 jit_solution(1243687970430631558)
XLA Ops:
  0.6 1.1 %faces_x.1 = (f32[4,2,64,128]{3,2,1,0:T(8,128)S(1)}, f32[4,2,64,128]{3,2,1,0:T(8,128)S(1)}) custom-call(f32[4,64,64,128]{3,2,1,0:T(8,128)} %field.2), custom_call_target="tpu_custom_call" | custom-call | flops 1 | bytes 1 | tf_op jit(solution)/shard_map/faces_x/pallas_call | solution.py:84
  1.7 5.0 %load.1 = (f32[4,68,72,128]{3,2,1,0:T(8,128)S(1)}, f32[64,64,128]{2,1,0:T(8,128)S(1)}, f32[4,2,64,128]{3,2,1,0:T(8,128)S(1)}, f32[4,2,64,128]{3,2,1,0:T(8,128)S(1)}, f32[4,2,64,128]{3,2,1,0:T(8,128)S(1)}) custom-call(f32[4,64,64,128]{3,2,1,0:T(8,128)} %field.2, f32[64,64,128]{2,1,0:T(8,128)} %potential.1), custom_call_target="tpu_custom_call" | custom-call | flops 1 | bytes 1 | tf_op jit(solution)/shard_map/load/pallas_call | solution.py:170
  6.7 0.5 collective-permute-start
  7.2 2.6 %collective-permute-start.1 = (f32[4,2,64,128]{3,2,1,0:T(8,128)S(1)}, f32[4,2,64,128]{3,2,1,0:T(8,128)S(1)}, u32[]{:S(2)}, u32[]{:S(2)}) collective-permute-start(f32[4,2,64,128]{3,2,1,0:T(8,128)S(1)} %get-tuple-element.35), channel_id=1, source_target_pairs={{0,8},{8,0},{16,24},{24,16},{1,9},{9,1},{17,25},{25,17},{2,10},{10... | collective-permute-start | bytes 786440 | tf_op jit(solution)/shard_map/ppermute | solution.py:51
  9.8 0.7 collective-permute-start.2
  10.4 1.6 %collective-permute-start.3 = (f32[4,2,64,128]{3,2,1,0:T(8,128)S(1)}, f32[4,2,64,128]{3,2,1,0:T(8,128)S(1)}, u32[]{:S(2)}, u32[]{:S(2)}) collective-permute-start(f32[4,2,64,128]{3,2,1,0:T(8,128)S(1)} %get-tuple-element.37), channel_id=1, source_target_pairs={{0,2},{2,0},{4,6},{6,4},{1,3},{3,1},{5,7},{7,5},{8,10},{10,8},{12,... | collective-permute-start | bytes 786440 | tf_op jit(solution)/shard_map/ppermute | solution.py:51
  12.1 0.7 collective-permute-start.4
  12.8 7.8 %step.3 = (f32[4,68,72,128]{3,2,1,0:T(8,128)S(1)}, f32[4,2,64,128]{3,2,1,0:T(8,128)S(1)}) custom-call(f32[4,68,72,128]{3,2,1,0:T(8,128)S(1)} %get-tuple-element.31.field.rest_0_, f32[64,64,128]{2,1,0:T(8,128)S(1)} %get-tuple-element.32.weight, f32[4,2,64,128]{3,2,1,0:T(8,128)S(1)} %collective-permute-done.z_even, f32[4,2,64,128]{3,2,1,0:T(8,128)S(1)} %broadcast_1_z_odd.2.z_odd), custom_call_target="tpu_custom_call" | custom-call | flops 1 | bytes 1 | tf_op jit(solution)/shard_map/step/pallas_call | solution.py:312
  20.6 1.3 %edges.3 = (f32[4,68,72,128]{3,2,1,0:T(8,128)S(1)}, f32[4,2,64,128]{3,2,1,0:T(8,128)S(1)}, f32[4,2,64,128]{3,2,1,0:T(8,128)S(1)}, f32[4,2,64,128]{3,2,1,0:T(8,12...) custom-call(f32[4,68,72,128]{3,2,1,0:T(8,128)S(1)} %get-tuple-elemen, ...), custom_call_target="tpu_custom_call", output_to_operand_aliasing={{0}: (0, {}), {5}: (5, {})} | custom-call | flops 1 | bytes 1 | tf_op jit(solution)/shard_map/edges/pallas_call | solution.py:406
  22.0 4.4 %collective-permute-start.6 = (f32[4,2,64,128]{3,2,1,0:T(8,128)S(1)}, f32[4,2,64,128]{3,2,1,0:T(8,128)S(1)}, u32[]{:S(2)}, u32[]{:S(2)}) collective-permute-start(f32[4,2,64,128]{3,2,1,0:T(8,128)S(1)} %get-tuple-element.43), channel_id=1, source_target_pairs={{0,8},{8,0},{16,24},{24,16},{1,9},{9,1},{17,25},{25,17},{2,10},{10... | collective-permute-start | bytes 786440 | tf_op jit(solution)/shard_map/ppermute | solution.py:51
  26.4 0.7 collective-permute-start.7
  27.1 4.3 %collective-permute-start.8 = (f32[4,2,64,128]{3,2,1,0:T(8,128)S(1)}, f32[4,2,64,128]{3,2,1,0:T(8,128)S(1)}, u32[]{:S(2)}, u32[]{:S(2)}) collective-permute-start(f32[4,2,64,128]{3,2,1,0:T(8,128)S(1)} %get-tuple-element.45), channel_id=1, source_target_pairs={{0,2},{2,0},{4,6},{6,4},{1,3},{3,1},{5,7},{7,5},{8,10},{10,8},{12,... | collective-permute-start | bytes 786440 | tf_op jit(solution)/shard_map/ppermute | solution.py:51
  31.4 0.7 collective-permute-start.9
  32.1 7.8 %step.4 = (f32[4,68,72,128]{3,2,1,0:T(8,128)S(1)}, f32[4,2,64,128]{3,2,1,0:T(8,128)S(1)}) custom-call(f32[4,68,72,128]{3,2,1,0:T(8,128)S(1)} %get-tuple-element.40.field.rest_0_, f32[64,64,128]{2,1,0:T(8,128)S(1)} %get-tuple-element.32.weight, f32[4,2,64,128]{3,2,1,0:T(8,128)S(1)} %collective-permute-done.5.z_even, ...), custom_call_target="tpu_custom_call", output_to_operand_aliasing={{0}: (4, {})} | custom-call | flops 1 | bytes 1 | tf_op jit(solution)/shard_map/step/pallas_call | solution.py:312
  39.9 1.3 %edges.4 = (f32[4,68,72,128]{3,2,1,0:T(8,128)S(1)}, f32[4,2,64,128]{3,2,1,0:T(8,128)S(1)}, f32[4,2,64,128]{3,2,1,0:T(8,128)S(1)}, f32[4,2,64,128]{3,2,1,0:T(8,12...) custom-call(f32[4,68,72,128]{3,2,1,0:T(8,128)S(1)} %get-tuple-elemen, ...), custom_call_target="tpu_custom_call", output_to_operand_aliasing={{0}: (0, {}), {5}: (5, {})} | custom-call | flops 1 | bytes 1 | tf_op jit(solution)/shard_map/edges/pallas_call | solution.py:406
  41.3 1.8 %collective-permute-start.11 = (f32[4,2,64,128]{3,2,1,0:T(8,128)S(1)}, f32[4,2,64,128]{3,2,1,0:T(8,128)S(1)}, u32[]{:S(2)}, u32[]{:S(2)}) collective-permute-start(f32[4,2,64,128]{3,2,1,0:T(8,128)S(1)} %get-tuple-element.50), channel_id=1, source_target_pairs={{0,8},{8,0},{16,24},{24,16},{1,9},{9,1},{17,25},{25,17},{2,10},{10... | collective-permute-start | bytes 786440 | tf_op jit(solution)/shard_map/ppermute | solution.py:51
  43.1 0.7 collective-permute-start.12
  43.8 2.0 %collective-permute-start.13 = (f32[4,2,64,128]{3,2,1,0:T(8,128)S(1)}, f32[4,2,64,128]{3,2,1,0:T(8,128)S(1)}, u32[]{:S(2)}, u32[]{:S(2)}) collective-permute-start(f32[4,2,64,128]{3,2,1,0:T(8,128)S(1)} %get-tuple-element.52), channel_id=1, source_target_pairs={{0,2},{2,0},{4,6},{6,4},{1,3},{3,1},{5,7},{7,5},{8,10},{10,8},{12,... | collective-permute-start | bytes 786440 | tf_op jit(solution)/shard_map/ppermute | solution.py:51
  45.8 0.7 collective-permute-start.14
  46.5 6.9 %step.5.field = f32[4,68,72,128]{3,2,1,0:T(8,128)S(1)} custom-call(f32[4,68,72,128]{3,2,1,0:T(8,128)S(1)} %get-tuple-element.48.field, f32[64,64,128]{2,1,0:T(8,128)S(1)} %get-tuple-element.32.weight, f32[4,2,64,128]{3,2,1,0:T(8,128)S(1)} %collective-permute-done.10.z_even, ...), custom_call_target="tpu_custom_call", output_to_operand_aliasing={{}: (4, {})} | custom-call | flops 1 | bytes 1 | tf_op jit(solution)/shard_map/step/pallas_call | solution.py:312
  53.8 1.6 %gram.1 = f32[16,128]{1,0:T(8,128)S(1)} custom-call(f32[4,68,72,128]{3,2,1,0:T(8,128)S(1)} %edges.5.field), custom_call_target="tpu_custom_call" | custom-call | flops 1 | bytes 1 | tf_op jit(solution)/shard_map/gram/pallas_call | solution.py:447
  55.5 1.2 %collective-permute-done.15 = f32[16,128]{1,0:T(8,128)S(1)} collective-permute-done((f32[16,128]{1,0:T(8,128)S(1)}, f32[16,128]{1,0:T(8,128)S(1)}, u32[]{:S(2)}, u32[]{:S(2)}) %collective-permute-start.15) | collective-permute-done | bytes 8224 | tf_op jit(solution)/shard_map/ppermute | solution.py:565
  56.7 2.2 %collective-permute-start.18 = (f32[16,128]{1,0:T(8,128)S(1)}, f32[16,128]{1,0:T(8,128)S(1)}, u32[]{:S(2)}, u32[]{:S(2)}) collective-permute-start(f32[16,128]{1,0:T(8,128)S(1)} %add.12), channel_id=1, source_target_pairs={{0,6},{2,4},{4,2},{6,0},{1,7},{3,5},{5,3},{7,1},{8,14},{10,12},{12... | collective-permute-start | bytes 24584 | tf_op jit(solution)/shard_map/ppermute | solution.py:565
  58.9 1.9 %collective-permute-start.17 = (f32[16,128]{1,0:T(8,128)S(1)}, f32[16,128]{1,0:T(8,128)S(1)}, u32[]{:S(2)}, u32[]{:S(2)}) collective-permute-start(f32[16,128]{1,0:T(8,128)S(1)} %add.12), channel_id=1, source_target_pairs={{0,4},{2,6},{4,0},{6,2},{1,5},{3,7},{5,1},{7,3},{8,12},{10,14},{12... | collective-permute-start | bytes 24584 | tf_op jit(solution)/shard_map/ppermute | solution.py:565
  61.1 1.1 %collective-permute-done.18 = f32[16,128]{1,0:T(8,128)S(1)} collective-permute-done((f32[16,128]{1,0:T(8,128)S(1)}, f32[16,128]{1,0:T(8,128)S(1)}, u32[]{:S(2)}, u32[]{:S(2)}) %collective-permute-start.18) | collective-permute-done | bytes 8224 | tf_op jit(solution)/shard_map/ppermute | solution.py:565
  62.1 1.3 %collective-permute-done.17 = f32[16,128]{1,0:T(8,128)S(1)} collective-permute-done((f32[16,128]{1,0:T(8,128)S(1)}, f32[16,128]{1,0:T(8,128)S(1)}, u32[]{:S(2)}, u32[]{:S(2)}) %collective-permute-start.17) | collective-permute-done | bytes 8224 | tf_op jit(solution)/shard_map/ppermute | solution.py:565
  63.5 1.0 %collective-permute-done.16 = f32[16,128]{1,0:T(8,128)S(1)} collective-permute-done((f32[16,128]{1,0:T(8,128)S(1)}, f32[16,128]{1,0:T(8,128)S(1)}, u32[]{:S(2)}, u32[]{:S(2)}) %collective-permute-start.16) | collective-permute-done | bytes 8224 | tf_op jit(solution)/shard_map/ppermute | solution.py:565
  64.5 2.4 %collective-permute-start.21 = (f32[16,128]{1,0:T(8,128)S(1)}, f32[16,128]{1,0:T(8,128)S(1)}, u32[]{:S(2)}, u32[]{:S(2)}) collective-permute-start(f32[16,128]{1,0:T(8,128)S(1)} %add_add_fusion.rest_0_), channel_id=1, source_target_pairs={{0,24},{8,16},{16,8},{24,0},{1,25},{9,17},{17,9},{25,1},{2,26},{10... | collective-permute-start | bytes 24584 | tf_op jit(solution)/shard_map/ppermute | solution.py:565
  66.9 3.0 %collective-permute-start.20 = (f32[16,128]{1,0:T(8,128)S(1)}, f32[16,128]{1,0:T(8,128)S(1)}, u32[]{:S(2)}, u32[]{:S(2)}) collective-permute-start(f32[16,128]{1,0:T(8,128)S(1)} %add_add_fusion.rest_0_), channel_id=1, source_target_pairs={{0,16},{8,24},{16,0},{24,8},{1,17},{9,25},{17,1},{25,9},{2,18},{10... | collective-permute-start | bytes 24584 | tf_op jit(solution)/shard_map/ppermute | solution.py:565
  69.9 1.6 %collective-permute-done.20.rest_2_ = f32[16,128]{1,0:T(8,128)S(1)} collective-permute-done((f32[16,128]{1,0:T(8,128)S(1)}, f32[16,128]{1,0:T(8,128)S(1)}, u32[]{:S(2)}, u32[]{:S(2)}) %collective-permute-start.20) | collective-permute-done | bytes 8224 | tf_op jit(solution)/shard_map/ppermute | solution.py:565
  71.5 2.0 %collective-permute-done.19.rest_1_ = f32[16,128]{1,0:T(8,128)S(1)} collective-permute-done((f32[16,128]{1,0:T(8,128)S(1)}, f32[16,128]{1,0:T(8,128)S(1)}, u32[]{:S(2)}, u32[]{:S(2)}) %collective-permute-start.19) | collective-permute-done | bytes 8224 | tf_op jit(solution)/shard_map/ppermute | solution.py:565
  73.5 4.2 %basis.1 = (f32[4,64,64,128]{3,2,1,0:T(8,128)}, f32[4,4]{1,0:T(4,128)}) custom-call(f32[4,68,72,128]{3,2,1,0:T(8,128)S(1)} %edges.5.field, f32[16,128]{1,0:T(8,128)S(1)} %add_add_fusion.rest_0_, f32[16,128]{1,0:T(8,128)S(1)} %collective-permute-done.19.rest_1_, f32[16,128]{1,0:T(8,128)S(1)} %collective-permute-done.20.rest_2_, ...), custom_call_target="tpu_custom_call" | custom-call | flops 1 | bytes 1 | tf_op jit(solution)/shard_map/basis/pallas_call | solution.py:541
  (25 shorter events, 0.9 us)
Async XLA Ops:
  6.7 6.1 %collective-permute-start = (f32[4,2,64,128]{3,2,1,0:T(8,128)S(1)}, f32[4,2,64,128]{3,2,1,0:T(8,128)S(1)}, u32[]{:S(2)}, u32[]{:S(2)}) collective-permute-start(f32[4,2,64,128]{3,2,1,0:T(8,128)S(1)} %get-tuple-element.33), channel_id=1, source_target_pairs={{0,1},{1,0},{2,3},{3,2},{4,5},{5,4},{6,7},{7,6},{8,9},{9,8},{10,11... | collective-permute-start | bytes 786440 | tf_op jit(solution)/shard_map/ppermute | solution.py:51
  7.2 13.4 %collective-permute-start.1 = (f32[4,2,64,128]{3,2,1,0:T(8,128)S(1)}, f32[4,2,64,128]{3,2,1,0:T(8,128)S(1)}, u32[]{:S(2)}, u32[]{:S(2)}) collective-permute-start(f32[4,2,64,128]{3,2,1,0:T(8,128)S(1)} %get-tuple-element.35), channel_id=1, source_target_pairs={{0,8},{8,0},{16,24},{24,16},{1,9},{9,1},{17,25},{25,17},{2,10},{10... | collective-permute-start | bytes 786440 | tf_op jit(solution)/shard_map/ppermute | solution.py:51
  9.8 10.8 %collective-permute-start.2 = (f32[4,2,64,128]{3,2,1,0:T(8,128)S(1)}, f32[4,2,64,128]{3,2,1,0:T(8,128)S(1)}, u32[]{:S(2)}, u32[]{:S(2)}) collective-permute-start(f32[4,2,64,128]{3,2,1,0:T(8,128)S(1)} %get-tuple-element.36), channel_id=1, source_target_pairs={{8,16},{16,8},{9,17},{17,9},{10,18},{18,10},{11,19},{19,11},{12,20... | collective-permute-start | bytes 786440 | tf_op jit(solution)/shard_map/ppermute | solution.py:51
  10.4 10.2 %collective-permute-start.3 = (f32[4,2,64,128]{3,2,1,0:T(8,128)S(1)}, f32[4,2,64,128]{3,2,1,0:T(8,128)S(1)}, u32[]{:S(2)}, u32[]{:S(2)}) collective-permute-start(f32[4,2,64,128]{3,2,1,0:T(8,128)S(1)} %get-tuple-element.37), channel_id=1, source_target_pairs={{0,2},{2,0},{4,6},{6,4},{1,3},{3,1},{5,7},{7,5},{8,10},{10,8},{12,... | collective-permute-start | bytes 786440 | tf_op jit(solution)/shard_map/ppermute | solution.py:51
  12.1 8.5 %collective-permute-start.4 = (f32[4,2,64,128]{3,2,1,0:T(8,128)S(1)}, f32[4,2,64,128]{3,2,1,0:T(8,128)S(1)}, u32[]{:S(2)}, u32[]{:S(2)}) collective-permute-start(f32[4,2,64,128]{3,2,1,0:T(8,128)S(1)} %get-tuple-element.38), channel_id=1, source_target_pairs={{2,4},{4,2},{3,5},{5,3},{10,12},{12,10},{11,13},{13,11},{18,20},{2... | collective-permute-start | bytes 786440 | tf_op jit(solution)/shard_map/ppermute | solution.py:51
  21.9 10.2 %collective-permute-start.5 = (f32[4,2,64,128]{3,2,1,0:T(8,128)S(1)}, f32[4,2,64,128]{3,2,1,0:T(8,128)S(1)}, u32[]{:S(2)}, u32[]{:S(2)}) collective-permute-start(f32[4,2,64,128]{3,2,1,0:T(8,128)S(1)} %get-tuple-element.41), channel_id=1, source_target_pairs={{0,1},{1,0},{2,3},{3,2},{4,5},{5,4},{6,7},{7,6},{8,9},{9,8},{10,11... | collective-permute-start | bytes 786440 | tf_op jit(solution)/shard_map/ppermute | solution.py:51
  22.0 17.9 %collective-permute-start.6 = (f32[4,2,64,128]{3,2,1,0:T(8,128)S(1)}, f32[4,2,64,128]{3,2,1,0:T(8,128)S(1)}, u32[]{:S(2)}, u32[]{:S(2)}) collective-permute-start(f32[4,2,64,128]{3,2,1,0:T(8,128)S(1)} %get-tuple-element.43), channel_id=1, source_target_pairs={{0,8},{8,0},{16,24},{24,16},{1,9},{9,1},{17,25},{25,17},{2,10},{10... | collective-permute-start | bytes 786440 | tf_op jit(solution)/shard_map/ppermute | solution.py:51
  26.4 13.5 %collective-permute-start.7 = (f32[4,2,64,128]{3,2,1,0:T(8,128)S(1)}, f32[4,2,64,128]{3,2,1,0:T(8,128)S(1)}, u32[]{:S(2)}, u32[]{:S(2)}) collective-permute-start(f32[4,2,64,128]{3,2,1,0:T(8,128)S(1)} %get-tuple-element.44), channel_id=1, source_target_pairs={{8,16},{16,8},{9,17},{17,9},{10,18},{18,10},{11,19},{19,11},{12,20... | collective-permute-start | bytes 786440 | tf_op jit(solution)/shard_map/ppermute | solution.py:51
  27.1 12.8 %collective-permute-start.8 = (f32[4,2,64,128]{3,2,1,0:T(8,128)S(1)}, f32[4,2,64,128]{3,2,1,0:T(8,128)S(1)}, u32[]{:S(2)}, u32[]{:S(2)}) collective-permute-start(f32[4,2,64,128]{3,2,1,0:T(8,128)S(1)} %get-tuple-element.45), channel_id=1, source_target_pairs={{0,2},{2,0},{4,6},{6,4},{1,3},{3,1},{5,7},{7,5},{8,10},{10,8},{12,... | collective-permute-start | bytes 786440 | tf_op jit(solution)/shard_map/ppermute | solution.py:51
  31.4 8.5 %collective-permute-start.9 = (f32[4,2,64,128]{3,2,1,0:T(8,128)S(1)}, f32[4,2,64,128]{3,2,1,0:T(8,128)S(1)}, u32[]{:S(2)}, u32[]{:S(2)}) collective-permute-start(f32[4,2,64,128]{3,2,1,0:T(8,128)S(1)} %get-tuple-element.46), channel_id=1, source_target_pairs={{2,4},{4,2},{3,5},{5,3},{10,12},{12,10},{11,13},{13,11},{18,20},{2... | collective-permute-start | bytes 786440 | tf_op jit(solution)/shard_map/ppermute | solution.py:51
  41.2 5.3 %collective-permute-start.10 = (f32[4,2,64,128]{3,2,1,0:T(8,128)S(1)}, f32[4,2,64,128]{3,2,1,0:T(8,128)S(1)}, u32[]{:S(2)}, u32[]{:S(2)}) collective-permute-start(f32[4,2,64,128]{3,2,1,0:T(8,128)S(1)} %get-tuple-element.49), channel_id=1, source_target_pairs={{0,1},{1,0},{2,3},{3,2},{4,5},{5,4},{6,7},{7,6},{8,9},{9,8},{10,11... | collective-permute-start | bytes 786440 | tf_op jit(solution)/shard_map/ppermute | solution.py:51
  41.3 12.1 %collective-permute-start.11 = (f32[4,2,64,128]{3,2,1,0:T(8,128)S(1)}, f32[4,2,64,128]{3,2,1,0:T(8,128)S(1)}, u32[]{:S(2)}, u32[]{:S(2)}) collective-permute-start(f32[4,2,64,128]{3,2,1,0:T(8,128)S(1)} %get-tuple-element.50), channel_id=1, source_target_pairs={{0,8},{8,0},{16,24},{24,16},{1,9},{9,1},{17,25},{25,17},{2,10},{10... | collective-permute-start | bytes 786440 | tf_op jit(solution)/shard_map/ppermute | solution.py:51
  43.1 10.3 %collective-permute-start.12 = (f32[4,2,64,128]{3,2,1,0:T(8,128)S(1)}, f32[4,2,64,128]{3,2,1,0:T(8,128)S(1)}, u32[]{:S(2)}, u32[]{:S(2)}) collective-permute-start(f32[4,2,64,128]{3,2,1,0:T(8,128)S(1)} %get-tuple-element.51), channel_id=1, source_target_pairs={{8,16},{16,8},{9,17},{17,9},{10,18},{18,10},{11,19},{19,11},{12,20... | collective-permute-start | bytes 786440 | tf_op jit(solution)/shard_map/ppermute | solution.py:51
  43.8 9.6 %collective-permute-start.13 = (f32[4,2,64,128]{3,2,1,0:T(8,128)S(1)}, f32[4,2,64,128]{3,2,1,0:T(8,128)S(1)}, u32[]{:S(2)}, u32[]{:S(2)}) collective-permute-start(f32[4,2,64,128]{3,2,1,0:T(8,128)S(1)} %get-tuple-element.52), channel_id=1, source_target_pairs={{0,2},{2,0},{4,6},{6,4},{1,3},{3,1},{5,7},{7,5},{8,10},{10,8},{12,... | collective-permute-start | bytes 786440 | tf_op jit(solution)/shard_map/ppermute | solution.py:51
  45.8 7.6 %collective-permute-start.14 = (f32[4,2,64,128]{3,2,1,0:T(8,128)S(1)}, f32[4,2,64,128]{3,2,1,0:T(8,128)S(1)}, u32[]{:S(2)}, u32[]{:S(2)}) collective-permute-start(f32[4,2,64,128]{3,2,1,0:T(8,128)S(1)} %get-tuple-element.53), channel_id=1, source_target_pairs={{2,4},{4,2},{3,5},{5,3},{10,12},{12,10},{11,13},{13,11},{18,20},{2... | collective-permute-start | bytes 786440 | tf_op jit(solution)/shard_map/ppermute | solution.py:51
  55.4 1.2 %collective-permute-start.15 = (f32[16,128]{1,0:T(8,128)S(1)}, f32[16,128]{1,0:T(8,128)S(1)}, u32[]{:S(2)}, u32[]{:S(2)}) collective-permute-start(f32[16,128]{1,0:T(8,128)S(1)} %gram.1), channel_id=1, source_target_pairs={{0,1},{1,0},{2,3},{3,2},{4,5},{5,4},{6,7},{7,6},{8,9},{9,8},{10,11... | collective-permute-start | bytes 24584 | tf_op jit(solution)/shard_map/ppermute | solution.py:565
  56.7 5.4 %collective-permute-start.18 = (f32[16,128]{1,0:T(8,128)S(1)}, f32[16,128]{1,0:T(8,128)S(1)}, u32[]{:S(2)}, u32[]{:S(2)}) collective-permute-start(f32[16,128]{1,0:T(8,128)S(1)} %add.12), channel_id=1, source_target_pairs={{0,6},{2,4},{4,2},{6,0},{1,7},{3,5},{5,3},{7,1},{8,14},{10,12},{12... | collective-permute-start | bytes 24584 | tf_op jit(solution)/shard_map/ppermute | solution.py:565
  58.9 4.5 %collective-permute-start.17 = (f32[16,128]{1,0:T(8,128)S(1)}, f32[16,128]{1,0:T(8,128)S(1)}, u32[]{:S(2)}, u32[]{:S(2)}) collective-permute-start(f32[16,128]{1,0:T(8,128)S(1)} %add.12), channel_id=1, source_target_pairs={{0,4},{2,6},{4,0},{6,2},{1,5},{3,7},{5,1},{7,3},{8,12},{10,14},{12... | collective-permute-start | bytes 24584 | tf_op jit(solution)/shard_map/ppermute | solution.py:565
  60.8 3.7 %collective-permute-start.16 = (f32[16,128]{1,0:T(8,128)S(1)}, f32[16,128]{1,0:T(8,128)S(1)}, u32[]{:S(2)}, u32[]{:S(2)}) collective-permute-start(f32[16,128]{1,0:T(8,128)S(1)} %add.12), channel_id=1, source_target_pairs={{0,2},{2,0},{4,6},{6,4},{1,3},{3,1},{5,7},{7,5},{8,10},{10,8},{12,... | collective-permute-start | bytes 24584 | tf_op jit(solution)/shard_map/ppermute | solution.py:565
  64.5 5.4 %collective-permute-start.21 = (f32[16,128]{1,0:T(8,128)S(1)}, f32[16,128]{1,0:T(8,128)S(1)}, u32[]{:S(2)}, u32[]{:S(2)}) collective-permute-start(f32[16,128]{1,0:T(8,128)S(1)} %add_add_fusion.rest_0_), channel_id=1, source_target_pairs={{0,24},{8,16},{16,8},{24,0},{1,25},{9,17},{17,9},{25,1},{2,26},{10... | collective-permute-start | bytes 24584 | tf_op jit(solution)/shard_map/ppermute | solution.py:565
  66.9 4.6 %collective-permute-start.20 = (f32[16,128]{1,0:T(8,128)S(1)}, f32[16,128]{1,0:T(8,128)S(1)}, u32[]{:S(2)}, u32[]{:S(2)}) collective-permute-start(f32[16,128]{1,0:T(8,128)S(1)} %add_add_fusion.rest_0_), channel_id=1, source_target_pairs={{0,16},{8,24},{16,0},{24,8},{1,17},{9,25},{17,1},{25,9},{2,18},{10... | collective-permute-start | bytes 24584 | tf_op jit(solution)/shard_map/ppermute | solution.py:565
  69.9 3.7 %collective-permute-start.19 = (f32[16,128]{1,0:T(8,128)S(1)}, f32[16,128]{1,0:T(8,128)S(1)}, u32[]{:S(2)}, u32[]{:S(2)}) collective-permute-start(f32[16,128]{1,0:T(8,128)S(1)} %add_add_fusion.rest_0_), channel_id=1, source_target_pairs={{0,8},{8,0},{16,24},{24,16},{1,9},{9,1},{17,25},{25,17},{2,10},{10... | collective-permute-start | bytes 24584 | tf_op jit(solution)/shard_map/ppermute | solution.py:565

commit v3 on v2

--- a/solution.py
+++ b/solution.py
@@ -9,8 +9,9 @@
 
 CENTRE = 4.5
 HALF_WIDTH = 3.5
-SCALE = 2.0 / HALF_WIDTH
-EDGE = SCALE / 24.0
+EDGE = 2.0 / HALF_WIDTH / 24.0
+BACK = (None, 2.0 / EDGE**2, 1.0 / EDGE**2)
+FINAL = 0.5 * EDGE**3
 LANES = 128
 TILE = 8
 PAD = 8
@@ -53,44 +54,6 @@
 
 def is_odd(axis):
     return lax.rem(lax.axis_index(axis), 2) == 1
-
-
-def faces_x_kernel(field, even, odd, sems):
-    count = field.shape[1]
-    low = field.at[:, pl.ds(0, 2)]
-    high = field.at[:, pl.ds(count - 2, 2)]
-    flip = is_odd("gx")
-
-    def move(first, second):
-        one = pltpu.make_async_copy(first, even, sems.at[0])
-        two = pltpu.make_async_copy(second, odd, sems.at[1])
-        one.start()
-        two.start()
-        one.wait()
-        two.wait()
-
-    @pl.when(flip)
-    def _():
-        move(low, high)
-
-    @pl.when(jnp.logical_not(flip))
-    def _():
-        move(high, low)
-
-
-def faces_x(orbitals):
-    orbs, _, ny, nz = orbitals.shape
-    shape = vmem_out((orbs, 2, ny, nz))
-    return pl.pallas_call(
-        faces_x_kernel,
-        out_shape=(shape, shape),
-        in_specs=[ANYWHERE],
-        out_specs=(WHOLE, WHOLE),
-        scratch_shapes=[pltpu.SemaphoreType.DMA((2,))],
-        compiler_params=params(),
-        cost_estimate=LITTLE,
-        name="faces_x",
-    )(orbitals)
 
 
 def pack_y_group(rows, even, odd, orb, group, flip):
@@ -118,20 +81,35 @@
         packed[orb, group, pl.ds(tile * TILE, TILE), :] = totals[number]
 
 
-def load_kernel(nx, ny, field, potential, out, weight, even, odd, packed, sems):
+def pack_x(flat, even, odd, pitch, nx, ny, orb, flip):
+    for layer in range(2):
+        low = flat[orb, pl.ds((2 + layer) * pitch, ny), :]
+        high = flat[orb, pl.ds((nx + layer) * pitch, ny), :]
+        even[orb, layer] = jnp.where(flip, low, high)
+        odd[orb, layer] = jnp.where(flip, high, low)
+
+
+def load_kernel(
+    nx, ny, field, potential, out, weight, x_even, x_odd, y_even, y_odd, packed, sems
+):
     orbs = field.shape[0]
     pitch = ny + PAD
+    groups = nx // PER
     flat = out.reshape(orbs, (nx + 4) * pitch, LANES)
-    copies = []
+
+    def copy(orb, group):
+        return pltpu.make_async_copy(
+            field.at[orb, pl.ds(group * PER, PER)],
+            out.at[orb, pl.ds(2 + group * PER, PER), pl.ds(0, ny)],
+            sems.at[orb * groups + group],
+        )
+
+    first = pltpu.make_async_copy(potential, weight, sems.at[orbs * groups])
+    first.start()
     for orb in range(orbs):
-        copy = pltpu.make_async_copy(
-            field.at[orb], out.at[orb, pl.ds(2, nx), pl.ds(0, ny)], sems.at[orb]
-        )
-        copy.start()
-        copies.append(copy)
-    last = pltpu.make_async_copy(potential, weight, sems.at[orbs])
-    last.start()
-    flip = is_odd("gy")
+        for group in range(groups):
+            copy(orb, group).start()
+    flip_x, flip_y = is_odd("gx"), is_odd("gy")
     zero_planes = jnp.zeros((2 * pitch, LANES), jnp.float32)
     zero_rows = jnp.zeros((PAD, LANES), jnp.float32)
     for orb in range(orbs):
@@ -142,50 +120,63 @@
         def _(x):
             flat[orb, pl.ds(pl.multiple_of((x + 2) * pitch + ny, TILE), PAD), :] = zero_rows
 
-    for orb in range(orbs):
-        copies[orb].wait()
-
-        @pl.loop(0, nx // TILE, unroll=2)
-        def _(group):
-            start = (group * TILE + 2) * pitch
+    first.wait()
+
+    @pl.loop(0, nx, unroll=2)
+    def _(x):
+        weight[x] = 24.0 * weight[x] + 24.0 * (0.5 * 7.5 - CENTRE)
+
+    @pl.loop(0, orbs * groups)
+    def _(index):
+        orb, group = index // groups, lax.rem(index, groups)
+        copy(orb, group).wait()
+        pack_z_tiles(flat, packed, pitch, orb, group, range(ny // TILE))
+        for part in range(PER // TILE):
+            place = group * (PER // TILE) + part
+            start = (place * TILE + 2) * pitch
             rows = [
                 flat[orb, pl.ds(start + y, TILE, stride=pitch), :] for y in (0, 1, ny - 2, ny - 1)
             ]
-            pack_y_group(rows, even, odd, orb, group, flip)
-
-        @pl.loop(0, nx // PER)
-        def _(group):
-            pack_z_tiles(flat, packed, pitch, orb, group, range(ny // TILE))
-
-    last.wait()
-
-    @pl.loop(0, nx, unroll=2)
-    def _(x):
-        weight[x] = SCALE * weight[x] + SCALE * (0.5 * 7.5 - CENTRE)
+            pack_y_group(rows, y_even, y_odd, orb, place, flip_y)
+
+    @pl.loop(0, orbs)
+    def _(orb):
+        pack_x(flat, x_even, x_odd, pitch, nx, ny, orb, flip_x)
 
 
 def load(orbitals, potential):
     orbs, nx, ny, nz = orbitals.shape
-    face = vmem_out((orbs, 2, nx, nz))
     return pl.pallas_call(
         functools.partial(load_kernel, nx, ny),
         out_shape=(
             vmem_out((orbs, nx + 4, ny + PAD, nz)),
             vmem_out((nx, ny, nz)),
-            face,
-            face,
+            *[vmem_out((orbs, 2, ny, nz))] * 2,
+            *[vmem_out((orbs, 2, nx, nz))] * 2,
             vmem_out((orbs, nx // PER, ny, nz)),
         ),
         in_specs=[ANYWHERE, ANYWHERE],
-        out_specs=(WHOLE,) * 5,
-        scratch_shapes=[pltpu.SemaphoreType.DMA((orbs + 1,))],
+        out_specs=(WHOLE,) * 7,
+        scratch_shapes=[pltpu.SemaphoreType.DMA((orbs * (nx // PER) + 1,))],
         compiler_params=params(),
         cost_estimate=LITTLE,
         name="load",
     )(orbitals, potential)
 
 
-def step_kernel(nx, ny, first, last, field, weight, z_even, z_odd, *rest):
+def store_late(ref, works):
+    waiting = []
+    for work, *where in works:
+        ready = work(*where)
+        for there, value in waiting:
+            ref[there] = value
+        waiting = ready
+    for there, value in waiting:
+        ref[there] = value
+
+
+def step_kernel(nx, ny, back, last, field, weight, z_even, z_odd, *rest):
+    first = back is None
     rest = rest if first else rest[1:]
     out, packed = rest[0], None if last else rest[1]
     correction, mix = rest[-2:]
@@ -193,7 +184,6 @@
     pitch = ny + PAD
     flat = field.reshape(orbs, (nx + 4) * pitch, LANES)
     flat_out = out.reshape(orbs, (nx + 4) * pitch, LANES)
-    edge = EDGE * (0.5 if first else 1.0)
     groups = nx // PER
     tiles = ny // TILE
     flip = is_odd("gz")
@@ -220,19 +210,20 @@
     mix[pl.ds(0, LANES), :] = weights
     mix[pl.ds(LANES, LANES), :] = weights
 
-    for orb in range(orbs):
-        for group in range(groups):
-            even, odd = z_even[orb, group], z_odd[orb, group]
-            below = jnp.where(flip, even, odd)
-            above = jnp.where(flip, odd, even)
-            beyond = jnp.where(place < 2, below, above)
-            left = pltpu.roll(beyond, LANES - 2, 1) - 16.0 * jnp.where(
-                place == 1, pltpu.roll(beyond, LANES - 1, 1), 0.0
-            )
-            right = pltpu.roll(beyond, 2, 1) - 16.0 * jnp.where(
-                place == 2, pltpu.roll(beyond, 1, 1), 0.0
-            )
-            correction[orb, group] = jnp.where(place < 2, left, right)
+    def add_beyond(orb, group):
+        even, odd = z_even[orb, group], z_odd[orb, group]
+        below = jnp.where(flip, even, odd)
+        above = jnp.where(flip, odd, even)
+        beyond = jnp.where(place < 2, below, above)
+        left = pltpu.roll(beyond, LANES - 2, 1) - 16.0 * jnp.where(
+            place == 1, pltpu.roll(beyond, LANES - 1, 1), 0.0
+        )
+        right = pltpu.roll(beyond, 2, 1) - 16.0 * jnp.where(
+            place == 2, pltpu.roll(beyond, 1, 1), 0.0
+        )
+        return [((orb, group), jnp.where(place < 2, left, right))]
+
+    store_late(correction, [(add_beyond, orb, group) for orb in range(orbs) for group in range(groups)])
 
     def locate(index, tile):
         orb, group = index // groups, lax.rem(index, groups)
@@ -278,6 +269,7 @@
                 start = pl.multiple_of(start, TILE)
             return flat[orb, pl.ds(start, TILE), :]
 
+        inner = not last and 0 < tile < tiles - 1
         mine = [rows(plane) for plane in range(-2, PER + 2)]
         values = []
         total = None
@@ -285,32 +277,30 @@
             near = (mine[plane + 1] + mine[plane + 3]) + (rows(plane, -1) + rows(plane, 1))
             far = (mine[plane] + mine[plane + 4]) + (rows(plane, -2) + rows(plane, 2))
             ours = weight[group * PER + plane, pl.ds(tile * TILE, TILE), :]
-            if first:
-                ours = 0.5 * ours
-            value = ours * mine[plane + 2] + edge * ((far - 16.0 * near) + sums[plane])
+            value = ours * mine[plane + 2] + ((far - 16.0 * near) + sums[plane])
             if not first:
                 start = pl.multiple_of(base + plane * pitch, TILE)
-                value = value - flat_out[orb, pl.ds(start, TILE), :]
-            if not last:
+                value = value - back * flat_out[orb, pl.ds(start, TILE), :]
+            if inner:
                 total = pack_z_lanes(value, plane, total)
             values.append(value)
         for plane in range(PER):
             start = pl.multiple_of(base + plane * pitch, TILE)
             flat_out[orb, pl.ds(start, TILE), :] = values[plane]
-        if not last:
+        if inner:
             packed[orb, group, pl.ds(tile * TILE, TILE), :] = total
 
     lax.fori_loop(0, orbs * groups, block, along_z(0, 0))
 
 
-def step(field, weight, z_even, z_odd, before, last):
+def step(field, weight, z_even, z_odd, before, back, last):
     orbs = field.shape[0]
     nx, ny, nz = weight.shape
     first = before is None
     args = [field, weight, z_even, z_odd] + ([] if first else [before])
     shapes = [vmem_out(field.shape)] + ([] if last else [vmem_out(z_even.shape)])
     return pl.pallas_call(
-        functools.partial(step_kernel, nx, ny, first, last),
+        functools.partial(step_kernel, nx, ny, back, last),
         out_shape=tuple(shapes),
         in_specs=[WHOLE] * len(args),
         out_specs=(WHOLE,) * len(shapes),
@@ -325,86 +315,137 @@
     )(*[in_vmem(arg) for arg in args])
 
 
-def edges_kernel(nx, ny, edge, last, field, x_even, x_odd, y_even, y_odd, *rest):
+def edges_kernel(nx, ny, last, field, x_even, y_odd, y_even, x_odd, extra, *rest):
     orbs = field.shape[0]
     pitch = ny + PAD
     if last:
-        (out,) = rest
+        out, products = rest
     else:
-        _, out, next_x_even, next_x_odd, next_y_even, next_y_odd, packed = rest
+        out, next_x_even, next_x_odd, next_y_even, next_y_odd, packed = rest
     flat = out.reshape(orbs, (nx + 4) * pitch, LANES)
     flip_x, flip_y = is_odd("gx"), is_odd("gy")
 
+    tiles = ny // TILE
+
     def plane_rows(x):
         return pl.ds((x + 2) * pitch, ny)
 
-    @pl.loop(0, orbs)
-    def _(orb):
+    def fix_x(orb):
         def halves(layer):
             even, odd = x_even[orb, layer], x_odd[orb, layer]
             return jnp.where(flip_x, even, odd), jnp.where(flip_x, odd, even)
 
         low_far, high_near = halves(0)
         low_near, high_far = halves(1)
-        flat[orb, plane_rows(0), :] += edge * (low_far - 16.0 * low_near)
-        flat[orb, plane_rows(1), :] += edge * low_near
-        flat[orb, plane_rows(nx - 2), :] += edge * high_near
-        flat[orb, plane_rows(nx - 1), :] += edge * (high_far - 16.0 * high_near)
-
-        @pl.loop(0, nx // TILE, unroll=2)
-        def _(group):
-            place = pl.ds(group * TILE, TILE)
-
-            def pick(layer):
-                even, odd = y_even[orb, layer, place, :], y_odd[orb, layer, place, :]
-                return jnp.where(flip_y, even, odd), jnp.where(flip_y, odd, even)
-
-            low_far, high_near = pick(0)
-            low_near, high_far = pick(1)
-            adds = (
-                edge * (low_far - 16.0 * low_near),
-                edge * low_near,
-                edge * high_near,
-                edge * (high_far - 16.0 * high_near),
-            )
-            start = (group * TILE + 2) * pitch
-            rows = []
-            for y, add in zip((0, 1, ny - 2, ny - 1), adds):
-                there = pl.ds(start + y, TILE, stride=pitch)
-                value = flat[orb, there, :] + add
-                flat[orb, there, :] = value
-                rows.append(value)
-            if not last:
-                pack_y_group(rows, next_y_even, next_y_odd, orb, group, flip_y)
-
-        if not last:
-            for layer in range(2):
-                low = flat[orb, plane_rows(layer), :]
-                high = flat[orb, plane_rows(nx - 2 + layer), :]
-                next_x_even[orb, layer] = jnp.where(flip_x, low, high)
-                next_x_odd[orb, layer] = jnp.where(flip_x, high, low)
-
-            tiles = ny // TILE
-            for group in range(nx // PER):
-                pack_z_tiles(flat, packed, pitch, orb, group, (0, tiles - 1))
-            for x in (0, 1, nx - 2, nx - 1):
-                group, plane = x // PER, x % PER
-                there = pl.ds(TILE, ny - 2 * TILE)
-                rows = flat[orb, pl.ds((x + 2) * pitch + TILE, ny - 2 * TILE), :]
-                packed[orb, group, there, :] = pack_z_lanes(
-                    rows, plane, packed[orb, group, there, :]
-                )
-
-
-def edges(field, packed, nx, ny, halos, edge, last):
+        adds = (
+            low_far - 16.0 * low_near,
+            low_near,
+            high_near,
+            high_far - 16.0 * high_near,
+        )
+        return [
+            ((orb, plane_rows(x), slice(None)), flat[orb, plane_rows(x), :] + add)
+            for x, add in zip((0, 1, nx - 2, nx - 1), adds)
+        ]
+
+    store_late(flat, [(fix_x, orb) for orb in range(orbs)])
+
+    def fix_y(orb, group):
+        place = pl.ds(group * TILE, TILE)
+
+        def pick(layer):
+            even, odd = y_even[orb, layer, place, :], y_odd[orb, layer, place, :]
+            return jnp.where(flip_y, even, odd), jnp.where(flip_y, odd, even)
+
+        low_far, high_near = pick(0)
+        low_near, high_far = pick(1)
+        adds = (
+            low_far - 16.0 * low_near,
+            low_near,
+            high_near,
+            high_far - 16.0 * high_near,
+        )
+        start = (group * TILE + 2) * pitch
+        rows = []
+        for y, add in zip((0, 1, ny - 2, ny - 1), adds):
+            there = pl.ds(start + y, TILE, stride=pitch)
+            rows.append((there, flat[orb, there, :] + add))
+        return rows
+
+    @pl.loop(0, orbs)
+    def _(orb):
+        groups = range(nx // TILE)
+        for half in (groups[: len(groups) // 2], groups[len(groups) // 2 :]):
+            rows = [fix_y(orb, group) for group in half]
+            for group, values in zip(half, rows):
+                for there, value in values:
+                    flat[orb, there, :] = value
+                if not last:
+                    pack_y_group(
+                        [value for _, value in values], next_y_even, next_y_odd, orb, group, flip_y
+                    )
+
+    if not last:
+        for orb in range(orbs):
+            pack_x(flat, next_x_even, next_x_odd, pitch, nx, ny, orb, flip_x)
+
+        def border(orb, group):
+            ends = (0, tiles - 1)
+            totals = [None] * len(ends)
+            for plane in range(PER):
+                for number, tile in enumerate(ends):
+                    start = (group * PER + plane + 2) * pitch + tile * TILE
+                    rows = flat[orb, pl.ds(start, TILE), :]
+                    totals[number] = pack_z_lanes(rows, plane, totals[number])
+            return [
+                ((orb, group, pl.ds(tile * TILE, TILE), slice(None)), total)
+                for tile, total in zip(ends, totals)
+            ]
+
+        def planes(orb, group):
+            there = pl.ds(TILE, ny - 2 * TILE)
+            total = extra[orb, group, there, :]
+            for x in sorted({0, 1, nx - 2, nx - 1}):
+                if x // PER == group:
+                    rows = flat[orb, pl.ds((x + 2) * pitch + TILE, ny - 2 * TILE), :]
+                    total = pack_z_lanes(rows, x % PER, total)
+            return [((orb, group, there, slice(None)), total)]
+
+        store_late(
+            packed,
+            [
+                (work, orb, group)
+                for orb in range(orbs)
+                for group in range(nx // PER)
+                for work in (border, planes)
+            ],
+        )
+
+    if last:
+        inside, border = range(1, tiles - 1), (0, tiles - 1)
+        totals = [jnp.zeros((TILE, LANES), jnp.float32) for _ in pair_list(orbs)]
+        for start, stop, tiles in (
+            (0, nx, border),
+            (0, 2, inside),
+            (nx - 2, nx, inside),
+        ):
+            totals = add_products(flat, pitch, start, stop, tiles, totals)
+        for index, total in enumerate(totals):
+            there = pl.ds(index, 1)
+            products[there, :] = extra[there, :] + jnp.sum(total, axis=0, keepdims=True)
+        unused = pl.ds(len(totals), products.shape[0] - len(totals))
+        products[unused, :] = extra[unused, :]
+
+
+def edges(field, extra, nx, ny, halos, last):
     orbs, nz = field.shape[0], field.shape[-1]
-    args = [field, *halos] + ([] if last else [packed])
+    args = [field, *halos, extra]
     shapes = [vmem_out(field.shape)]
     if not last:
         shapes += [vmem_out((orbs, 2, ny, nz))] * 2 + [vmem_out((orbs, 2, nx, nz))] * 2
-        shapes += [vmem_out(packed.shape)]
+    shapes += [vmem_out(extra.shape)]
     return pl.pallas_call(
-        functools.partial(edges_kernel, nx, ny, edge, last),
+        functools.partial(edges_kernel, nx, ny, last),
         out_shape=tuple(shapes),
         in_specs=[WHOLE] * len(args),
         out_specs=(WHOLE,) * len(shapes),
@@ -419,39 +460,43 @@
     return [(line, column) for line in range(orbs) for column in range(line, orbs)]
 
 
-def gram_kernel(nx, ny, field, out):
+def add_products(flat, pitch, first, stop, tiles, totals):
+    orbs = flat.shape[0]
+
+    def plane(x, totals):
+        totals = list(totals)
+        for tile in tiles:
+            start = pl.multiple_of((x + 2) * pitch + tile * TILE, TILE)
+            rows = [flat[orb, pl.ds(start, TILE), :] for orb in range(orbs)]
+            for index, (line, column) in enumerate(pair_list(orbs)):
+                totals[index] = totals[index] + rows[line] * rows[column]
+        return tuple(totals)
+
+    return list(lax.fori_loop(first, stop, plane, tuple(totals)))
+
+
+def products_kernel(nx, ny, field, out):
     orbs = field.shape[0]
     pitch = ny + PAD
     flat = field.reshape(orbs, (nx + 4) * pitch, LANES)
-    pairs = pair_list(orbs)
-
-    def plane(x, totals):
-        totals = list(totals)
-        for tile in range(ny // TILE):
-            start = pl.multiple_of((x + 2) * pitch + tile * TILE, TILE)
-            rows = [flat[orb, pl.ds(start, TILE), :] for orb in range(orbs)]
-            for index, (line, column) in enumerate(pairs):
-                totals[index] = totals[index] + rows[line] * rows[column]
-        return tuple(totals)
-
-    zero = jnp.zeros((TILE, LANES), jnp.float32)
-    totals = lax.fori_loop(0, nx, plane, (zero,) * len(pairs))
+    totals = [jnp.zeros((TILE, LANES), jnp.float32) for _ in pair_list(orbs)]
+    totals = add_products(flat, pitch, 2, nx - 2, range(1, ny // TILE - 1), totals)
     out[...] = jnp.zeros_like(out)
     for index, total in enumerate(totals):
         out[pl.ds(index, 1), :] = jnp.sum(total, axis=0, keepdims=True)
 
 
-def gram(field, nx, ny):
+def products_inside(field, nx, ny):
     orbs = field.shape[0]
     rows = -(-len(pair_list(orbs)) // TILE) * TILE
     return pl.pallas_call(
-        functools.partial(gram_kernel, nx, ny),
-        out_shape=jax.ShapeDtypeStruct((rows, LANES), jnp.float32),
+        functools.partial(products_kernel, nx, ny),
+        out_shape=vmem_out((rows, LANES)),
         in_specs=[WHOLE],
         out_specs=WHOLE,
         compiler_params=params(),
         cost_estimate=LITTLE,
-        name="gram",
+        name="products",
     )(in_vmem(field))
 
 
@@ -465,7 +510,8 @@
     total = sums[0][...]
     for part in sums[1:]:
         total = total + part[...]
-    total = jnp.broadcast_to(jnp.sum(total, axis=1, keepdims=True), total.shape) / cells
+    total = jnp.broadcast_to(jnp.sum(total, axis=1, keepdims=True), total.shape)
+    total = total * (FINAL * FINAL / cells)
     entry = {}
     for index, pair in enumerate(pairs):
         entry[pair] = total[index : index + 1, :]
@@ -476,8 +522,8 @@
             for inner in range(line):
                 value = value - upper[inner, line] * upper[inner, column]
             if column == line:
-                upper[line, line] = jnp.sqrt(value)
-                inv[line, line] = 1.0 / upper[line, line]
+                inv[line, line] = lax.rsqrt(value)
+                upper[line, line] = value * inv[line, line]
             else:
                 upper[line, column] = value * inv[line, line]
     for column in range(orbs):
@@ -493,7 +539,7 @@
         there = (row == line) & (col == column)
         whole = jnp.where(there, jnp.broadcast_to(value, whole.shape), whole)
     factor[...] = whole[:orbs, :orbs]
-    gains = {pair: jnp.broadcast_to(inv[pair], (TILE, LANES)) for pair in pairs}
+    gains = {pair: jnp.broadcast_to(inv[pair] * FINAL, (TILE, LANES)) for pair in pairs}
 
     half = ny // TILE // 2
     pieces = [(plane, part) for plane in range(chunk) for part in (0, half)]
@@ -575,23 +621,19 @@
     )
     orbitals = pltpu.with_memory_space_constraint(orbitals, pltpu.HBM)
     potential = pltpu.with_memory_space_constraint(potential, pltpu.HBM)
-    x_faces = faces_x(orbitals)
-    x_faces, orbitals = lax.optimization_barrier((x_faces, orbitals))
-    field, weight, *y_faces, packed = load(orbitals, potential)
+    field, weight, *faces, packed = load(orbitals, potential)
     before = None
     for level in range(3):
         last = level == 2
-        halo_x = [swap(face, "gx", parity) for parity, face in enumerate(x_faces)]
-        halo_y = [swap(face, "gy", parity) for parity, face in enumerate(y_faces)]
+        halos = []
+        for axis, (even, odd) in (("gx", faces[:2]), ("gy", faces[2:])):
+            halos += [swap(odd, axis, 1), swap(even, axis, 0)]
         z_even, z_odd = swap(packed, "gz", 0), swap(packed, "gz", 1)
-        after, *packed = step(field, weight, z_even, z_odd, before, last)
-        packed = None if last else packed[0]
-        edge = EDGE * (0.5 if level == 0 else 1.0)
-        after, *faces = edges(after, packed, nx, ny, (*halo_x, *halo_y), edge, last)
-        if not last:
-            x_faces, y_faces, packed = faces[:2], faces[2:4], faces[4]
+        after, *extra = step(field, weight, z_even, z_odd, before, BACK[level], last)
+        extra = products_inside(after, nx, ny) if last else extra[0]
+        after, *faces, packed = edges(after, extra, nx, ny, [halos[1], halos[2], halos[3], halos[0]], last)
         before, field = field, after
-    local = gram(field, nx, ny)
+    local = packed
     for axis in ("gz", "gy"):
         for part in exchanges(local, axis):
             local = local + part

time: 78 us -> 75 us (0.962)
  Pallas kernels: 37.3 us -> 34.9 us
  waiting for transfers between devices: 8.23 us -> 6.73 us
  starting transfers between devices: 31.3 us -> 32.3 us
    pallas_call x8 -> x7, Pallas kernels: 28.1 us -> 25.9 us  [the longest x3 21.8 us: step(): pl.pallas_call(functools.partial(step_kernel, nx, ny, back, last), out_sh...]
    ppermute x15, starting transfers between devices: 21.4 us -> 23.6 us  [swap(): return lax.ppermute(array, axis, pairs)]
    ppermute x7, waiting for transfers between devices: 8.19 us -> 6.69 us  [exchanges(): return [lax.ppermute(array, axis, move) for move in moves]]
    ppermute x7, starting transfers between devices: 9.87 us -> 8.71 us  [exchanges(): return [lax.ppermute(array, axis, move) for move in moves]]
  transfers between devices with their start and end apart: 22 -> 22, of which waited for: 6 -> 6; matrix products, arithmetic and copies ran while one was open for 0% -> 0% of each run, Pallas kernels for 29% -> 31%
where the time goes in v3:
time: 75 us; the launch traced here: 74.8 us
  Pallas kernels  34.9 us (47%)
  starting transfers between devices  32.3 us (43%)
  waiting for transfers between devices  6.73 us (9%)
  between operations  0.89 us (1%)
    ppermute x15, starting transfers between devices, swap(): return lax.ppermute(array, axis, pairs)  23.6 us
    pallas_call x3, Pallas kernels, step(): pl.pallas_call(functools.partial(step_kernel, nx, ny, back, last), out_sh...  21.8 us
    ppermute x7, starting transfers between devices, exchanges(): return [lax.ppermute(array, axis, move) for move in moves]  8.71 us
    ppermute x7, waiting for transfers between devices, exchanges(): return [lax.ppermute(array, axis, move) for move in moves]  6.69 us
    pallas_call x1, Pallas kernels, load(): pl.pallas_call(functools.partial(load_kernel, nx, ny), out_shape=(vmem_ou...  4.75 us
    pallas_call x1, Pallas kernels, basis(): pl.pallas_call(functools.partial(basis_kernel, nx, ny, chunk, cells, len(...  4.2 us
    pallas_call x3, Pallas kernels, edges(): pl.pallas_call(functools.partial(edges_kernel, nx, ny, last), out_shape=t...  2.9 us
  transfers between devices with their start and end apart: 22, of which 6 were waited for; matrix products, arithmetic and copies ran while one was open for 0% of the time, Pallas kernels for 31%

profile of v3, /device:TPU:0, one launch (start us, length us, event | category | flops | bytes accessed | tf_op | source)
XLA Modules:
  0.0 74.8 jit_solution(16860712787016233129)
XLA Ops:
  0.6 4.8 %load.1 = (f32[4,68,72,128]{3,2,1,0:T(8,128)S(1)}, f32[64,64,128]{2,1,0:T(8,128)S(1)}, f32[4,2,64,128]{3,2,1,0:T(8,128)S(1)}, f32[4,2,64,128]{3,2,1,0:T(8,128)S(...) custom-call(f32[4,64,64,128]{3,2,1,0:T(8,128)} %field.1, ...), custom_call_target="tpu_custom_call" | custom-call | flops 1 | bytes 1 | tf_op jit(solution)/shard_map/load/pallas_call | solution.py:149
  5.4 0.5 collective-permute-start
  5.9 2.6 %collective-permute-start.1 = (f32[4,2,64,128]{3,2,1,0:T(8,128)S(1)}, f32[4,2,64,128]{3,2,1,0:T(8,128)S(1)}, u32[]{:S(2)}, u32[]{:S(2)}) collective-permute-start(f32[4,2,64,128]{3,2,1,0:T(8,128)S(1)} %get-tuple-element.31), channel_id=1, source_target_pairs={{0,8},{8,0},{16,24},{24,16},{1,9},{9,1},{17,25},{25,17},{2,10},{10... | collective-permute-start | bytes 786440 | tf_op jit(solution)/shard_map/ppermute | solution.py:52
  8.5 0.7 collective-permute-start.2
  9.1 4.4 %collective-permute-start.3 = (f32[4,2,64,128]{3,2,1,0:T(8,128)S(1)}, f32[4,2,64,128]{3,2,1,0:T(8,128)S(1)}, u32[]{:S(2)}, u32[]{:S(2)}) collective-permute-start(f32[4,2,64,128]{3,2,1,0:T(8,128)S(1)} %get-tuple-element.33), channel_id=1, source_target_pairs={{0,2},{2,0},{4,6},{6,4},{1,3},{3,1},{5,7},{7,5},{8,10},{10,8},{12,... | collective-permute-start | bytes 786440 | tf_op jit(solution)/shard_map/ppermute | solution.py:52
  13.6 0.7 collective-permute-start.4
  14.3 7.2 %step.3 = (f32[4,68,72,128]{3,2,1,0:T(8,128)S(1)}, f32[4,2,64,128]{3,2,1,0:T(8,128)S(1)}) custom-call(f32[4,68,72,128]{3,2,1,0:T(8,128)S(1)} %get-tuple-element.27.field.rest_0_, f32[64,64,128]{2,1,0:T(8,128)S(1)} %get-tuple-element.28.weight, f32[4,2,64,128]{3,2,1,0:T(8,128)S(1)} %collective-permute-done.z_even, f32[4,2,64,128]{3,2,1,0:T(8,128)S(1)} %broadcast_1_z_odd.2.z_odd), custom_call_target="tpu_custom_call" | custom-call | flops 1 | bytes 1 | tf_op jit(solution)/shard_map/step/pallas_call | solution.py:302
  21.6 1.0 %edges.3 = (f32[4,68,72,128]{3,2,1,0:T(8,128)S(1)}, f32[4,2,64,128]{3,2,1,0:T(8,128)S(1)}, f32[4,2,64,128]{3,2,1,0:T(8,128)S(1)}, f32[4,2,64,128]{3,2,1,0:T(8,12...) custom-call(f32[4,68,72,128]{3,2,1,0:T(8,128)S(1)} %get-tuple-elemen, ...), custom_call_target="tpu_custom_call", output_to_operand_aliasing={{0}: (0, {}), {5}: (5, {})} | custom-call | flops 1 | bytes 1 | tf_op jit(solution)/shard_map/edges/pallas_call | solution.py:447
  22.6 4.3 %collective-permute-start.6 = (f32[4,2,64,128]{3,2,1,0:T(8,128)S(1)}, f32[4,2,64,128]{3,2,1,0:T(8,128)S(1)}, u32[]{:S(2)}, u32[]{:S(2)}) collective-permute-start(f32[4,2,64,128]{3,2,1,0:T(8,128)S(1)} %get-tuple-element.39), channel_id=1, source_target_pairs={{0,8},{8,0},{16,24},{24,16},{1,9},{9,1},{17,25},{25,17},{2,10},{10... | collective-permute-start | bytes 786440 | tf_op jit(solution)/shard_map/ppermute | solution.py:52
  26.9 0.7 collective-permute-start.7
  27.6 2.3 %collective-permute-start.8 = (f32[4,2,64,128]{3,2,1,0:T(8,128)S(1)}, f32[4,2,64,128]{3,2,1,0:T(8,128)S(1)}, u32[]{:S(2)}, u32[]{:S(2)}) collective-permute-start(f32[4,2,64,128]{3,2,1,0:T(8,128)S(1)} %get-tuple-element.41), channel_id=1, source_target_pairs={{0,2},{2,0},{4,6},{6,4},{1,3},{3,1},{5,7},{7,5},{8,10},{10,8},{12,... | collective-permute-start | bytes 786440 | tf_op jit(solution)/shard_map/ppermute | solution.py:52
  29.9 0.7 collective-permute-start.9
  30.6 7.5 %step.4 = (f32[4,68,72,128]{3,2,1,0:T(8,128)S(1)}, f32[4,2,64,128]{3,2,1,0:T(8,128)S(1)}) custom-call(f32[4,68,72,128]{3,2,1,0:T(8,128)S(1)} %get-tuple-element.36.field.rest_0_, f32[64,64,128]{2,1,0:T(8,128)S(1)} %get-tuple-element.28.weight, f32[4,2,64,128]{3,2,1,0:T(8,128)S(1)} %collective-permute-done.5.z_even, ...), custom_call_target="tpu_custom_call", output_to_operand_aliasing={{0}: (4, {})} | custom-call | flops 1 | bytes 1 | tf_op jit(solution)/shard_map/step/pallas_call | solution.py:302
  38.2 1.0 %edges.4 = (f32[4,68,72,128]{3,2,1,0:T(8,128)S(1)}, f32[4,2,64,128]{3,2,1,0:T(8,128)S(1)}, f32[4,2,64,128]{3,2,1,0:T(8,128)S(1)}, f32[4,2,64,128]{3,2,1,0:T(8,12...) custom-call(f32[4,68,72,128]{3,2,1,0:T(8,128)S(1)} %get-tuple-elemen, ...), custom_call_target="tpu_custom_call", output_to_operand_aliasing={{0}: (0, {}), {5}: (5, {})} | custom-call | flops 1 | bytes 1 | tf_op jit(solution)/shard_map/edges/pallas_call | solution.py:447
  39.2 2.7 %collective-permute-start.11 = (f32[4,2,64,128]{3,2,1,0:T(8,128)S(1)}, f32[4,2,64,128]{3,2,1,0:T(8,128)S(1)}, u32[]{:S(2)}, u32[]{:S(2)}) collective-permute-start(f32[4,2,64,128]{3,2,1,0:T(8,128)S(1)} %get-tuple-element.46), channel_id=1, source_target_pairs={{0,8},{8,0},{16,24},{24,16},{1,9},{9,1},{17,25},{25,17},{2,10},{10... | collective-permute-start | bytes 786440 | tf_op jit(solution)/shard_map/ppermute | solution.py:52
  41.9 0.7 collective-permute-start.12
  42.6 2.6 %collective-permute-start.13 = (f32[4,2,64,128]{3,2,1,0:T(8,128)S(1)}, f32[4,2,64,128]{3,2,1,0:T(8,128)S(1)}, u32[]{:S(2)}, u32[]{:S(2)}) collective-permute-start(f32[4,2,64,128]{3,2,1,0:T(8,128)S(1)} %get-tuple-element.48), channel_id=1, source_target_pairs={{0,2},{2,0},{4,6},{6,4},{1,3},{3,1},{5,7},{7,5},{8,10},{10,8},{12,... | collective-permute-start | bytes 786440 | tf_op jit(solution)/shard_map/ppermute | solution.py:52
  45.2 0.7 collective-permute-start.14
  45.9 7.0 %step.5.field = f32[4,68,72,128]{3,2,1,0:T(8,128)S(1)} custom-call(f32[4,68,72,128]{3,2,1,0:T(8,128)S(1)} %get-tuple-element.44.field, f32[64,64,128]{2,1,0:T(8,128)S(1)} %get-tuple-element.28.weight, f32[4,2,64,128]{3,2,1,0:T(8,128)S(1)} %collective-permute-done.10.z_even, ...), custom_call_target="tpu_custom_call", output_to_operand_aliasing={{}: (4, {})} | custom-call | flops 1 | bytes 1 | tf_op jit(solution)/shard_map/step/pallas_call | solution.py:302
  52.9 1.2 %products.1.extra = f32[16,128]{1,0:T(8,128)S(1)} custom-call(f32[4,68,72,128]{3,2,1,0:T(8,128)S(1)} %step.5.field), custom_call_target="tpu_custom_call" | custom-call | flops 1 | bytes 1 | tf_op jit(solution)/shard_map/products/pallas_call | solution.py:492
  54.2 1.0 %edges.5 = (f32[4,68,72,128]{3,2,1,0:T(8,128)S(1)}, f32[16,128]{1,0:T(8,128)S(1)}) custom-call(f32[4,68,72,128]{3,2,1,0:T(8,128)S(1)} %step.5.field, f32[4,2,64,128]{3,2,1,0:T(8,128)S(1)} %collective-permute-done.11.x_even, f32[4,2,64,128]{3,2,1,0:T(8,128)S(1)} %collective-permute-done.12.y_odd, ...), custom_call_target="tpu_custom_call", output_to_operand_aliasing={{0}: (0, {})} | custom-call | flops 1 | bytes 1 | tf_op jit(solution)/shard_map/edges/pallas_call | solution.py:447
  55.3 1.2 %collective-permute-done.15 = f32[16,128]{1,0:T(8,128)S(1)} collective-permute-done((f32[16,128]{1,0:T(8,128)S(1)}, f32[16,128]{1,0:T(8,128)S(1)}, u32[]{:S(2)}, u32[]{:S(2)}) %collective-permute-start.15) | collective-permute-done | bytes 8224 | tf_op jit(solution)/shard_map/ppermute | solution.py:611
  56.4 1.9 %collective-permute-start.18 = (f32[16,128]{1,0:T(8,128)S(1)}, f32[16,128]{1,0:T(8,128)S(1)}, u32[]{:S(2)}, u32[]{:S(2)}) collective-permute-start(f32[16,128]{1,0:T(8,128)S(1)} %add.12), channel_id=1, source_target_pairs={{0,6},{2,4},{4,2},{6,0},{1,7},{3,5},{5,3},{7,1},{8,14},{10,12},{12... | collective-permute-start | bytes 24584 | tf_op jit(solution)/shard_map/ppermute | solution.py:611
  58.3 2.5 %collective-permute-start.16 = (f32[16,128]{1,0:T(8,128)S(1)}, f32[16,128]{1,0:T(8,128)S(1)}, u32[]{:S(2)}, u32[]{:S(2)}) collective-permute-start(f32[16,128]{1,0:T(8,128)S(1)} %add.12), channel_id=1, source_target_pairs={{0,2},{2,0},{4,6},{6,4},{1,3},{3,1},{5,7},{7,5},{8,10},{10,8},{12,... | collective-permute-start | bytes 24584 | tf_op jit(solution)/shard_map/ppermute | solution.py:611
  60.8 1.1 %collective-permute-done.18 = f32[16,128]{1,0:T(8,128)S(1)} collective-permute-done((f32[16,128]{1,0:T(8,128)S(1)}, f32[16,128]{1,0:T(8,128)S(1)}, u32[]{:S(2)}, u32[]{:S(2)}) %collective-permute-start.18) | collective-permute-done | bytes 8224 | tf_op jit(solution)/shard_map/ppermute | solution.py:611
  61.9 1.0 %collective-permute-done.17 = f32[16,128]{1,0:T(8,128)S(1)} collective-permute-done((f32[16,128]{1,0:T(8,128)S(1)}, f32[16,128]{1,0:T(8,128)S(1)}, u32[]{:S(2)}, u32[]{:S(2)}) %collective-permute-start.17) | collective-permute-done | bytes 8224 | tf_op jit(solution)/shard_map/ppermute | solution.py:611
  62.9 1.3 %collective-permute-start.21 = (f32[16,128]{1,0:T(8,128)S(1)}, f32[16,128]{1,0:T(8,128)S(1)}, u32[]{:S(2)}, u32[]{:S(2)}) collective-permute-start(f32[16,128]{1,0:T(8,128)S(1)} %add_add_fusion.rest_0_), channel_id=1, source_target_pairs={{0,24},{8,16},{16,8},{24,0},{1,25},{9,17},{17,9},{25,1},{2,26},{10... | collective-permute-start | bytes 24584 | tf_op jit(solution)/shard_map/ppermute | solution.py:611
  64.2 2.7 %collective-permute-start.20 = (f32[16,128]{1,0:T(8,128)S(1)}, f32[16,128]{1,0:T(8,128)S(1)}, u32[]{:S(2)}, u32[]{:S(2)}) collective-permute-start(f32[16,128]{1,0:T(8,128)S(1)} %add_add_fusion.rest_0_), channel_id=1, source_target_pairs={{0,16},{8,24},{16,0},{24,8},{1,17},{9,25},{17,1},{25,9},{2,18},{10... | collective-permute-start | bytes 24584 | tf_op jit(solution)/shard_map/ppermute | solution.py:611
  67.1 0.4 collective-permute-done.21.rest_3_
  67.5 1.1 %collective-permute-done.20.rest_2_ = f32[16,128]{1,0:T(8,128)S(1)} collective-permute-done((f32[16,128]{1,0:T(8,128)S(1)}, f32[16,128]{1,0:T(8,128)S(1)}, u32[]{:S(2)}, u32[]{:S(2)}) %collective-permute-start.20) | collective-permute-done | bytes 8224 | tf_op jit(solution)/shard_map/ppermute | solution.py:611
  68.6 2.0 %collective-permute-done.19.rest_1_ = f32[16,128]{1,0:T(8,128)S(1)} collective-permute-done((f32[16,128]{1,0:T(8,128)S(1)}, f32[16,128]{1,0:T(8,128)S(1)}, u32[]{:S(2)}, u32[]{:S(2)}) %collective-permute-start.19) | collective-permute-done | bytes 8224 | tf_op jit(solution)/shard_map/ppermute | solution.py:611
  70.6 4.2 %basis.1 = (f32[4,64,64,128]{3,2,1,0:T(8,128)}, f32[4,4]{1,0:T(4,128)}) custom-call(f32[4,68,72,128]{3,2,1,0:T(8,128)S(1)} %get-tuple-element.50.field, f32[16,128]{1,0:T(8,128)S(1)} %add_add_fusion.rest_0_, f32[16,128]{1,0:T(8,128)S(1)} %collective-permute-done.19.rest_1_, f32[16,128]{1,0:T(8,128)S(1)} %collective-permute-done.20.rest_2_, ...), custom_call_target="tpu_custom_call" | custom-call | flops 1 | bytes 1 | tf_op jit(solution)/shard_map/basis/pallas_call | solution.py:587
  (24 shorter events, 0.5 us)
Async XLA Ops:
  5.4 8.9 %collective-permute-start = (f32[4,2,64,128]{3,2,1,0:T(8,128)S(1)}, f32[4,2,64,128]{3,2,1,0:T(8,128)S(1)}, u32[]{:S(2)}, u32[]{:S(2)}) collective-permute-start(f32[4,2,64,128]{3,2,1,0:T(8,128)S(1)} %get-tuple-element.29), channel_id=1, source_target_pairs={{0,1},{1,0},{2,3},{3,2},{4,5},{5,4},{6,7},{7,6},{8,9},{9,8},{10,11... | collective-permute-start | bytes 786440 | tf_op jit(solution)/shard_map/ppermute | solution.py:52
  5.9 15.7 %collective-permute-start.1 = (f32[4,2,64,128]{3,2,1,0:T(8,128)S(1)}, f32[4,2,64,128]{3,2,1,0:T(8,128)S(1)}, u32[]{:S(2)}, u32[]{:S(2)}) collective-permute-start(f32[4,2,64,128]{3,2,1,0:T(8,128)S(1)} %get-tuple-element.31), channel_id=1, source_target_pairs={{0,8},{8,0},{16,24},{24,16},{1,9},{9,1},{17,25},{25,17},{2,10},{10... | collective-permute-start | bytes 786440 | tf_op jit(solution)/shard_map/ppermute | solution.py:52
  8.5 13.1 %collective-permute-start.2 = (f32[4,2,64,128]{3,2,1,0:T(8,128)S(1)}, f32[4,2,64,128]{3,2,1,0:T(8,128)S(1)}, u32[]{:S(2)}, u32[]{:S(2)}) collective-permute-start(f32[4,2,64,128]{3,2,1,0:T(8,128)S(1)} %get-tuple-element.32), channel_id=1, source_target_pairs={{2,4},{4,2},{3,5},{5,3},{10,12},{12,10},{11,13},{13,11},{18,20},{2... | collective-permute-start | bytes 786440 | tf_op jit(solution)/shard_map/ppermute | solution.py:52
  9.1 12.4 %collective-permute-start.3 = (f32[4,2,64,128]{3,2,1,0:T(8,128)S(1)}, f32[4,2,64,128]{3,2,1,0:T(8,128)S(1)}, u32[]{:S(2)}, u32[]{:S(2)}) collective-permute-start(f32[4,2,64,128]{3,2,1,0:T(8,128)S(1)} %get-tuple-element.33), channel_id=1, source_target_pairs={{0,2},{2,0},{4,6},{6,4},{1,3},{3,1},{5,7},{7,5},{8,10},{10,8},{12,... | collective-permute-start | bytes 786440 | tf_op jit(solution)/shard_map/ppermute | solution.py:52
  13.6 8.0 %collective-permute-start.4 = (f32[4,2,64,128]{3,2,1,0:T(8,128)S(1)}, f32[4,2,64,128]{3,2,1,0:T(8,128)S(1)}, u32[]{:S(2)}, u32[]{:S(2)}) collective-permute-start(f32[4,2,64,128]{3,2,1,0:T(8,128)S(1)} %get-tuple-element.34), channel_id=1, source_target_pairs={{8,16},{16,8},{9,17},{17,9},{10,18},{18,10},{11,19},{19,11},{12,20... | collective-permute-start | bytes 786440 | tf_op jit(solution)/shard_map/ppermute | solution.py:52
  22.6 8.0 %collective-permute-start.5 = (f32[4,2,64,128]{3,2,1,0:T(8,128)S(1)}, f32[4,2,64,128]{3,2,1,0:T(8,128)S(1)}, u32[]{:S(2)}, u32[]{:S(2)}) collective-permute-start(f32[4,2,64,128]{3,2,1,0:T(8,128)S(1)} %get-tuple-element.37), channel_id=1, source_target_pairs={{0,1},{1,0},{2,3},{3,2},{4,5},{5,4},{6,7},{7,6},{8,9},{9,8},{10,11... | collective-permute-start | bytes 786440 | tf_op jit(solution)/shard_map/ppermute | solution.py:52
  22.6 15.5 %collective-permute-start.6 = (f32[4,2,64,128]{3,2,1,0:T(8,128)S(1)}, f32[4,2,64,128]{3,2,1,0:T(8,128)S(1)}, u32[]{:S(2)}, u32[]{:S(2)}) collective-permute-start(f32[4,2,64,128]{3,2,1,0:T(8,128)S(1)} %get-tuple-element.39), channel_id=1, source_target_pairs={{0,8},{8,0},{16,24},{24,16},{1,9},{9,1},{17,25},{25,17},{2,10},{10... | collective-permute-start | bytes 786440 | tf_op jit(solution)/shard_map/ppermute | solution.py:52
  26.9 11.2 %collective-permute-start.7 = (f32[4,2,64,128]{3,2,1,0:T(8,128)S(1)}, f32[4,2,64,128]{3,2,1,0:T(8,128)S(1)}, u32[]{:S(2)}, u32[]{:S(2)}) collective-permute-start(f32[4,2,64,128]{3,2,1,0:T(8,128)S(1)} %get-tuple-element.40), channel_id=1, source_target_pairs={{2,4},{4,2},{3,5},{5,3},{10,12},{12,10},{11,13},{13,11},{18,20},{2... | collective-permute-start | bytes 786440 | tf_op jit(solution)/shard_map/ppermute | solution.py:52
  27.6 10.6 %collective-permute-start.8 = (f32[4,2,64,128]{3,2,1,0:T(8,128)S(1)}, f32[4,2,64,128]{3,2,1,0:T(8,128)S(1)}, u32[]{:S(2)}, u32[]{:S(2)}) collective-permute-start(f32[4,2,64,128]{3,2,1,0:T(8,128)S(1)} %get-tuple-element.41), channel_id=1, source_target_pairs={{0,2},{2,0},{4,6},{6,4},{1,3},{3,1},{5,7},{7,5},{8,10},{10,8},{12,... | collective-permute-start | bytes 786440 | tf_op jit(solution)/shard_map/ppermute | solution.py:52
  29.9 8.2 %collective-permute-start.9 = (f32[4,2,64,128]{3,2,1,0:T(8,128)S(1)}, f32[4,2,64,128]{3,2,1,0:T(8,128)S(1)}, u32[]{:S(2)}, u32[]{:S(2)}) collective-permute-start(f32[4,2,64,128]{3,2,1,0:T(8,128)S(1)} %get-tuple-element.42), channel_id=1, source_target_pairs={{8,16},{16,8},{9,17},{17,9},{10,18},{18,10},{11,19},{19,11},{12,20... | collective-permute-start | bytes 786440 | tf_op jit(solution)/shard_map/ppermute | solution.py:52
  39.1 6.7 %collective-permute-start.10 = (f32[4,2,64,128]{3,2,1,0:T(8,128)S(1)}, f32[4,2,64,128]{3,2,1,0:T(8,128)S(1)}, u32[]{:S(2)}, u32[]{:S(2)}) collective-permute-start(f32[4,2,64,128]{3,2,1,0:T(8,128)S(1)} %get-tuple-element.45), channel_id=1, source_target_pairs={{0,1},{1,0},{2,3},{3,2},{4,5},{5,4},{6,7},{7,6},{8,9},{9,8},{10,11... | collective-permute-start | bytes 786440 | tf_op jit(solution)/shard_map/ppermute | solution.py:52
  39.2 14.9 %collective-permute-start.11 = (f32[4,2,64,128]{3,2,1,0:T(8,128)S(1)}, f32[4,2,64,128]{3,2,1,0:T(8,128)S(1)}, u32[]{:S(2)}, u32[]{:S(2)}) collective-permute-start(f32[4,2,64,128]{3,2,1,0:T(8,128)S(1)} %get-tuple-element.46), channel_id=1, source_target_pairs={{0,8},{8,0},{16,24},{24,16},{1,9},{9,1},{17,25},{25,17},{2,10},{10... | collective-permute-start | bytes 786440 | tf_op jit(solution)/shard_map/ppermute | solution.py:52
  41.9 12.2 %collective-permute-start.12 = (f32[4,2,64,128]{3,2,1,0:T(8,128)S(1)}, f32[4,2,64,128]{3,2,1,0:T(8,128)S(1)}, u32[]{:S(2)}, u32[]{:S(2)}) collective-permute-start(f32[4,2,64,128]{3,2,1,0:T(8,128)S(1)} %get-tuple-element.47), channel_id=1, source_target_pairs={{2,4},{4,2},{3,5},{5,3},{10,12},{12,10},{11,13},{13,11},{18,20},{2... | collective-permute-start | bytes 786440 | tf_op jit(solution)/shard_map/ppermute | solution.py:52
  42.6 11.6 %collective-permute-start.13 = (f32[4,2,64,128]{3,2,1,0:T(8,128)S(1)}, f32[4,2,64,128]{3,2,1,0:T(8,128)S(1)}, u32[]{:S(2)}, u32[]{:S(2)}) collective-permute-start(f32[4,2,64,128]{3,2,1,0:T(8,128)S(1)} %get-tuple-element.48), channel_id=1, source_target_pairs={{0,2},{2,0},{4,6},{6,4},{1,3},{3,1},{5,7},{7,5},{8,10},{10,8},{12,... | collective-permute-start | bytes 786440 | tf_op jit(solution)/shard_map/ppermute | solution.py:52
  45.2 9.0 %collective-permute-start.14 = (f32[4,2,64,128]{3,2,1,0:T(8,128)S(1)}, f32[4,2,64,128]{3,2,1,0:T(8,128)S(1)}, u32[]{:S(2)}, u32[]{:S(2)}) collective-permute-start(f32[4,2,64,128]{3,2,1,0:T(8,128)S(1)} %get-tuple-element.49), channel_id=1, source_target_pairs={{8,16},{16,8},{9,17},{17,9},{10,18},{18,10},{11,19},{19,11},{12,20... | collective-permute-start | bytes 786440 | tf_op jit(solution)/shard_map/ppermute | solution.py:52
  55.2 1.2 %collective-permute-start.15 = (f32[16,128]{1,0:T(8,128)S(1)}, f32[16,128]{1,0:T(8,128)S(1)}, u32[]{:S(2)}, u32[]{:S(2)}) collective-permute-start(f32[16,128]{1,0:T(8,128)S(1)} %get-tuple-element.51), channel_id=1, source_target_pairs={{0,1},{1,0},{2,3},{3,2},{4,5},{5,4},{6,7},{7,6},{8,9},{9,8},{10,11... | collective-permute-start | bytes 24584 | tf_op jit(solution)/shard_map/ppermute | solution.py:611
  56.4 5.5 %collective-permute-start.18 = (f32[16,128]{1,0:T(8,128)S(1)}, f32[16,128]{1,0:T(8,128)S(1)}, u32[]{:S(2)}, u32[]{:S(2)}) collective-permute-start(f32[16,128]{1,0:T(8,128)S(1)} %add.12), channel_id=1, source_target_pairs={{0,6},{2,4},{4,2},{6,0},{1,7},{3,5},{5,3},{7,1},{8,14},{10,12},{12... | collective-permute-start | bytes 24584 | tf_op jit(solution)/shard_map/ppermute | solution.py:611
  58.3 4.5 %collective-permute-start.17 = (f32[16,128]{1,0:T(8,128)S(1)}, f32[16,128]{1,0:T(8,128)S(1)}, u32[]{:S(2)}, u32[]{:S(2)}) collective-permute-start(f32[16,128]{1,0:T(8,128)S(1)} %add.12), channel_id=1, source_target_pairs={{0,4},{2,6},{4,0},{6,2},{1,5},{3,7},{5,1},{7,3},{8,12},{10,14},{12... | collective-permute-start | bytes 24584 | tf_op jit(solution)/shard_map/ppermute | solution.py:611
  58.3 4.5 %collective-permute-start.16 = (f32[16,128]{1,0:T(8,128)S(1)}, f32[16,128]{1,0:T(8,128)S(1)}, u32[]{:S(2)}, u32[]{:S(2)}) collective-permute-start(f32[16,128]{1,0:T(8,128)S(1)} %add.12), channel_id=1, source_target_pairs={{0,2},{2,0},{4,6},{6,4},{1,3},{3,1},{5,7},{7,5},{8,10},{10,8},{12,... | collective-permute-start | bytes 24584 | tf_op jit(solution)/shard_map/ppermute | solution.py:611
  62.9 4.6 %collective-permute-start.21 = (f32[16,128]{1,0:T(8,128)S(1)}, f32[16,128]{1,0:T(8,128)S(1)}, u32[]{:S(2)}, u32[]{:S(2)}) collective-permute-start(f32[16,128]{1,0:T(8,128)S(1)} %add_add_fusion.rest_0_), channel_id=1, source_target_pairs={{0,24},{8,16},{16,8},{24,0},{1,25},{9,17},{17,9},{25,1},{2,26},{10... | collective-permute-start | bytes 24584 | tf_op jit(solution)/shard_map/ppermute | solution.py:611
  64.2 4.3 %collective-permute-start.20 = (f32[16,128]{1,0:T(8,128)S(1)}, f32[16,128]{1,0:T(8,128)S(1)}, u32[]{:S(2)}, u32[]{:S(2)}) collective-permute-start(f32[16,128]{1,0:T(8,128)S(1)} %add_add_fusion.rest_0_), channel_id=1, source_target_pairs={{0,16},{8,24},{16,0},{24,8},{1,17},{9,25},{17,1},{25,9},{2,18},{10... | collective-permute-start | bytes 24584 | tf_op jit(solution)/shard_map/ppermute | solution.py:611
  67.0 3.7 %collective-permute-start.19 = (f32[16,128]{1,0:T(8,128)S(1)}, f32[16,128]{1,0:T(8,128)S(1)}, u32[]{:S(2)}, u32[]{:S(2)}) collective-permute-start(f32[16,128]{1,0:T(8,128)S(1)} %add_add_fusion.rest_0_), channel_id=1, source_target_pairs={{0,8},{8,0},{16,24},{24,16},{1,9},{9,1},{17,25},{25,17},{2,10},{10... | collective-permute-start | bytes 24584 | tf_op jit(solution)/shard_map/ppermute | solution.py:611

commit v4 on v3

--- a/solution.py
+++ b/solution.py
@@ -16,6 +16,7 @@
 TILE = 8
 PAD = 8
 PER = LANES // 4
+BATCH = 8
 VMEM_LIMIT = 8 * 1024 * 1024
 
 
@@ -70,15 +71,33 @@
     return moved if total is None else jnp.where(lane // 4 == plane, moved, total)
 
 
+class Packer:
+    def __init__(self):
+        self.parts = []
+        self.plane = 0
+
+    def add(self, rows):
+        lane = lax.broadcasted_iota(jnp.int32, rows.shape, 1)
+        part, width = pltpu.roll(rows, (4 * self.plane + 2) % LANES, 1), 4
+        while self.parts and self.parts[-1][1] == width:
+            part = jnp.where(lane % (2 * width) < width, self.parts.pop()[0], part)
+            width *= 2
+        self.parts.append((part, width))
+        self.plane += 1
+
+    def total(self):
+        ((part, _),) = self.parts
+        return part
+
+
 def pack_z_tiles(flat, packed, pitch, orb, group, tiles):
-    totals = [None] * len(tiles)
+    packers = [Packer() for _ in tiles]
     for plane in range(PER):
-        for number, tile in enumerate(tiles):
+        for packer, tile in zip(packers, tiles):
             start = pl.multiple_of((group * PER + plane + 2) * pitch + tile * TILE, TILE)
-            rows = flat[orb, pl.ds(start, TILE), :]
-            totals[number] = pack_z_lanes(rows, plane, totals[number])
-    for number, tile in enumerate(tiles):
-        packed[orb, group, pl.ds(tile * TILE, TILE), :] = totals[number]
+            packer.add(flat[orb, pl.ds(start, TILE), :])
+    for packer, tile in zip(packers, tiles):
+        packed[orb, group, pl.ds(tile * TILE, TILE), :] = packer.total()
 
 
 def pack_x(flat, even, odd, pitch, nx, ny, orb, flip):
@@ -90,12 +109,13 @@
 
 
 def load_kernel(
-    nx, ny, field, potential, out, weight, x_even, x_odd, y_even, y_odd, packed, sems
+    nx, ny, field, potential, out, weight, x_even, x_odd, y_even, y_odd, packed, blank, mix, sems
 ):
     orbs = field.shape[0]
     pitch = ny + PAD
     groups = nx // PER
     flat = out.reshape(orbs, (nx + 4) * pitch, LANES)
+    other = blank.reshape(orbs, (nx + 4) * pitch, LANES)
 
     def copy(orb, group):
         return pltpu.make_async_copy(
@@ -112,13 +132,21 @@
     flip_x, flip_y = is_odd("gx"), is_odd("gy")
     zero_planes = jnp.zeros((2 * pitch, LANES), jnp.float32)
     zero_rows = jnp.zeros((PAD, LANES), jnp.float32)
-    for orb in range(orbs):
-        flat[orb, pl.ds(0, 2 * pitch), :] = zero_planes
-        flat[orb, pl.ds((nx + 2) * pitch, 2 * pitch), :] = zero_planes
-
-        @pl.loop(0, nx, unroll=8)
-        def _(x):
-            flat[orb, pl.ds(pl.multiple_of((x + 2) * pitch + ny, TILE), PAD), :] = zero_rows
+    for rows in (flat, other):
+        for orb in range(orbs):
+            rows[orb, pl.ds(0, 2 * pitch), :] = zero_planes
+            rows[orb, pl.ds((nx + 2) * pitch, 2 * pitch), :] = zero_planes
+
+            @pl.loop(0, nx, unroll=8)
+            def _(x):
+                rows[orb, pl.ds(pl.multiple_of((x + 2) * pitch + ny, TILE), PAD), :] = zero_rows
+
+    line = lax.broadcasted_iota(jnp.int32, (LANES, LANES), 0)
+    column = lax.broadcasted_iota(jnp.int32, (LANES, LANES), 1)
+    apart = jnp.abs(line - column)
+    weights = jnp.where(apart == 1, -16.0, jnp.where(apart == 2, 1.0, 0.0)).astype(jnp.bfloat16)
+    mix[pl.ds(0, LANES), :] = weights
+    mix[pl.ds(LANES, LANES), :] = weights
 
     first.wait()
 
@@ -154,9 +182,11 @@
             *[vmem_out((orbs, 2, ny, nz))] * 2,
             *[vmem_out((orbs, 2, nx, nz))] * 2,
             vmem_out((orbs, nx // PER, ny, nz)),
+            vmem_out((orbs, nx + 4, ny + PAD, nz)),
+            pltpu.VMEM((2 * nz, nz), jnp.bfloat16),
         ),
         in_specs=[ANYWHERE, ANYWHERE],
-        out_specs=(WHOLE,) * 7,
+        out_specs=(WHOLE,) * 9,
         scratch_shapes=[pltpu.SemaphoreType.DMA((orbs * (nx // PER) + 1,))],
         compiler_params=params(),
         cost_estimate=LITTLE,
@@ -175,11 +205,9 @@
         ref[there] = value
 
 
-def step_kernel(nx, ny, back, last, field, weight, z_even, z_odd, *rest):
+def step_kernel(nx, ny, back, last, field, weight, mix, z_even, z_odd, before, out, *rest):
     first = back is None
-    rest = rest if first else rest[1:]
-    out, packed = rest[0], None if last else rest[1]
-    correction, mix = rest[-2:]
+    packed, correction = None if last else rest[0], rest[-1]
     orbs = field.shape[0]
     pitch = ny + PAD
     flat = field.reshape(orbs, (nx + 4) * pitch, LANES)
@@ -190,25 +218,6 @@
     place = lax.broadcasted_iota(jnp.int32, (ny, LANES), 1) % 4
     lane = lax.broadcasted_iota(jnp.int32, (TILE, LANES), 1)
     ends = (lane < 2) | (lane >= LANES - 2)
-
-    if first:
-        zero_planes = jnp.zeros((2 * pitch, LANES), jnp.float32)
-        zero_rows = jnp.zeros((PAD, LANES), jnp.float32)
-        for orb in range(orbs):
-            flat_out[orb, pl.ds(0, 2 * pitch), :] = zero_planes
-            flat_out[orb, pl.ds((nx + 2) * pitch, 2 * pitch), :] = zero_planes
-
-            @pl.loop(0, nx, unroll=8)
-            def _(x):
-                there = pl.ds(pl.multiple_of((x + 2) * pitch + ny, TILE), PAD)
-                flat_out[orb, there, :] = zero_rows
-
-    line = lax.broadcasted_iota(jnp.int32, (LANES, LANES), 0)
-    column = lax.broadcasted_iota(jnp.int32, (LANES, LANES), 1)
-    apart = jnp.abs(line - column)
-    weights = jnp.where(apart == 1, -16.0, jnp.where(apart == 2, 1.0, 0.0)).astype(jnp.bfloat16)
-    mix[pl.ds(0, LANES), :] = weights
-    mix[pl.ds(LANES, LANES), :] = weights
 
     def add_beyond(orb, group):
         even, odd = z_even[orb, group], z_odd[orb, group]
@@ -270,45 +279,44 @@
             return flat[orb, pl.ds(start, TILE), :]
 
         inner = not last and 0 < tile < tiles - 1
-        mine = [rows(plane) for plane in range(-2, PER + 2)]
-        values = []
-        total = None
-        for plane in range(PER):
-            near = (mine[plane + 1] + mine[plane + 3]) + (rows(plane, -1) + rows(plane, 1))
-            far = (mine[plane] + mine[plane + 4]) + (rows(plane, -2) + rows(plane, 2))
-            ours = weight[group * PER + plane, pl.ds(tile * TILE, TILE), :]
-            value = ours * mine[plane + 2] + ((far - 16.0 * near) + sums[plane])
-            if not first:
-                start = pl.multiple_of(base + plane * pitch, TILE)
-                value = value - back * flat_out[orb, pl.ds(start, TILE), :]
-            if inner:
-                total = pack_z_lanes(value, plane, total)
-            values.append(value)
-        for plane in range(PER):
-            start = pl.multiple_of(base + plane * pitch, TILE)
-            flat_out[orb, pl.ds(start, TILE), :] = values[plane]
+        mine = {plane: rows(plane) for plane in range(-2, 2)}
+        packer = Packer()
+
+        def some(first_plane):
+            values = []
+            for plane in range(first_plane, first_plane + BATCH):
+                mine[plane + 2] = rows(plane + 2)
+                near = (mine[plane - 1] + mine[plane + 1]) + (rows(plane, -1) + rows(plane, 1))
+                far = (mine[plane - 2] + mine[plane + 2]) + (rows(plane, -2) + rows(plane, 2))
+                ours = weight[group * PER + plane, pl.ds(tile * TILE, TILE), :]
+                value = ours * mine[plane] + ((far - 16.0 * near) + sums[plane])
+                there = pl.ds(pl.multiple_of(base + plane * pitch, TILE), TILE)
+                if not first:
+                    value = value - back * flat_out[orb, there, :]
+                if inner:
+                    packer.add(value)
+                values.append(((orb, there, slice(None)), value))
+            return values
+
+        store_late(flat_out, [(some, plane) for plane in range(0, PER, BATCH)])
         if inner:
-            packed[orb, group, pl.ds(tile * TILE, TILE), :] = total
+            packed[orb, group, pl.ds(tile * TILE, TILE), :] = packer.total()
 
     lax.fori_loop(0, orbs * groups, block, along_z(0, 0))
 
 
-def step(field, weight, z_even, z_odd, before, back, last):
+def step(field, weight, mix, z_even, z_odd, before, back, last):
     orbs = field.shape[0]
     nx, ny, nz = weight.shape
-    first = before is None
-    args = [field, weight, z_even, z_odd] + ([] if first else [before])
+    args = [field, weight, mix, z_even, z_odd, before]
     shapes = [vmem_out(field.shape)] + ([] if last else [vmem_out(z_even.shape)])
     return pl.pallas_call(
         functools.partial(step_kernel, nx, ny, back, last),
         out_shape=tuple(shapes),
         in_specs=[WHOLE] * len(args),
         out_specs=(WHOLE,) * len(shapes),
-        scratch_shapes=[
-            pltpu.VMEM((orbs, nx // PER, ny, nz), jnp.float32),
-            pltpu.VMEM((2 * nz, nz), jnp.bfloat16),
-        ],
-        input_output_aliases={} if first else {4: 0},
+        scratch_shapes=[pltpu.VMEM((orbs, nx // PER, ny, nz), jnp.float32)],
+        input_output_aliases={5: 0},
         compiler_params=params(),
         cost_estimate=LITTLE,
         name="step",
@@ -391,15 +399,14 @@
 
         def border(orb, group):
             ends = (0, tiles - 1)
-            totals = [None] * len(ends)
+            packers = [Packer() for _ in ends]
             for plane in range(PER):
-                for number, tile in enumerate(ends):
+                for packer, tile in zip(packers, ends):
                     start = (group * PER + plane + 2) * pitch + tile * TILE
-                    rows = flat[orb, pl.ds(start, TILE), :]
-                    totals[number] = pack_z_lanes(rows, plane, totals[number])
+                    packer.add(flat[orb, pl.ds(start, TILE), :])
             return [
-                ((orb, group, pl.ds(tile * TILE, TILE), slice(None)), total)
-                for tile, total in zip(ends, totals)
+                ((orb, group, pl.ds(tile * TILE, TILE), slice(None)), packer.total())
+                for packer, tile in zip(packers, ends)
             ]
 
         def planes(orb, group):
@@ -621,15 +628,14 @@
     )
     orbitals = pltpu.with_memory_space_constraint(orbitals, pltpu.HBM)
     potential = pltpu.with_memory_space_constraint(potential, pltpu.HBM)
-    field, weight, *faces, packed = load(orbitals, potential)
-    before = None
+    field, weight, *faces, packed, before, mix = load(orbitals, potential)
     for level in range(3):
         last = level == 2
         halos = []
         for axis, (even, odd) in (("gx", faces[:2]), ("gy", faces[2:])):
             halos += [swap(odd, axis, 1), swap(even, axis, 0)]
         z_even, z_odd = swap(packed, "gz", 0), swap(packed, "gz", 1)
-        after, *extra = step(field, weight, z_even, z_odd, before, BACK[level], last)
+        after, *extra = step(field, weight, mix, z_even, z_odd, before, BACK[level], last)
         extra = products_inside(after, nx, ny) if last else extra[0]
         after, *faces, packed = edges(after, extra, nx, ny, [halos[1], halos[2], halos[3], halos[0]], last)
         before, field = field, after

time: 75 us -> 75.1 us (level)
  transfers between devices with their start and end apart: 22 -> 22, of which waited for: 6 -> 6; matrix products, arithmetic and copies ran while one was open for 0% -> 0% of each run, Pallas kernels for 31% -> 30%
where the time goes in v4:
time: 75.1 us; the launch traced here: 74.8 us
  Pallas kernels  34.6 us (46%)
  starting transfers between devices  32.5 us (43%)
  waiting for transfers between devices  6.77 us (9%)
  between operations  0.9 us (1%)
    ppermute x15, starting transfers between devices, swap(): return lax.ppermute(array, axis, pairs)  23.8 us
    pallas_call x3, Pallas kernels, step(): pl.pallas_call(functools.partial(step_kernel, nx, ny, back, last), out_sh...  21.5 us
    ppermute x7, starting transfers between devices, exchanges(): return [lax.ppermute(array, axis, move) for move in moves]  8.71 us
    ppermute x7, waiting for transfers between devices, exchanges(): return [lax.ppermute(array, axis, move) for move in moves]  6.73 us
    pallas_call x1, Pallas kernels, load(): pl.pallas_call(functools.partial(load_kernel, nx, ny), out_shape=(vmem_ou...  4.81 us
    pallas_call x1, Pallas kernels, basis(): pl.pallas_call(functools.partial(basis_kernel, nx, ny, chunk, cells, len(...  4.2 us
    pallas_call x3, Pallas kernels, edges(): pl.pallas_call(functools.partial(edges_kernel, nx, ny, last), out_shape=t...  2.93 us
  transfers between devices with their start and end apart: 22, of which 6 were waited for; matrix products, arithmetic and copies ran while one was open for 0% of the time, Pallas kernels for 30%

profile of v4, /device:TPU:0, one launch (start us, length us, event | category | flops | bytes accessed | tf_op | source)
XLA Modules:
  0.0 74.8 jit_solution(7555868194471885426)
XLA Ops:
  0.6 4.8 %load.1 = (f32[4,68,72,128]{3,2,1,0:T(8,128)S(1)}, f32[64,64,128]{2,1,0:T(8,128)S(1)}, f32[4,2,64,128]{3,2,1,0:T(8,128)S(1)}, f32[4,2,64,128]{3,2,1,0:T(8,128)S(...) custom-call(f32[4,64,64,128]{3,2,1,0:T(8,128)} %field.1, ...), custom_call_target="tpu_custom_call" | custom-call | flops 1 | bytes 1 | tf_op jit(solution)/shard_map/load/pallas_call | solution.py:177
  5.5 0.5 collective-permute-start
  6.0 2.6 %collective-permute-start.1 = (f32[4,2,64,128]{3,2,1,0:T(8,128)S(1)}, f32[4,2,64,128]{3,2,1,0:T(8,128)S(1)}, u32[]{:S(2)}, u32[]{:S(2)}) collective-permute-start(f32[4,2,64,128]{3,2,1,0:T(8,128)S(1)} %get-tuple-element.35), channel_id=1, source_target_pairs={{0,8},{8,0},{16,24},{24,16},{1,9},{9,1},{17,25},{25,17},{2,10},{10... | collective-permute-start | bytes 786440 | tf_op jit(solution)/shard_map/ppermute | solution.py:53
  8.5 0.7 collective-permute-start.2
  9.2 4.4 %collective-permute-start.3 = (f32[4,2,64,128]{3,2,1,0:T(8,128)S(1)}, f32[4,2,64,128]{3,2,1,0:T(8,128)S(1)}, u32[]{:S(2)}, u32[]{:S(2)}) collective-permute-start(f32[4,2,64,128]{3,2,1,0:T(8,128)S(1)} %get-tuple-element.37), channel_id=1, source_target_pairs={{0,2},{2,0},{4,6},{6,4},{1,3},{3,1},{5,7},{7,5},{8,10},{10,8},{12,... | collective-permute-start | bytes 786440 | tf_op jit(solution)/shard_map/ppermute | solution.py:53
  13.7 0.7 collective-permute-start.4
  14.4 7.0 %step.3 = (f32[4,68,72,128]{3,2,1,0:T(8,128)S(1)}, f32[4,2,64,128]{3,2,1,0:T(8,128)S(1)}) custom-call(f32[4,68,72,128]{3,2,1,0:T(8,128)S(1)} %get-tuple-element.29.field.before, f32[64,64,128]{2,1,0:T(8,128)S(1)} %get-tuple-element.30.weight, bf16[256,128]{1,0:T(8,128)(2,1)S(1)} %get-tuple-element.31.mix, ...), custom_call_target="tpu_custom_call", output_to_operand_aliasing={{0}: (5, {})} | custom-call | flops 1 | bytes 1 | tf_op jit(solution)/shard_map/step/pallas_call | solution.py:313
  21.4 1.0 %edges.3 = (f32[4,68,72,128]{3,2,1,0:T(8,128)S(1)}, f32[4,2,64,128]{3,2,1,0:T(8,128)S(1)}, f32[4,2,64,128]{3,2,1,0:T(8,128)S(1)}, f32[4,2,64,128]{3,2,1,0:T(8,12...) custom-call(f32[4,68,72,128]{3,2,1,0:T(8,128)S(1)} %get-tuple-elemen, ...), custom_call_target="tpu_custom_call", output_to_operand_aliasing={{0}: (0, {}), {5}: (5, {})} | custom-call | flops 1 | bytes 1 | tf_op jit(solution)/shard_map/edges/pallas_call | solution.py:454
  22.5 4.3 %collective-permute-start.6 = (f32[4,2,64,128]{3,2,1,0:T(8,128)S(1)}, f32[4,2,64,128]{3,2,1,0:T(8,128)S(1)}, u32[]{:S(2)}, u32[]{:S(2)}) collective-permute-start(f32[4,2,64,128]{3,2,1,0:T(8,128)S(1)} %get-tuple-element.43), channel_id=1, source_target_pairs={{0,8},{8,0},{16,24},{24,16},{1,9},{9,1},{17,25},{25,17},{2,10},{10... | collective-permute-start | bytes 786440 | tf_op jit(solution)/shard_map/ppermute | solution.py:53
  26.8 0.7 collective-permute-start.7
  27.5 2.5 %collective-permute-start.8 = (f32[4,2,64,128]{3,2,1,0:T(8,128)S(1)}, f32[4,2,64,128]{3,2,1,0:T(8,128)S(1)}, u32[]{:S(2)}, u32[]{:S(2)}) collective-permute-start(f32[4,2,64,128]{3,2,1,0:T(8,128)S(1)} %get-tuple-element.45), channel_id=1, source_target_pairs={{0,2},{2,0},{4,6},{6,4},{1,3},{3,1},{5,7},{7,5},{8,10},{10,8},{12,... | collective-permute-start | bytes 786440 | tf_op jit(solution)/shard_map/ppermute | solution.py:53
  30.0 0.7 collective-permute-start.9
  30.7 7.5 %step.4 = (f32[4,68,72,128]{3,2,1,0:T(8,128)S(1)}, f32[4,2,64,128]{3,2,1,0:T(8,128)S(1)}) custom-call(f32[4,68,72,128]{3,2,1,0:T(8,128)S(1)} %get-tuple-element.40.field.before, f32[64,64,128]{2,1,0:T(8,128)S(1)} %get-tuple-element.30.weight, bf16[256,128]{1,0:T(8,128)(2,1)S(1)} %get-tuple-element.31.mix, ...), custom_call_target="tpu_custom_call", output_to_operand_aliasing={{0}: (5, {})} | custom-call | flops 1 | bytes 1 | tf_op jit(solution)/shard_map/step/pallas_call | solution.py:313
  38.2 1.0 %edges.4 = (f32[4,68,72,128]{3,2,1,0:T(8,128)S(1)}, f32[4,2,64,128]{3,2,1,0:T(8,128)S(1)}, f32[4,2,64,128]{3,2,1,0:T(8,128)S(1)}, f32[4,2,64,128]{3,2,1,0:T(8,12...) custom-call(f32[4,68,72,128]{3,2,1,0:T(8,128)S(1)} %get-tuple-elemen, ...), custom_call_target="tpu_custom_call", output_to_operand_aliasing={{0}: (0, {}), {5}: (5, {})} | custom-call | flops 1 | bytes 1 | tf_op jit(solution)/shard_map/edges/pallas_call | solution.py:454
  39.3 2.7 %collective-permute-start.11 = (f32[4,2,64,128]{3,2,1,0:T(8,128)S(1)}, f32[4,2,64,128]{3,2,1,0:T(8,128)S(1)}, u32[]{:S(2)}, u32[]{:S(2)}) collective-permute-start(f32[4,2,64,128]{3,2,1,0:T(8,128)S(1)} %get-tuple-element.50), channel_id=1, source_target_pairs={{0,8},{8,0},{16,24},{24,16},{1,9},{9,1},{17,25},{25,17},{2,10},{10... | collective-permute-start | bytes 786440 | tf_op jit(solution)/shard_map/ppermute | solution.py:53
  42.0 0.7 collective-permute-start.12
  42.7 2.6 %collective-permute-start.13 = (f32[4,2,64,128]{3,2,1,0:T(8,128)S(1)}, f32[4,2,64,128]{3,2,1,0:T(8,128)S(1)}, u32[]{:S(2)}, u32[]{:S(2)}) collective-permute-start(f32[4,2,64,128]{3,2,1,0:T(8,128)S(1)} %get-tuple-element.52), channel_id=1, source_target_pairs={{0,2},{2,0},{4,6},{6,4},{1,3},{3,1},{5,7},{7,5},{8,10},{10,8},{12,... | collective-permute-start | bytes 786440 | tf_op jit(solution)/shard_map/ppermute | solution.py:53
  45.3 0.7 collective-permute-start.14
  46.0 6.9 %step.5.field = f32[4,68,72,128]{3,2,1,0:T(8,128)S(1)} custom-call(f32[4,68,72,128]{3,2,1,0:T(8,128)S(1)} %get-tuple-element.48.field, f32[64,64,128]{2,1,0:T(8,128)S(1)} %get-tuple-element.30.weight, bf16[256,128]{1,0:T(8,128)(2,1)S(1)} %get-tuple-element.31.mix, ...), custom_call_target="tpu_custom_call", output_to_operand_aliasing={{}: (5, {})} | custom-call | flops 1 | bytes 1 | tf_op jit(solution)/shard_map/step/pallas_call | solution.py:313
  52.9 1.2 %products.1.extra = f32[16,128]{1,0:T(8,128)S(1)} custom-call(f32[4,68,72,128]{3,2,1,0:T(8,128)S(1)} %step.5.field), custom_call_target="tpu_custom_call" | custom-call | flops 1 | bytes 1 | tf_op jit(solution)/shard_map/products/pallas_call | solution.py:499
  54.2 1.0 %edges.5 = (f32[4,68,72,128]{3,2,1,0:T(8,128)S(1)}, f32[16,128]{1,0:T(8,128)S(1)}) custom-call(f32[4,68,72,128]{3,2,1,0:T(8,128)S(1)} %step.5.field, f32[4,2,64,128]{3,2,1,0:T(8,128)S(1)} %collective-permute-done.11.x_even, f32[4,2,64,128]{3,2,1,0:T(8,128)S(1)} %collective-permute-done.12.y_odd, ...), custom_call_target="tpu_custom_call", output_to_operand_aliasing={{0}: (0, {})} | custom-call | flops 1 | bytes 1 | tf_op jit(solution)/shard_map/edges/pallas_call | solution.py:454
  55.3 1.2 %collective-permute-done.15 = f32[16,128]{1,0:T(8,128)S(1)} collective-permute-done((f32[16,128]{1,0:T(8,128)S(1)}, f32[16,128]{1,0:T(8,128)S(1)}, u32[]{:S(2)}, u32[]{:S(2)}) %collective-permute-start.15) | collective-permute-done | bytes 8224 | tf_op jit(solution)/shard_map/ppermute | solution.py:618
  56.4 1.9 %collective-permute-start.18 = (f32[16,128]{1,0:T(8,128)S(1)}, f32[16,128]{1,0:T(8,128)S(1)}, u32[]{:S(2)}, u32[]{:S(2)}) collective-permute-start(f32[16,128]{1,0:T(8,128)S(1)} %add.12), channel_id=1, source_target_pairs={{0,6},{2,4},{4,2},{6,0},{1,7},{3,5},{5,3},{7,1},{8,14},{10,12},{12... | collective-permute-start | bytes 24584 | tf_op jit(solution)/shard_map/ppermute | solution.py:618
  58.4 2.4 %collective-permute-start.16 = (f32[16,128]{1,0:T(8,128)S(1)}, f32[16,128]{1,0:T(8,128)S(1)}, u32[]{:S(2)}, u32[]{:S(2)}) collective-permute-start(f32[16,128]{1,0:T(8,128)S(1)} %add.12), channel_id=1, source_target_pairs={{0,2},{2,0},{4,6},{6,4},{1,3},{3,1},{5,7},{7,5},{8,10},{10,8},{12,... | collective-permute-start | bytes 24584 | tf_op jit(solution)/shard_map/ppermute | solution.py:618
  60.8 1.1 %collective-permute-done.18 = f32[16,128]{1,0:T(8,128)S(1)} collective-permute-done((f32[16,128]{1,0:T(8,128)S(1)}, f32[16,128]{1,0:T(8,128)S(1)}, u32[]{:S(2)}, u32[]{:S(2)}) %collective-permute-start.18) | collective-permute-done | bytes 8224 | tf_op jit(solution)/shard_map/ppermute | solution.py:618
  61.9 1.0 %collective-permute-done.17 = f32[16,128]{1,0:T(8,128)S(1)} collective-permute-done((f32[16,128]{1,0:T(8,128)S(1)}, f32[16,128]{1,0:T(8,128)S(1)}, u32[]{:S(2)}, u32[]{:S(2)}) %collective-permute-start.17) | collective-permute-done | bytes 8224 | tf_op jit(solution)/shard_map/ppermute | solution.py:618
  62.9 1.3 %collective-permute-start.21 = (f32[16,128]{1,0:T(8,128)S(1)}, f32[16,128]{1,0:T(8,128)S(1)}, u32[]{:S(2)}, u32[]{:S(2)}) collective-permute-start(f32[16,128]{1,0:T(8,128)S(1)} %add_add_fusion.rest_0_), channel_id=1, source_target_pairs={{0,24},{8,16},{16,8},{24,0},{1,25},{9,17},{17,9},{25,1},{2,26},{10... | collective-permute-start | bytes 24584 | tf_op jit(solution)/shard_map/ppermute | solution.py:618
  64.3 2.7 %collective-permute-start.20 = (f32[16,128]{1,0:T(8,128)S(1)}, f32[16,128]{1,0:T(8,128)S(1)}, u32[]{:S(2)}, u32[]{:S(2)}) collective-permute-start(f32[16,128]{1,0:T(8,128)S(1)} %add_add_fusion.rest_0_), channel_id=1, source_target_pairs={{0,16},{8,24},{16,0},{24,8},{1,17},{9,25},{17,1},{25,9},{2,18},{10... | collective-permute-start | bytes 24584 | tf_op jit(solution)/shard_map/ppermute | solution.py:618
  67.2 0.4 collective-permute-done.21.rest_3_
  67.5 1.1 %collective-permute-done.20.rest_2_ = f32[16,128]{1,0:T(8,128)S(1)} collective-permute-done((f32[16,128]{1,0:T(8,128)S(1)}, f32[16,128]{1,0:T(8,128)S(1)}, u32[]{:S(2)}, u32[]{:S(2)}) %collective-permute-start.20) | collective-permute-done | bytes 8224 | tf_op jit(solution)/shard_map/ppermute | solution.py:618
  68.6 2.0 %collective-permute-done.19.rest_1_ = f32[16,128]{1,0:T(8,128)S(1)} collective-permute-done((f32[16,128]{1,0:T(8,128)S(1)}, f32[16,128]{1,0:T(8,128)S(1)}, u32[]{:S(2)}, u32[]{:S(2)}) %collective-permute-start.19) | collective-permute-done | bytes 8224 | tf_op jit(solution)/shard_map/ppermute | solution.py:618
  70.6 4.2 %basis.1 = (f32[4,64,64,128]{3,2,1,0:T(8,128)}, f32[4,4]{1,0:T(4,128)}) custom-call(f32[4,68,72,128]{3,2,1,0:T(8,128)S(1)} %get-tuple-element.54.field, f32[16,128]{1,0:T(8,128)S(1)} %add_add_fusion.rest_0_, f32[16,128]{1,0:T(8,128)S(1)} %collective-permute-done.19.rest_1_, f32[16,128]{1,0:T(8,128)S(1)} %collective-permute-done.20.rest_2_, ...), custom_call_target="tpu_custom_call" | custom-call | flops 1 | bytes 1 | tf_op jit(solution)/shard_map/basis/pallas_call | solution.py:594
  (24 shorter events, 0.5 us)
Async XLA Ops:
  5.5 8.9 %collective-permute-start = (f32[4,2,64,128]{3,2,1,0:T(8,128)S(1)}, f32[4,2,64,128]{3,2,1,0:T(8,128)S(1)}, u32[]{:S(2)}, u32[]{:S(2)}) collective-permute-start(f32[4,2,64,128]{3,2,1,0:T(8,128)S(1)} %get-tuple-element.32), channel_id=1, source_target_pairs={{0,1},{1,0},{2,3},{3,2},{4,5},{5,4},{6,7},{7,6},{8,9},{9,8},{10,11... | collective-permute-start | bytes 786440 | tf_op jit(solution)/shard_map/ppermute | solution.py:53
  6.0 15.4 %collective-permute-start.1 = (f32[4,2,64,128]{3,2,1,0:T(8,128)S(1)}, f32[4,2,64,128]{3,2,1,0:T(8,128)S(1)}, u32[]{:S(2)}, u32[]{:S(2)}) collective-permute-start(f32[4,2,64,128]{3,2,1,0:T(8,128)S(1)} %get-tuple-element.35), channel_id=1, source_target_pairs={{0,8},{8,0},{16,24},{24,16},{1,9},{9,1},{17,25},{25,17},{2,10},{10... | collective-permute-start | bytes 786440 | tf_op jit(solution)/shard_map/ppermute | solution.py:53
  8.5 12.9 %collective-permute-start.2 = (f32[4,2,64,128]{3,2,1,0:T(8,128)S(1)}, f32[4,2,64,128]{3,2,1,0:T(8,128)S(1)}, u32[]{:S(2)}, u32[]{:S(2)}) collective-permute-start(f32[4,2,64,128]{3,2,1,0:T(8,128)S(1)} %get-tuple-element.36), channel_id=1, source_target_pairs={{2,4},{4,2},{3,5},{5,3},{10,12},{12,10},{11,13},{13,11},{18,20},{2... | collective-permute-start | bytes 786440 | tf_op jit(solution)/shard_map/ppermute | solution.py:53
  9.2 12.2 %collective-permute-start.3 = (f32[4,2,64,128]{3,2,1,0:T(8,128)S(1)}, f32[4,2,64,128]{3,2,1,0:T(8,128)S(1)}, u32[]{:S(2)}, u32[]{:S(2)}) collective-permute-start(f32[4,2,64,128]{3,2,1,0:T(8,128)S(1)} %get-tuple-element.37), channel_id=1, source_target_pairs={{0,2},{2,0},{4,6},{6,4},{1,3},{3,1},{5,7},{7,5},{8,10},{10,8},{12,... | collective-permute-start | bytes 786440 | tf_op jit(solution)/shard_map/ppermute | solution.py:53
  13.7 7.8 %collective-permute-start.4 = (f32[4,2,64,128]{3,2,1,0:T(8,128)S(1)}, f32[4,2,64,128]{3,2,1,0:T(8,128)S(1)}, u32[]{:S(2)}, u32[]{:S(2)}) collective-permute-start(f32[4,2,64,128]{3,2,1,0:T(8,128)S(1)} %get-tuple-element.38), channel_id=1, source_target_pairs={{8,16},{16,8},{9,17},{17,9},{10,18},{18,10},{11,19},{19,11},{12,20... | collective-permute-start | bytes 786440 | tf_op jit(solution)/shard_map/ppermute | solution.py:53
  22.4 8.3 %collective-permute-start.5 = (f32[4,2,64,128]{3,2,1,0:T(8,128)S(1)}, f32[4,2,64,128]{3,2,1,0:T(8,128)S(1)}, u32[]{:S(2)}, u32[]{:S(2)}) collective-permute-start(f32[4,2,64,128]{3,2,1,0:T(8,128)S(1)} %get-tuple-element.41), channel_id=1, source_target_pairs={{0,1},{1,0},{2,3},{3,2},{4,5},{5,4},{6,7},{7,6},{8,9},{9,8},{10,11... | collective-permute-start | bytes 786440 | tf_op jit(solution)/shard_map/ppermute | solution.py:53
  22.5 15.7 %collective-permute-start.6 = (f32[4,2,64,128]{3,2,1,0:T(8,128)S(1)}, f32[4,2,64,128]{3,2,1,0:T(8,128)S(1)}, u32[]{:S(2)}, u32[]{:S(2)}) collective-permute-start(f32[4,2,64,128]{3,2,1,0:T(8,128)S(1)} %get-tuple-element.43), channel_id=1, source_target_pairs={{0,8},{8,0},{16,24},{24,16},{1,9},{9,1},{17,25},{25,17},{2,10},{10... | collective-permute-start | bytes 786440 | tf_op jit(solution)/shard_map/ppermute | solution.py:53
  26.8 11.4 %collective-permute-start.7 = (f32[4,2,64,128]{3,2,1,0:T(8,128)S(1)}, f32[4,2,64,128]{3,2,1,0:T(8,128)S(1)}, u32[]{:S(2)}, u32[]{:S(2)}) collective-permute-start(f32[4,2,64,128]{3,2,1,0:T(8,128)S(1)} %get-tuple-element.44), channel_id=1, source_target_pairs={{2,4},{4,2},{3,5},{5,3},{10,12},{12,10},{11,13},{13,11},{18,20},{2... | collective-permute-start | bytes 786440 | tf_op jit(solution)/shard_map/ppermute | solution.py:53
  27.5 10.8 %collective-permute-start.8 = (f32[4,2,64,128]{3,2,1,0:T(8,128)S(1)}, f32[4,2,64,128]{3,2,1,0:T(8,128)S(1)}, u32[]{:S(2)}, u32[]{:S(2)}) collective-permute-start(f32[4,2,64,128]{3,2,1,0:T(8,128)S(1)} %get-tuple-element.45), channel_id=1, source_target_pairs={{0,2},{2,0},{4,6},{6,4},{1,3},{3,1},{5,7},{7,5},{8,10},{10,8},{12,... | collective-permute-start | bytes 786440 | tf_op jit(solution)/shard_map/ppermute | solution.py:53
  30.0 8.2 %collective-permute-start.9 = (f32[4,2,64,128]{3,2,1,0:T(8,128)S(1)}, f32[4,2,64,128]{3,2,1,0:T(8,128)S(1)}, u32[]{:S(2)}, u32[]{:S(2)}) collective-permute-start(f32[4,2,64,128]{3,2,1,0:T(8,128)S(1)} %get-tuple-element.46), channel_id=1, source_target_pairs={{8,16},{16,8},{9,17},{17,9},{10,18},{18,10},{11,19},{19,11},{12,20... | collective-permute-start | bytes 786440 | tf_op jit(solution)/shard_map/ppermute | solution.py:53
  39.2 6.7 %collective-permute-start.10 = (f32[4,2,64,128]{3,2,1,0:T(8,128)S(1)}, f32[4,2,64,128]{3,2,1,0:T(8,128)S(1)}, u32[]{:S(2)}, u32[]{:S(2)}) collective-permute-start(f32[4,2,64,128]{3,2,1,0:T(8,128)S(1)} %get-tuple-element.49), channel_id=1, source_target_pairs={{0,1},{1,0},{2,3},{3,2},{4,5},{5,4},{6,7},{7,6},{8,9},{9,8},{10,11... | collective-permute-start | bytes 786440 | tf_op jit(solution)/shard_map/ppermute | solution.py:53
  39.3 14.9 %collective-permute-start.11 = (f32[4,2,64,128]{3,2,1,0:T(8,128)S(1)}, f32[4,2,64,128]{3,2,1,0:T(8,128)S(1)}, u32[]{:S(2)}, u32[]{:S(2)}) collective-permute-start(f32[4,2,64,128]{3,2,1,0:T(8,128)S(1)} %get-tuple-element.50), channel_id=1, source_target_pairs={{0,8},{8,0},{16,24},{24,16},{1,9},{9,1},{17,25},{25,17},{2,10},{10... | collective-permute-start | bytes 786440 | tf_op jit(solution)/shard_map/ppermute | solution.py:53
  42.0 12.2 %collective-permute-start.12 = (f32[4,2,64,128]{3,2,1,0:T(8,128)S(1)}, f32[4,2,64,128]{3,2,1,0:T(8,128)S(1)}, u32[]{:S(2)}, u32[]{:S(2)}) collective-permute-start(f32[4,2,64,128]{3,2,1,0:T(8,128)S(1)} %get-tuple-element.51), channel_id=1, source_target_pairs={{2,4},{4,2},{3,5},{5,3},{10,12},{12,10},{11,13},{13,11},{18,20},{2... | collective-permute-start | bytes 786440 | tf_op jit(solution)/shard_map/ppermute | solution.py:53
  42.7 11.5 %collective-permute-start.13 = (f32[4,2,64,128]{3,2,1,0:T(8,128)S(1)}, f32[4,2,64,128]{3,2,1,0:T(8,128)S(1)}, u32[]{:S(2)}, u32[]{:S(2)}) collective-permute-start(f32[4,2,64,128]{3,2,1,0:T(8,128)S(1)} %get-tuple-element.52), channel_id=1, source_target_pairs={{0,2},{2,0},{4,6},{6,4},{1,3},{3,1},{5,7},{7,5},{8,10},{10,8},{12,... | collective-permute-start | bytes 786440 | tf_op jit(solution)/shard_map/ppermute | solution.py:53
  45.3 8.9 %collective-permute-start.14 = (f32[4,2,64,128]{3,2,1,0:T(8,128)S(1)}, f32[4,2,64,128]{3,2,1,0:T(8,128)S(1)}, u32[]{:S(2)}, u32[]{:S(2)}) collective-permute-start(f32[4,2,64,128]{3,2,1,0:T(8,128)S(1)} %get-tuple-element.53), channel_id=1, source_target_pairs={{8,16},{16,8},{9,17},{17,9},{10,18},{18,10},{11,19},{19,11},{12,20... | collective-permute-start | bytes 786440 | tf_op jit(solution)/shard_map/ppermute | solution.py:53
  55.2 1.2 %collective-permute-start.15 = (f32[16,128]{1,0:T(8,128)S(1)}, f32[16,128]{1,0:T(8,128)S(1)}, u32[]{:S(2)}, u32[]{:S(2)}) collective-permute-start(f32[16,128]{1,0:T(8,128)S(1)} %get-tuple-element.55), channel_id=1, source_target_pairs={{0,1},{1,0},{2,3},{3,2},{4,5},{5,4},{6,7},{7,6},{8,9},{9,8},{10,11... | collective-permute-start | bytes 24584 | tf_op jit(solution)/shard_map/ppermute | solution.py:618
  56.4 5.5 %collective-permute-start.18 = (f32[16,128]{1,0:T(8,128)S(1)}, f32[16,128]{1,0:T(8,128)S(1)}, u32[]{:S(2)}, u32[]{:S(2)}) collective-permute-start(f32[16,128]{1,0:T(8,128)S(1)} %add.12), channel_id=1, source_target_pairs={{0,6},{2,4},{4,2},{6,0},{1,7},{3,5},{5,3},{7,1},{8,14},{10,12},{12... | collective-permute-start | bytes 24584 | tf_op jit(solution)/shard_map/ppermute | solution.py:618
  58.4 4.5 %collective-permute-start.17 = (f32[16,128]{1,0:T(8,128)S(1)}, f32[16,128]{1,0:T(8,128)S(1)}, u32[]{:S(2)}, u32[]{:S(2)}) collective-permute-start(f32[16,128]{1,0:T(8,128)S(1)} %add.12), channel_id=1, source_target_pairs={{0,4},{2,6},{4,0},{6,2},{1,5},{3,7},{5,1},{7,3},{8,12},{10,14},{12... | collective-permute-start | bytes 24584 | tf_op jit(solution)/shard_map/ppermute | solution.py:618
  58.4 4.5 %collective-permute-start.16 = (f32[16,128]{1,0:T(8,128)S(1)}, f32[16,128]{1,0:T(8,128)S(1)}, u32[]{:S(2)}, u32[]{:S(2)}) collective-permute-start(f32[16,128]{1,0:T(8,128)S(1)} %add.12), channel_id=1, source_target_pairs={{0,2},{2,0},{4,6},{6,4},{1,3},{3,1},{5,7},{7,5},{8,10},{10,8},{12,... | collective-permute-start | bytes 24584 | tf_op jit(solution)/shard_map/ppermute | solution.py:618
  62.9 4.6 %collective-permute-start.21 = (f32[16,128]{1,0:T(8,128)S(1)}, f32[16,128]{1,0:T(8,128)S(1)}, u32[]{:S(2)}, u32[]{:S(2)}) collective-permute-start(f32[16,128]{1,0:T(8,128)S(1)} %add_add_fusion.rest_0_), channel_id=1, source_target_pairs={{0,24},{8,16},{16,8},{24,0},{1,25},{9,17},{17,9},{25,1},{2,26},{10... | collective-permute-start | bytes 24584 | tf_op jit(solution)/shard_map/ppermute | solution.py:618
  64.3 4.4 %collective-permute-start.20 = (f32[16,128]{1,0:T(8,128)S(1)}, f32[16,128]{1,0:T(8,128)S(1)}, u32[]{:S(2)}, u32[]{:S(2)}) collective-permute-start(f32[16,128]{1,0:T(8,128)S(1)} %add_add_fusion.rest_0_), channel_id=1, source_target_pairs={{0,16},{8,24},{16,0},{24,8},{1,17},{9,25},{17,1},{25,9},{2,18},{10... | collective-permute-start | bytes 24584 | tf_op jit(solution)/shard_map/ppermute | solution.py:618
  67.0 3.7 %collective-permute-start.19 = (f32[16,128]{1,0:T(8,128)S(1)}, f32[16,128]{1,0:T(8,128)S(1)}, u32[]{:S(2)}, u32[]{:S(2)}) collective-permute-start(f32[16,128]{1,0:T(8,128)S(1)} %add_add_fusion.rest_0_), channel_id=1, source_target_pairs={{0,8},{8,0},{16,24},{24,16},{1,9},{9,1},{17,25},{25,17},{2,10},{10... | collective-permute-start | bytes 24584 | tf_op jit(solution)/shard_map/ppermute | solution.py:618
